TPU v7x, 128 devices: a whole 4x4x4 slice. The times are simulated.
128 devices in a mesh: feed: 4 (over x), freq: 32 (over z, y, core).
Axes of the slice: x: 4, y: 4, z: 4, core: 2. Of those that a mesh axis runs over, the one named last changes fastest.
Arguments:
- voltage: bfloat16 [2, 1024, 131072], P(None, 'feed', 'freq'), may hold values from -6 to 6
- flags: int32 [4, 512], P('feed'), may hold values 0 or 1
- owner_slot: int32 [512], replicated, may hold values from 0 to 639, as said below
Outputs:
- visibility: bfloat16 [640, 2, 1024, 1024], P('freq', None, 'feed')
Inputs may be any that keep to these rules, and one draw needn't show every extreme that they name: `owner_slot`: distinct slots; slot s belongs to owner s // 20 of freq. No owner gets more than 20 channels, and some owner gets exactly 20.
All inputs are finite; a program needn't handle non-finite values. No bound on the sum of `flags` on one device may be relied on, other than what follows from the above.
Results may differ from a plain program's by a relative error of at most 0.0073.
Values may be sent and summed in bfloat16 or wider, within the bound.
No kernel may reach another device: no remote copies, remote signals or barrier semaphores. Data moves between devices by JAX's collectives and lax.ppermute only.
A program may use at most 192 MiB of HBM per device.

v0:
```python
import math

import jax
import jax.numpy as jnp
from jax import lax
from jax.sharding import PartitionSpec as P

CH = 1024
TAPS = 4
BAND_LO = 256
CAP = 20


def passed_along(value, axis, steps):
    count = lax.axis_size(axis)
    initial, last = (max(0, -steps), min(count, count - steps))
    return lax.ppermute(value, axis, [(source, source + steps) for source in range(initial, last)])


def prototype():
    total = TAPS * CH
    position = jnp.arange(total, dtype=jnp.int32).astype(jnp.float32)
    offset = (position - total / 2 + 0.5) / CH
    taper = 0.5 - 0.5 * jnp.cos(2 * jnp.pi * (position + 0.5) / total)
    coeffs = jnp.sinc(offset) * taper
    coeffs = coeffs * jnp.sqrt(CH / jnp.sum(coeffs * coeffs))
    return coeffs.reshape(TAPS, CH)


def tables(band):
    sample = jnp.arange(CH, dtype=jnp.int32)
    channel = jnp.arange(band, dtype=jnp.int32) + BAND_LO
    phase = (sample[:, None] * channel[None, :] % CH).astype(jnp.float32) * (2 * jnp.pi / CH)
    return (jnp.cos(phase).astype(jnp.bfloat16), jnp.sin(phase).astype(jnp.bfloat16))


def channelize(voltage, extra, flag_row):
    band = flag_row.shape[0]
    longer = jnp.concatenate([voltage, extra], 2)
    count = voltage.shape[2] // CH
    feeds = voltage.shape[1]
    blocks = longer.reshape(2, feeds, count + TAPS - 1, CH)
    coeffs = prototype()
    summed = blocks[:, :, 0:count, :].astype(jnp.float32) * coeffs[0]
    for tap_index in range(1, TAPS):
        summed = (
            summed
            + blocks[:, :, tap_index : tap_index + count, :].astype(jnp.float32) * coeffs[tap_index]
        )
    weighted = summed.astype(jnp.bfloat16)
    cosine, sine = tables(band)
    real_rows = weighted[0].reshape(feeds * count, CH)
    imag_rows = weighted[1].reshape(feeds * count, CH)
    real_part = jnp.dot(real_rows, cosine, preferred_element_type=jnp.float32) + jnp.dot(
        imag_rows, sine, preferred_element_type=jnp.float32
    )
    imag_part = jnp.dot(imag_rows, cosine, preferred_element_type=jnp.float32) - jnp.dot(
        real_rows, sine, preferred_element_type=jnp.float32
    )
    joined = jnp.stack([real_part, imag_part], 0).reshape(2, feeds, count, band)
    joined = joined * (flag_row.astype(jnp.float32) * (1.0 / math.sqrt(CH)))
    return jnp.transpose(joined, (3, 0, 2, 1)).astype(jnp.bfloat16)


def correlate(own_rows, columns, inverse):
    swapped = jnp.stack([columns[:, :, 1], -columns[:, :, 0]], 2)
    real_vis = jnp.einsum("cpzsf,cpzsg->cfg", own_rows, columns, preferred_element_type=jnp.float32)
    imag_vis = jnp.einsum("cpzsf,cpzsg->cfg", own_rows, swapped, preferred_element_type=jnp.float32)
    return (jnp.stack([real_vis, imag_vis], 1) * inverse).astype(jnp.bfloat16)


def body(voltage, flags, owner_slot):
    tail_width = (TAPS - 1) * CH
    incoming = passed_along(voltage[:, :, :tail_width], "freq", -1)
    spectra = channelize(voltage, incoming, flags[0])
    owners = lax.axis_size("freq")
    band = owner_slot.shape[0]
    row_index = jnp.arange(CAP * owners, dtype=jnp.int32)
    slot_ids = row_index % owners * CAP + row_index // owners
    selector = (owner_slot[None, :] == slot_ids[:, None]).astype(jnp.bfloat16)
    inverse = 1.0 / (owners * spectra.shape[2])
    complete = lax.all_gather(spectra, "feed", axis=3, tiled=True)
    flat = complete.reshape(band, -1)
    placed = jnp.dot(selector, flat, preferred_element_type=jnp.float32).astype(jnp.bfloat16)
    received = lax.all_to_all(
        placed.reshape((CAP, owners) + complete.shape[1:]),
        "freq",
        split_axis=1,
        concat_axis=1,
        tiled=True,
    )
    width = spectra.shape[3]
    own_rows = lax.dynamic_slice_in_dim(received, lax.axis_index("feed") * width, width, 4)
    result = correlate(own_rows, received, inverse)
    return result


def solution(mesh):
    placed = (P(None, "feed", "freq"), P("feed", None), P())
    return jax.shard_map(
        body, mesh=mesh, in_specs=placed, out_specs=P("freq", None, "feed", None), check_vma=False
    )
```

profile of v0, /device:TPU:0, one launch (start us, length us, event | category | flops | bytes accessed | tf_op | source)
XLA Modules:
  0.0 502.7 jit_solution(7575006859095113080)
XLA Ops:
  6.5 6.3 %copy.21 = bf16[2,256,4096]{1,2,0:T(8,128)(2,1)} copy(bf16[2,256,4096]{2,1,0:T(8,128)(2,1)} %param.3) | data formatting | bytes 8388608 | tf_op args[0]
  12.9 3.8 slice.56
  19.4 5.0 collective-permute-done
  24.4 5.7 %pad_maximum_fusion = bf16[2,256,7168]{1,2,0:T(8,128)(2,1)} fusion(bf16[2,256,3072]{1,2,0:T(8,128)(2,1)S(1)} %collective-permute-done, bf16[2,256,4096]{1,2,0:T(8,128)(2,1)} %copy.21), kind=kLoop, calls=%fused_computation.10 | loop fusion | flops 14680064 | bytes 14680064 | tf_op jit(solution)/shard_map/concatenate | solution.py:39
  30.1 8.1 %add_convert_fusion = bf16[2,256,4,1024]{1,3,2,0:T(8,128)(2,1)S(1)} fusion(bf16[2,256,7,1024]{1,3,2,0:T(8,128)(2,1)} %bitcast.23, f32[1024]{0:T(1024)S(1)} %get-tuple-element.10, f32[1024]{0:T(1024)S(1)} %get-tuple-element.11, f32[1024]{0:T(1024)S(1)} %get-tuple-element.12, f32[1024]{0:T(1024)S(1)} %get-tuple-element.9), kind=kLoop, calls=%fused_computation.9 | loop fusion | flops 25165824 | bytes 20987904 | tf_op jit(solution)/shard_map/convert_element_type | solution.py:50
  40.5 3.4 copy.22
  45.9 3.4 copy.23
  51.3 10.2 %fusion.20 = f32[1024,512]{1,0:T(8,128)S(1)} fusion(bf16[1024,1024]{1,0:T(8,128)(2,1)} %reshape_squeeze.6, s32[512]{0:T(512)S(1)} %iota_add_fusion), kind=kOutput, calls=%fused_computation.32 | convolution fusion | flops 1081606144 | bytes 4196352 | tf_op jit(solution)/shard_map/dot_general | solution.py:54
  61.5 21.6 %fusion.19 = f32[1024,512]{1,0:T(8,128)S(1)} fusion(bf16[1024,1024]{1,0:T(8,128)(2,1)S(1)} %copy-done.2, s32[512]{0:T(512)S(1)} %iota_add_fusion), kind=kOutput, calls=%fused_computation.31 | convolution fusion | flops 1081606144 | bytes 4196352 | tf_op jit(solution)/shard_map/dot_general | solution.py:57
  83.1 10.6 %convolution_add_fusion = f32[1024,512]{1,0:T(8,128)} fusion(f32[1024,512]{1,0:T(8,128)S(1)} %fusion.20, bf16[1024,1024]{1,0:T(8,128)(2,1)S(1)} %copy-done.2, s32[512]{0:T(512)S(1)} %iota_add_fusion), kind=kOutput, calls=%fused_computation.29 | convolution fusion | flops 1082130432 | bytes 6293504 | tf_op jit(solution)/shard_map/dot_general | solution.py:54
  93.7 9.0 %convolution_subtract_fusion = f32[1024,512]{1,0:T(8,128)S(1)} fusion(f32[1024,512]{1,0:T(8,128)S(1)} %fusion.19, bf16[1024,1024]{1,0:T(8,128)(2,1)S(1)} %copy-done.1, s32[512]{0:T(512)S(1)} %iota_add_fusion), kind=kOutput, calls=%fused_computation.28 | convolution fusion | flops 1082130432 | bytes 6293504 | tf_op jit(solution)/shard_map/dot_general | solution.py:57
  106.6 2.8 stack.22
  113.7 118.0 %all-gather.2.cloned.1.call-done = bf16[512,2,4,1024]{0,3,2,1:T(8,128)(2,1)} async-done(((bf16[512,2,4,256]{0,3,2,1:T(8,128)(2,1)}), bf16[512,2,4,1024]{0,3,2,1:T(8,128)(2,1)}) %all-gather.2.cloned.1.call-update) | async-done | bytes 8388624 | tf_op jit(solution)/shard_map/all_gather | solution.py:82
  231.7 11.7 %convolution_convert_fusion = bf16[640,8192]{1,0:T(8,128)(2,1)} fusion(bf16[512,8192]{0,1:T(8,128)(2,1)} %bitcast.25, s32[512]{0:T(512)S(1)} %copy-done.4, s32[640]{0:T(1024)S(1)} %fusion.42), kind=kOutput, calls=%fused_computation.2 | convolution fusion | flops 5374279680 | bytes 18878976 | tf_op jit(solution)/shard_map/dot_general | solution.py:84
  243.3 17.8 %reshape.65 = bf16[20,32,2,4,1024]{4,3,2,1,0:T(4,128)(2,1)} reshape(bf16[640,8192]{1,0:T(8,128)(2,1)} %convolution_convert_fusion) | data formatting | bytes 20971520 | tf_op jit(solution)/shard_map/reshape | solution.py:86
  261.1 16.1 %copy.26 = bf16[20,32,2,4,1024]{4,2,0,3,1:T(2,128)(2,1)} copy(bf16[20,32,2,4,1024]{4,3,2,1,0:T(4,128)(2,1)} %reshape.65) | data formatting | bytes 20971520 | tf_op jit(solution)/shard_map/reshape | solution.py:86
  277.2 7.7 %all-to-all-start = ((bf16[20,32,2,4,1024]{4,2,0,3,1:T(2,128)(2,1)}), bf16[20,32,2,4,1024]{4,2,0,3,1:T(2,128)(2,1)}, u32[]{:S(2)}, u32[]{:S(2)}) async-start(bf16[20,32,2,4,1024]{4,2,0,3,1:T(2,128)(2,1)} %copy.26), calls=%async_computation | async-start | bytes 20971520 | tf_op jit(solution)/shard_map/all_to_all | solution.py:85
  284.9 132.5 %all-to-all-done = bf16[20,32,2,4,1024]{4,2,0,3,1:T(2,128)(2,1)} async-done(((bf16[20,32,2,4,1024]{4,2,0,3,1:T(2,128)(2,1)}), bf16[20,32,2,4,1024]{4,2,0,3,1:T(2,128)(2,1)}, u32[]{:S(2)}, u32[]{:S(2)}) %all-to-all-start) | async-done | bytes 10485792 | tf_op jit(solution)/shard_map/all_to_all | solution.py:85
  417.3 19.2 %copy.27 = bf16[20,32,2,4,1024]{4,1,2,0,3:T(8,128)(2,1)} copy(bf16[20,32,2,4,1024]{4,2,0,3,1:T(2,128)(2,1)} %all-to-all-done) | data formatting | bytes 20971520 | tf_op jit(solution)/shard_map/all_to_all | solution.py:85
  436.5 9.0 %fusion.64 = (bf16[20,32,1,4,1024]{4,1,2,0,3:T(8,128)(2,1)}, bf16[20,32,1,4,1024]{4,1,2,0,3:T(8,128)(2,1)}) fusion(bf16[20,32,2,4,1024]{4,1,2,0,3:T(8,128)(2,1)} %copy.27), kind=kLoop, calls=%fused_computation.95 | loop fusion | flops 2621440 | bytes 20971520 | tf_op jit(solution)/shard_map/slice | solution.py:66
  445.5 14.8 %convolution_bitcast_fusion = f32[20,1,256,1024]{3,2,0,1:T(8,128)} fusion(bf16[20,32,2,4,1024]{4,1,2,0,3:T(8,128)(2,1)} %copy.27, s32[]{:T(128)S(6)} %select_n.75), kind=kOutput, calls=%fused_computation.7 | convolution fusion | flops 2684354560 | bytes 34078724 | tf_op jit(solution)/shard_map/cpzsf,cpzsg->cfg/dot_general | solution.py:67
  460.3 11.7 %fusion.5 = f32[20,1,256,1024]{3,2,0,1:T(8,128)} fusion(bf16[20,32,1,4,1024]{4,1,2,0,3:T(8,128)(2,1)} %get-tuple-element.6, bf16[20,32,1,4,1024]{4,1,2,0,3:T(8,128)(2,1)S(1)} %copy-done, bf16[20,32,2,4,1024]{4,1,2,0,3:T(8,128)(2,1)} %copy.27, s32[]{:T(128)S(6)} %select_n.75), kind=kOutput, calls=%fused_computation.8 | convolution fusion | flops 2689597440 | bytes 34078724 | tf_op jit(solution)/shard_map/cpzsf,cpzsg->cfg/dot_general | solution.py:68
  472.1 16.2 %fusion = bf16[20,2,256,1024]{3,2,0,1:T(8,128)(2,1)S(1)} fusion(f32[20,1,256,1024]{3,2,0,1:T(8,128)} %fusion.5, f32[20,1,256,1024]{3,2,0,1:T(8,128)} %convolution_bitcast_fusion), kind=kLoop, calls=%fused_computation.1 | loop fusion | flops 31457280 | bytes 62914560 | tf_op jit(solution)/shard_map/convert_element_type | solution.py:69
  488.3 7.3 %copy.31 = bf16[20,2,256,1024]{3,2,1,0:T(8,128)(2,1)} copy(bf16[20,2,256,1024]{3,2,0,1:T(8,128)(2,1)S(1)} %fusion) | data formatting | bytes 41943040 | tf_op jit(solution)/shard_map/convert_element_type | solution.py:69
  (26 shorter events, 16.6 us)
Async XLA Ops:
  6.5 225.1 %all-gather.2.cloned.1.call-start = ((), (), s32[]{:S(2)}) async-start(), calls=%async_computation.1 | async-start | bytes 10485760 | tf_op jit(solution)/shard_map/all_gather | solution.py:82
  12.9 6.5 %copy-start.3 = (s32[1,512]{1,0:T(1,128)S(1)}, s32[1,512]{1,0:T(1,128)}, u32[]{:S(2)}) copy-start(s32[1,512]{1,0:T(1,128)} %param.4) | copy-start | bytes 6148
  16.6 7.8 %collective-permute-start = (bf16[2,256,3072]{1,2,0:T(8,128)(2,1)}, bf16[2,256,3072]{1,2,0:T(8,128)(2,1)S(1)}, u32[]{:S(2)}, u32[]{:S(2)}) collective-permute-start(bf16[2,256,3072]{1,2,0:T(8,128)(2,1)} %slice.56), channel_id=1, source_target_pairs={{1,0},{2,1},{3,2},{4,3},{5,4},{6,5},{7,6},{8,7},{9,8},{10,9},{11,1... | collective-permute-start | bytes 9437192 | tf_op jit(solution)/shard_map/ppermute | solution.py:17
  51.3 10.2 %copy-start.2 = (bf16[1024,1024]{1,0:T(8,128)(2,1)S(1)}, bf16[1024,1024]{1,0:T(8,128)(2,1)}, u32[]{:S(2)}) copy-start(bf16[1024,1024]{1,0:T(8,128)(2,1)} %reshape_squeeze.7) | copy-start | bytes 6291460
  83.1 10.6 %copy-start.1 = (bf16[1024,1024]{1,0:T(8,128)(2,1)S(1)}, bf16[1024,1024]{1,0:T(8,128)(2,1)}, u32[]{:S(2)}) copy-start(bf16[1024,1024]{1,0:T(8,128)(2,1)} %reshape_squeeze.6) | copy-start | bytes 6291460
  113.6 118.0 %copy-start.4 = (s32[512]{0:T(512)S(1)}, s32[512]{0:T(512)}, u32[]{:S(2)}) copy-start(s32[512]{0:T(512)} %param.5) | copy-start | bytes 6148
  277.2 140.1 %all-to-all-start = ((bf16[20,32,2,4,1024]{4,2,0,3,1:T(2,128)(2,1)}), bf16[20,32,2,4,1024]{4,2,0,3,1:T(2,128)(2,1)}, u32[]{:S(2)}, u32[]{:S(2)}) async-start(bf16[20,32,2,4,1024]{4,2,0,3,1:T(2,128)(2,1)} %copy.26), calls=%async_computation | async-start | bytes 20971520 | tf_op jit(solution)/shard_map/all_to_all | solution.py:85
  445.5 14.8 %copy-start = (bf16[20,32,1,4,1024]{4,1,2,0,3:T(8,128)(2,1)S(1)}, bf16[20,32,1,4,1024]{4,1,2,0,3:T(8,128)(2,1)}, u32[]{:S(2)}) copy-start(bf16[20,32,1,4,1024]{4,1,2,0,3:T(8,128)(2,1)} %get-tuple-element.5) | copy-start | bytes 15728644
Sparse Core Ops, SparseCore 0:
  113.8 117.8 all-gather.1
where the time goes:
time: 513 us; the launch traced here: 503 us
  waiting for transfers between devices  255 us (50%)
  local copies, waits for them, and re-layouts  92.6 us (18%)
  matrix products  89.6 us (17%)
  other arithmetic  41.7 us (8%)
  between operations  14.4 us (3%)
  starting transfers between devices  8.95 us (2%)
    all_to_all x1, waiting for transfers between devices, body(): lax.all_to_all(placed.reshape((CAP, owners) + complete.shape[1:]), 'freq'...  132 us
    all_gather x1, waiting for transfers between devices, body(): complete = lax.all_gather(spectra, 'feed', axis=3, tiled=True)  118 us
    reshape x2, local copies, waits for them, and re-layouts, body(): placed.reshape((CAP, owners) + complete.shape[1:])  33.9 us
    dot_general x1, matrix products, channelize(): jnp.dot(imag_rows, cosine, preferred_element_type=jnp.float32)  21.6 us
    all_to_all x1, local copies, waits for them, and re-layouts, body(): lax.all_to_all(placed.reshape((CAP, owners) + complete.shape[1:]), 'freq'...  19.2 us
    convert_element_type x1, other arithmetic, correlate(): return (jnp.stack([real_vis, imag_vis], 1) * inverse).astype(jnp.bfloat16)  16.2 us
    dot_general x1, matrix products, correlate(): jnp.einsum('cpzsf,cpzsg->cfg', own_rows, columns, preferred_element_type=...  14.8 us
    dot_general x1, matrix products, correlate(): jnp.einsum('cpzsf,cpzsg->cfg', own_rows, swapped, preferred_element_type=...  11.7 us
  transfers between devices with their start and end apart: 3, of which 3 were waited for; matrix products, arithmetic and copies ran while one was open for 0% of the time, Pallas kernels for 0%

commit v1 on v0

v1 whole, which is shorter than its diff:
```python
import math

import jax
import jax.numpy as jnp
import ml_dtypes
import numpy as np
from jax import lax
from jax.experimental import pallas as pl
from jax.experimental.pallas import tpu as pltpu
from jax.sharding import PartitionSpec as P

CH = 1024
TAPS = 4
BAND_LO = 256
CAP = 20
CORES = 2
BLOCKS = 4
SPECTRA = 8
CHUNKS = (4, 4, 4, 4, 4)
VMEM = 60 * 1024 * 1024


def prototype():
    total = TAPS * CH
    position = np.arange(total).astype(np.float32)
    offset = (position - total / 2 + 0.5) / CH
    taper = 0.5 - 0.5 * np.cos(2 * np.pi * (position + 0.5) / total)
    coeffs = np.sinc(offset) * taper
    coeffs = coeffs * np.sqrt(CH / np.sum(coeffs * coeffs))
    return coeffs.reshape(TAPS, CH).astype(np.float32)


def tables(band):
    sample = np.arange(CH)
    channel = np.arange(band) + BAND_LO
    phase = (channel[:, None] * sample[None, :] % CH).astype(np.float32) * np.float32(2 * np.pi / CH)
    cosine = np.cos(phase).astype(ml_dtypes.bfloat16)
    sine = np.sin(phase).astype(ml_dtypes.bfloat16)
    return np.concatenate([cosine, sine, -sine, cosine], 1)


def moved(value, axis, pairs):
    return lax.ppermute(value, axis, pairs)


def weigh_kernel(place, voltage, other, after, before, coeffs, out, held, sems):
    core = place[0]
    half = voltage.shape[1] // CORES
    own_rows = pl.ds(pl.multiple_of(core * half, half), half)
    span = BLOCKS * CH
    own_at = pl.ds(pl.multiple_of(CH + core * span, CH), span)
    other_at = pl.ds(pl.multiple_of(CH + (1 - core) * span, CH), span)
    copies = [
        pltpu.make_async_copy(voltage.at[:, own_rows, :], held.at[:, :, own_at], sems.at[0]),
        pltpu.make_async_copy(other, held.at[:, :, other_at], sems.at[1]),
        pltpu.make_async_copy(after, held.at[:, :, pl.ds(CH + 2 * span, 2 * CH)], sems.at[2]),
        pltpu.make_async_copy(before, held.at[:, :, pl.ds(0, CH)], sems.at[3]),
    ]
    for copy in copies:
        copy.start()
    for copy in copies:
        copy.wait()
    keep = place[1].astype(jnp.float32)
    rows = 16
    width = 256

    def step(index, carry):
        at = pl.ds(pl.multiple_of(index * rows, rows), rows)
        for z in range(2):
            for start in range(0, CH, width):
                blocks = [
                    held[z, at, pl.ds(b * CH + start, width)].astype(jnp.float32)
                    for b in range(SPECTRA + TAPS - 1)
                ]
                taps = [coeffs[p : p + 1, pl.ds(start, width)] for p in range(TAPS)]
                for s in range(SPECTRA):
                    total = blocks[s] * taps[0]
                    for p in range(1, TAPS):
                        tap = taps[p] * keep if s == 0 else taps[p]
                        total = total + blocks[s + p] * tap
                    out[s, at, pl.ds(z * CH + start, width)] = total.astype(jnp.bfloat16)
        return carry

    lax.fori_loop(0, half // rows, step, 0)


def weigh(place, voltage, other, after, before):
    half = voltage.shape[1] // CORES
    anywhere = pl.BlockSpec(memory_space=pl.ANY)
    return pl.pallas_call(
        weigh_kernel,
        out_shape=jax.ShapeDtypeStruct((SPECTRA, half, 2 * CH), jnp.bfloat16),
        in_specs=[pl.BlockSpec(memory_space=pltpu.SMEM)]
        + [anywhere] * 4
        + [pl.BlockSpec(memory_space=pltpu.VMEM)],
        out_specs=pl.BlockSpec(memory_space=pltpu.VMEM),
        scratch_shapes=[
            pltpu.VMEM((2, half, (SPECTRA + TAPS - 1) * CH), jnp.bfloat16),
            pltpu.SemaphoreType.DMA((4,)),
        ],
        compiler_params=pltpu.CompilerParams(vmem_limit_bytes=VMEM),
        name="weigh",
    )(place, voltage, other, after, before, jnp.asarray(prototype()))


def transform_kernel(table, weighted, out, held):
    rows = table.shape[0]
    both = jnp.concatenate([table[:, : 2 * CH], table[:, 2 * CH :]], 0)
    half = weighted.shape[1]
    for s in range(0, SPECTRA, 2):
        samples = weighted[pl.ds(s, 2)].reshape(2 * half, 2 * CH)
        product = lax.dot_general(
            both, samples, (((1,), (1,)), ((), ())), preferred_element_type=jnp.float32
        )
        for z in range(2):
            for k in range(2):
                held[pl.ds(z * SPECTRA + s + k, rows, stride=2 * SPECTRA), :] = product[
                    z * rows : (z + 1) * rows, k * half : (k + 1) * half
                ]
    out[...] = held[...].reshape(out.shape).astype(jnp.bfloat16)


def transform(table, weighted):
    rows = table.shape[0]
    half = weighted.shape[1]
    return pl.pallas_call(
        transform_kernel,
        out_shape=jax.ShapeDtypeStruct((rows, 2 * SPECTRA, half), jnp.bfloat16),
        in_specs=[pl.BlockSpec(memory_space=pltpu.VMEM)] * 2,
        out_specs=pl.BlockSpec(memory_space=pltpu.VMEM),
        scratch_shapes=[pltpu.VMEM((rows * 2 * SPECTRA, half), jnp.float32)],
        compiler_params=pltpu.CompilerParams(vmem_limit_bytes=VMEM),
        name="transform",
    )(table, weighted)


def halves(block):
    count, _, rows, lanes = block.shape
    split = block.reshape(count // CORES, CORES, rows, lanes)
    return jnp.concatenate(
        [split[:, core].reshape(count // CORES * rows, lanes) for core in range(CORES)], 1
    )


def correlate_kernel(place, own, left, right, far_low, far_high, *rest):
    out = rest[-1]
    me = place[2]
    group = out.shape[2]
    groups = out.shape[3] // group
    scale = 1.0 / (SPECTRA * own.shape[0] // CORES)
    mine = halves(own[...])
    wide = mine.astype(jnp.float32).reshape(-1, 2, SPECTRA, group)
    turned = jnp.stack([-wide[:, 1], wide[:, 0]], 1).reshape(mine.shape)
    lhs = jnp.concatenate([wide.reshape(mine.shape), turned], 1)
    lhs = jnp.transpose(lhs).astype(jnp.bfloat16)
    far = jnp.concatenate([far_low[...], far_high[...]], 0)
    sources = [(0, mine), (groups - 1, halves(left[...])), (1, halves(right[...])), (2, halves(far))]
    for ahead, columns in sources:
        product = lax.dot_general(
            lhs, columns, (((1,), (0,)), ((), ())), preferred_element_type=jnp.float32
        )
        product = (product * scale).astype(jnp.bfloat16)
        at = pl.ds(pl.multiple_of(lax.rem(me + ahead, groups) * group, group), group)
        for z in range(2):
            out[0, z, :, at] = product[z * group : (z + 1) * group]


def correlate(place, parts, first, shape, result):
    own = parts[0]
    slots = own.shape[1]

    def part_spec(part):
        return pl.BlockSpec((part.shape[0], 1) + part.shape[2:], lambda j: (0, j, 0, 0))

    in_specs = [pl.BlockSpec(memory_space=pltpu.SMEM)] + [part_spec(part) for part in parts]
    operands = (place,) + tuple(parts)
    aliases = {}
    if result is not None:
        in_specs.append(pl.BlockSpec(memory_space=pl.ANY))
        aliases = {len(operands): 0}
        operands = operands + (result,)
    return pl.pallas_call(
        correlate_kernel,
        grid=(slots,),
        out_shape=jax.ShapeDtypeStruct(shape, jnp.bfloat16),
        in_specs=in_specs,
        out_specs=pl.BlockSpec((1,) + shape[1:], lambda j: (first + j, 0, 0, 0)),
        input_output_aliases=aliases,
        compiler_params=pltpu.CompilerParams(
            dimension_semantics=("arbitrary",), vmem_limit_bytes=VMEM
        ),
        name="correlate",
    )(*operands)


def body(voltage, flags, owner_slot):
    owners = lax.axis_size("freq")
    groups = lax.axis_size("feed")
    chips = owners // CORES
    band = owner_slot.shape[0]
    feeds = voltage.shape[1]
    half = feeds // CORES
    position = lax.axis_index("freq")
    core = position % CORES
    me = lax.axis_index("feed")
    place = jnp.stack([core, (position >= CORES).astype(jnp.int32), me]).astype(jnp.int32)

    after = [
        moved(
            voltage[:, c * half : (c + 1) * half, : 2 * CH],
            "freq",
            [(CORES * (k + 1), CORES * k + c) for k in range(chips - 1)],
        )
        for c in range(CORES)
    ]
    other = moved(
        lax.dynamic_slice_in_dim(voltage, (1 - core) * half, half, 1),
        "freq",
        [(k, k ^ 1) for k in range(owners)],
    )
    before = [
        moved(
            voltage[:, c * half : (c + 1) * half, (BLOCKS - 1) * CH :],
            "freq",
            [(CORES * k + CORES - 1, CORES * ((k + 1) % chips) + c) for k in range(chips)],
        )
        for c in range(CORES)
    ]
    table = jnp.asarray(tables(band))
    kept = flags[0].astype(jnp.float32) * (1.0 / math.sqrt(CH))
    chosen = []
    first = 0
    for slots in CHUNKS:
        row = jnp.arange(owners * slots, dtype=jnp.int32)
        slot = row // slots * CAP + first + row % slots
        select = jnp.where(owner_slot[None, :] == slot[:, None], kept[None, :], 0.0)
        chosen.append(
            jnp.dot(
                select.astype(jnp.bfloat16), table, preferred_element_type=jnp.float32
            ).astype(jnp.bfloat16)
        )
        first += slots

    low = core == 0
    weighted = weigh(
        place,
        voltage,
        other,
        jnp.where(low, after[0], after[1]),
        jnp.where(low, before[0], before[1]),
    )
    ring_up = [(k, (k + 1) % groups) for k in range(groups)]
    ring_down = [(k, (k - 1) % groups) for k in range(groups)]
    shape = (CAP, 2, feeds, feeds * groups)
    result = None
    first = 0
    for index, slots in enumerate(CHUNKS):
        spectra = transform(chosen[index], weighted)
        own = lax.all_to_all(
            spectra.reshape(owners, slots, 2 * SPECTRA, half), "freq", 0, 0, tiled=True
        )
        left = moved(own, "feed", ring_up)
        right = moved(own, "feed", ring_down)
        far_low = moved(left[: owners // 2], "feed", ring_up)
        far_high = moved(right[owners // 2 :], "feed", ring_down)
        result = correlate(place, (own, left, right, far_low, far_high), first, shape, result)
        first += slots
    return result


def solution(mesh):
    placed = (P(None, "feed", "freq"), P("feed", None), P())
    return jax.shard_map(
        body, mesh=mesh, in_specs=placed, out_specs=P("freq", None, "feed", None), check_vma=False
    )
```

time: 513 us -> 213 us (0.42); the launches traced: 503 us -> 212 us
  waiting for transfers between devices: 255 us -> 44.4 us
  local copies, waits for them, and re-layouts: 92.6 us -> 14.7 us
  matrix products: 89.6 us -> 19.7 us
  starting transfers between devices: 8.95 us -> 70.5 us
  Pallas kernels: 0 us -> 58.6 us
  other arithmetic: 41.7 us -> 3.64 us
  between operations: 14.4 us -> 0.27 us
    all_to_all x1 -> x5, waiting for transfers between devices: 132 us -> 14.1 us  [body(): lax.all_to_all(spectra.reshape(owners, slots, 2 * SPECTRA, half), 'freq',...]
    all_gather x1 -> x0, waiting for transfers between devices: 118 us -> none  [body(): complete = lax.all_gather(spectra, 'feed', axis=3, tiled=True)]
    dot_general x7 -> x5, matrix products: 89.6 us -> 19.7 us  [body(): jnp.dot(select.astype(jnp.bfloat16), table, preferred_element_type=jnp.fl...]
    pallas_call x0 -> x11, Pallas kernels: none -> 58.6 us  [the longest x5 26.5 us: correlate(): pl.pallas_call(correlate_kernel, grid=(slots,), out_shape=jax.ShapeDtypeS...]
    reshape x2 -> x0, local copies, waits for them, and re-layouts: 33.9 us -> none  [body(): placed.reshape((CAP, owners) + complete.shape[1:])]
    all_to_all x1 -> x5, starting transfers between devices: 7.66 us -> 39.7 us  [body(): lax.all_to_all(spectra.reshape(owners, slots, 2 * SPECTRA, half), 'freq',...]
    ppermute x1 -> x25, starting transfers between devices: 1.28 us -> 30.8 us  [moved(): return lax.ppermute(value, axis, pairs)]
    convert_element_type x3 -> x0, other arithmetic: 26.2 us -> none  [the longest x1 16.2 us: correlate(): return (jnp.stack([real_vis, imag_vis], 1) * inverse).astype(jnp.bfloat16)]
  transfers between devices with their start and end apart: 3 -> 30, of which waited for: 3 -> 11; matrix products, arithmetic and copies ran while one was open for 0% -> 17% of each run, Pallas kernels for 0% -> 19%
where the time goes in v1:
time: 213 us; the launch traced here: 212 us
  starting transfers between devices  70.5 us (33%)
  Pallas kernels  58.6 us (28%)
  waiting for transfers between devices  44.4 us (21%)
  matrix products  19.7 us (9%)
  local copies, waits for them, and re-layouts  14.7 us (7%)
  other arithmetic  3.64 us (2%)
    all_to_all x5, starting transfers between devices, body(): lax.all_to_all(spectra.reshape(owners, slots, 2 * SPECTRA, half), 'freq',...  39.7 us
    ppermute x25, starting transfers between devices, moved(): return lax.ppermute(value, axis, pairs)  30.8 us
    ppermute x25, waiting for transfers between devices, moved(): return lax.ppermute(value, axis, pairs)  30.3 us
    pallas_call x5, Pallas kernels, correlate(): pl.pallas_call(correlate_kernel, grid=(slots,), out_shape=jax.ShapeDtypeS...  26.5 us
    pallas_call x5, Pallas kernels, transform(): pl.pallas_call(transform_kernel, out_shape=jax.ShapeDtypeStruct((rows, 2...  24.2 us
    dot_general x5, matrix products, body(): jnp.dot(select.astype(jnp.bfloat16), table, preferred_element_type=jnp.fl...  19.7 us
    all_to_all x5, waiting for transfers between devices, body(): lax.all_to_all(spectra.reshape(owners, slots, 2 * SPECTRA, half), 'freq',...  14.1 us
    pallas_call x1, Pallas kernels, weigh(): pl.pallas_call(weigh_kernel, out_shape=jax.ShapeDtypeStruct((SPECTRA, hal...  7.92 us
  transfers between devices with their start and end apart: 30, of which 11 were waited for; matrix products, arithmetic and copies ran while one was open for 17% of the time, Pallas kernels for 19%

profile of v1, /device:TPU:0, one launch (start us, length us, event | category | flops | bytes accessed | tf_op | source)
XLA Modules:
  0.0 211.8 jit_solution(9654203493799021970)
XLA Ops:
  11.7 4.0 %convolution_convert_fusion.table = bf16[128,4096]{1,0:T(8,128)(2,1)} fusion(bf16[512,4096]{1,0:T(8,128)(2,1)} %constant.101.clone, f32[512]{0:T(512)S(1)} %bitcast.19, s32[512]{0:T(512)S(1)} %copy-done.13, s32[128]{0:T(128)S(1)} %fusion.21), kind=kOutput, calls=%fused_computation | convolution fusion | flops 537526272 | bytes 5247488 | tf_op jit(solution)/shard_map/dot_general | solution.py:238
  15.6 6.8 %collective-permute-done.3 = bf16[2,128,1024]{2,1,0:T(8,128)(2,1)} collective-permute-done((bf16[2,128,1024]{2,1,0:T(8,128)(2,1)}, bf16[2,128,1024]{2,1,0:T(8,128)(2,1)}, u32[]{:S(2)}, u32[]{:S(2)}) %collective-permute-start.3) | collective-permute-done | bytes 524320 | tf_op jit(solution)/shard_map/ppermute | solution.py:43
  25.4 7.9 %weigh.1.weighted = bf16[8,128,2048]{2,1,0:T(8,128)(2,1)} custom-call(s32[3]{0:T(128)} %pad_add_fusion.place, bf16[2,256,4096]{2,1,0:T(8,128)(2,1)} %voltage.1, bf16[2,128,4096]{2,1,0:T(8,128)(2,1)} %collective-permute-done.other, bf16[2,128,2048]{2,1,0:T(8,128)(2,1)} %broadcast_select_fusion.after, bf16[2,128,1024]{2,1,0:T(8,128)(2,1)} %broadcast_select_fusion.1.before, ...), custom_call_target="tpu_custom_call" | custom-call | tf_op jit(solution)/shard_map/weigh/pallas_call | solution.py:90
  33.3 4.9 %transform.9 = bf16[128,16,128]{2,1,0:T(8,128)(2,1)} custom-call(bf16[128,4096]{1,0:T(8,128)(2,1)} %convolution_convert_fusion.table, bf16[8,128,2048]{2,1,0:T(8,128)(2,1)} %weigh.1.weighted), custom_call_target="tpu_custom_call" | custom-call | tf_op jit(solution)/shard_map/transform/pallas_call | solution.py:126
  38.1 19.1 %all-to-all-start.4 = ((bf16[32,4,16,128]{3,2,1,0:T(8,128)(2,1)}), bf16[32,4,16,128]{3,2,1,0:T(8,128)(2,1)S(1)}, u32[]{:S(2)}, u32[]{:S(2)}) async-start(bf16[32,4,16,128]{3,2,1,0:T(8,128)(2,1)} %bitcast.18), calls=%async_computation.4 | async-start | bytes 1048576 | tf_op jit(solution)/shard_map/all_to_all | solution.py:259
  57.2 3.9 %convolution_convert_fusion.1.table = bf16[128,4096]{1,0:T(8,128)(2,1)} fusion(bf16[512,4096]{1,0:T(8,128)(2,1)} %constant.101.clone, f32[512]{0:T(512)S(1)} %bitcast.20, s32[512]{0:T(512)S(1)} %copy-done.13, s32[128]{0:T(128)S(1)} %add_add_fusion), kind=kOutput, calls=%fused_computation.1 | convolution fusion | flops 537526272 | bytes 5247488 | tf_op jit(solution)/shard_map/dot_general | solution.py:238
  61.2 4.8 %transform.8 = bf16[128,16,128]{2,1,0:T(8,128)(2,1)} custom-call(bf16[128,4096]{1,0:T(8,128)(2,1)} %convolution_convert_fusion.1.table, bf16[8,128,2048]{2,1,0:T(8,128)(2,1)} %weigh.1.weighted), custom_call_target="tpu_custom_call" | custom-call | tf_op jit(solution)/shard_map/transform/pallas_call | solution.py:126
  69.0 4.4 %all-to-all-start.3 = ((bf16[32,4,16,128]{3,2,1,0:T(8,128)(2,1)}), bf16[32,4,16,128]{3,2,1,0:T(8,128)(2,1)S(1)}, u32[]{:S(2)}, u32[]{:S(2)}) async-start(bf16[32,4,16,128]{3,2,1,0:T(8,128)(2,1)} %bitcast.16), calls=%async_computation.3 | async-start | bytes 1048576 | tf_op jit(solution)/shard_map/all_to_all | solution.py:259
  73.4 3.9 %convolution_convert_fusion.2.table = bf16[128,4096]{1,0:T(8,128)(2,1)} fusion(bf16[512,4096]{1,0:T(8,128)(2,1)} %constant.101.clone, f32[512]{0:T(512)S(1)} %bitcast.21, s32[512]{0:T(512)S(1)} %copy-done.13, s32[128]{0:T(128)S(1)} %add_add_fusion.1), kind=kOutput, calls=%fused_computation.2 | convolution fusion | flops 537526272 | bytes 5247488 | tf_op jit(solution)/shard_map/dot_general | solution.py:238
  77.4 4.9 %transform.7 = bf16[128,16,128]{2,1,0:T(8,128)(2,1)} custom-call(bf16[128,4096]{1,0:T(8,128)(2,1)} %convolution_convert_fusion.2.table, bf16[8,128,2048]{2,1,0:T(8,128)(2,1)} %weigh.1.weighted), custom_call_target="tpu_custom_call" | custom-call | tf_op jit(solution)/shard_map/transform/pallas_call | solution.py:126
  85.2 4.4 %all-to-all-start.2 = ((bf16[32,4,16,128]{3,2,1,0:T(8,128)(2,1)}), bf16[32,4,16,128]{3,2,1,0:T(8,128)(2,1)S(1)}, u32[]{:S(2)}, u32[]{:S(2)}) async-start(bf16[32,4,16,128]{3,2,1,0:T(8,128)(2,1)} %bitcast.17), calls=%async_computation.2 | async-start | bytes 1048576 | tf_op jit(solution)/shard_map/all_to_all | solution.py:259
  89.6 3.9 %convolution_convert_fusion.3.table = bf16[128,4096]{1,0:T(8,128)(2,1)} fusion(bf16[512,4096]{1,0:T(8,128)(2,1)} %constant.101.clone, f32[512]{0:T(512)S(1)} %bitcast.22, s32[512]{0:T(512)S(1)} %copy-done.13, s32[128]{0:T(128)S(1)} %add_add_fusion.2), kind=kOutput, calls=%fused_computation.3 | convolution fusion | flops 537526272 | bytes 5247488 | tf_op jit(solution)/shard_map/dot_general | solution.py:238
  93.6 4.8 %transform.6 = bf16[128,16,128]{2,1,0:T(8,128)(2,1)} custom-call(bf16[128,4096]{1,0:T(8,128)(2,1)} %convolution_convert_fusion.3.table, bf16[8,128,2048]{2,1,0:T(8,128)(2,1)} %weigh.1.weighted), custom_call_target="tpu_custom_call" | custom-call | tf_op jit(solution)/shard_map/transform/pallas_call | solution.py:126
  101.4 4.4 %all-to-all-start.1 = ((bf16[32,4,16,128]{3,2,1,0:T(8,128)(2,1)}), bf16[32,4,16,128]{3,2,1,0:T(8,128)(2,1)S(1)}, u32[]{:S(2)}, u32[]{:S(2)}) async-start(bf16[32,4,16,128]{3,2,1,0:T(8,128)(2,1)} %bitcast.14), calls=%async_computation.1 | async-start | bytes 1048576 | tf_op jit(solution)/shard_map/all_to_all | solution.py:259
  116.3 4.8 %transform.5 = bf16[128,16,128]{2,1,0:T(8,128)(2,1)} custom-call(bf16[128,4096]{1,0:T(8,128)(2,1)} %convolution_convert_fusion.4.table, bf16[8,128,2048]{2,1,0:T(8,128)(2,1)} %weigh.1.weighted), custom_call_target="tpu_custom_call" | custom-call | tf_op jit(solution)/shard_map/transform/pallas_call | solution.py:126
  121.1 7.4 %all-to-all-start = ((bf16[32,4,16,128]{3,2,1,0:T(8,128)(2,1)}), bf16[32,4,16,128]{3,2,1,0:T(8,128)(2,1)S(1)}, u32[]{:S(2)}, u32[]{:S(2)}) async-start(bf16[32,4,16,128]{3,2,1,0:T(8,128)(2,1)} %bitcast.15), calls=%async_computation | async-start | bytes 1048576 | tf_op jit(solution)/shard_map/all_to_all | solution.py:259
  135.1 5.2 %all-to-all-done.own = bf16[32,4,16,128]{3,2,1,0:T(8,128)(2,1)S(1)} async-done(((bf16[32,4,16,128]{3,2,1,0:T(8,128)(2,1)}), bf16[32,4,16,128]{3,2,1,0:T(8,128)(2,1)S(1)}, u32[]{:S(2)}, u32[]{:S(2)}) %all-to-all-start) | async-done | bytes 524320 | tf_op jit(solution)/shard_map/all_to_all | solution.py:259
  150.3 5.2 %collective-permute-done.9.left = bf16[32,4,16,128]{3,2,1,0:T(8,128)(2,1)S(1)} collective-permute-done((bf16[32,4,16,128]{3,2,1,0:T(8,128)(2,1)S(1)}, bf16[32,4,16,128]{3,2,1,0:T(8,128)(2,1)S(1)}, u32[]{:S(2)}, u32[]{:S(2)}) %collective-permute-start.9) | collective-permute-done | bytes 524320 | tf_op jit(solution)/shard_map/ppermute | solution.py:43
  157.6 9.2 %collective-permute-done.5.left = bf16[32,4,16,128]{3,2,1,0:T(8,128)(2,1)S(1)} collective-permute-done((bf16[32,4,16,128]{3,2,1,0:T(8,128)(2,1)S(1)}, bf16[32,4,16,128]{3,2,1,0:T(8,128)(2,1)S(1)}, u32[]{:S(2)}, u32[]{:S(2)}) %collective-permute-start.5) | collective-permute-done | bytes 524320 | tf_op jit(solution)/shard_map/ppermute | solution.py:43
  185.3 5.3 %correlate.5.rest_0_ = bf16[20,2,256,1024]{3,2,1,0:T(8,128)(2,1)} custom-call(s32[3]{0:T(128)} %pad_add_fusion.place, bf16[32,4,16,128]{3,2,1,0:T(8,128)(2,1)} %copy-done.5, bf16[32,4,16,128]{3,2,1,0:T(8,128)(2,1)} %collective-permute-done.21.left, bf16[32,4,16,128]{3,2,1,0:T(8,128)(2,1)} %collective-permute-done.22.right, ...), custom_call_target="tpu_custom_call" | custom-call | tf_op jit(solution)/shard_map/correlate/pallas_call | solution.py:182
  190.6 5.3 %correlate.6.rest_0_ = bf16[20,2,256,1024]{3,2,1,0:T(8,128)(2,1)} custom-call(s32[3]{0:T(128)} %pad_add_fusion.place, bf16[32,4,16,128]{3,2,1,0:T(8,128)(2,1)} %copy-done.1, bf16[32,4,16,128]{3,2,1,0:T(8,128)(2,1)} %collective-permute-done.17.left, bf16[32,4,16,128]{3,2,1,0:T(8,128)(2,1)} %collective-permute-done.18.right, ...), custom_call_target="tpu_custom_call", output_to_operand_aliasing={{}: (6, {})} | custom-call | tf_op jit(solution)/shard_map/correlate/pallas_call | solution.py:182
  195.9 5.3 %correlate.7.rest_0_ = bf16[20,2,256,1024]{3,2,1,0:T(8,128)(2,1)} custom-call(s32[3]{0:T(128)} %pad_add_fusion.place, bf16[32,4,16,128]{3,2,1,0:T(8,128)(2,1)} %copy-done.2, bf16[32,4,16,128]{3,2,1,0:T(8,128)(2,1)} %copy-done.6, bf16[32,4,16,128]{3,2,1,0:T(8,128)(2,1)} %collective-permute-done.14.right, ...), custom_call_target="tpu_custom_call", output_to_operand_aliasing={{}: (6, {})} | custom-call | tf_op jit(solution)/shard_map/correlate/pallas_call | solution.py:182
  201.2 5.3 %correlate.8.rest_0_ = bf16[20,2,256,1024]{3,2,1,0:T(8,128)(2,1)} custom-call(s32[3]{0:T(128)} %pad_add_fusion.place, bf16[32,4,16,128]{3,2,1,0:T(8,128)(2,1)} %copy-done.3, bf16[32,4,16,128]{3,2,1,0:T(8,128)(2,1)} %copy-done.7, bf16[32,4,16,128]{3,2,1,0:T(8,128)(2,1)} %collective-permute-done.10.right, ...), custom_call_target="tpu_custom_call", output_to_operand_aliasing={{}: (6, {})} | custom-call | tf_op jit(solution)/shard_map/correlate/pallas_call | solution.py:182
  206.5 5.3 %correlate.9 = bf16[20,2,256,1024]{3,2,1,0:T(8,128)(2,1)} custom-call(s32[3]{0:T(128)} %pad_add_fusion.place, bf16[32,4,16,128]{3,2,1,0:T(8,128)(2,1)} %copy-done.4, bf16[32,4,16,128]{3,2,1,0:T(8,128)(2,1)} %copy-done.8, bf16[32,4,16,128]{3,2,1,0:T(8,128)(2,1)} %copy-done.9, ...), custom_call_target="tpu_custom_call", output_to_operand_aliasing={{}: (6, {})} | custom-call | tf_op jit(solution)/shard_map/correlate/pallas_call | solution.py:182
  (104 shorter events, 71.1 us)
Async XLA Ops:
  1.9 23.5 %collective-permute-start = (bf16[2,128,4096]{2,1,0:T(8,128)(2,1)S(1)}, bf16[2,128,4096]{2,1,0:T(8,128)(2,1)}, u32[]{:S(2)}, u32[]{:S(2)}) collective-permute-start(bf16[2,128,4096]{2,1,0:T(8,128)(2,1)S(1)} %constant_dynamic-slice_fusion), channel_id=1, source_target_pairs={{0,1},{1,0},{2,3},{3,2},{4,5},{5,4},{6,7},{7,6},{8,9},{9,8},{10,11... | collective-permute-start | bytes 6291464 | tf_op jit(solution)/shard_map/ppermute | solution.py:43
  4.3 20.0 %collective-permute-start.1 = (bf16[2,128,2048]{2,1,0:T(8,128)(2,1)}, bf16[2,128,2048]{2,1,0:T(8,128)(2,1)S(1)}, u32[]{:S(2)}, u32[]{:S(2)}) collective-permute-start(bf16[2,128,2048]{2,1,0:T(8,128)(2,1)} %get-tuple-element.8), channel_id=1, source_target_pairs={{2,0},{4,2},{6,4},{8,6},{10,8},{12,10},{14,12},{16,14},{18,16},{20... | collective-permute-start | bytes 3145736 | tf_op jit(solution)/shard_map/ppermute | solution.py:43
  5.6 18.7 %collective-permute-start.2 = (bf16[2,128,2048]{2,1,0:T(8,128)(2,1)}, bf16[2,128,2048]{2,1,0:T(8,128)(2,1)}, u32[]{:S(2)}, u32[]{:S(2)}) collective-permute-start(bf16[2,128,2048]{2,1,0:T(8,128)(2,1)} %get-tuple-element.7), channel_id=1, source_target_pairs={{2,1},{4,3},{6,5},{8,7},{10,9},{12,11},{14,13},{16,15},{18,17},{20... | collective-permute-start | bytes 3145736 | tf_op jit(solution)/shard_map/ppermute | solution.py:43
  38.1 30.8 %all-to-all-start.4 = ((bf16[32,4,16,128]{3,2,1,0:T(8,128)(2,1)}), bf16[32,4,16,128]{3,2,1,0:T(8,128)(2,1)S(1)}, u32[]{:S(2)}, u32[]{:S(2)}) async-start(bf16[32,4,16,128]{3,2,1,0:T(8,128)(2,1)} %bitcast.18), calls=%async_computation.4 | async-start | bytes 1048576 | tf_op jit(solution)/shard_map/all_to_all | solution.py:259
  101.4 19.8 %all-to-all-start.1 = ((bf16[32,4,16,128]{3,2,1,0:T(8,128)(2,1)}), bf16[32,4,16,128]{3,2,1,0:T(8,128)(2,1)S(1)}, u32[]{:S(2)}, u32[]{:S(2)}) async-start(bf16[32,4,16,128]{3,2,1,0:T(8,128)(2,1)} %bitcast.14), calls=%async_computation.1 | async-start | bytes 1048576 | tf_op jit(solution)/shard_map/all_to_all | solution.py:259
  105.8 22.7 %collective-permute-start.21 = (bf16[32,4,16,128]{3,2,1,0:T(8,128)(2,1)S(1)}, bf16[32,4,16,128]{3,2,1,0:T(8,128)(2,1)}, u32[]{:S(2)}, u32[]{:S(2)}) collective-permute-start(bf16[32,4,16,128]{3,2,1,0:T(8,128)(2,1)S(1)} %all-to-all-done.4.own), channel_id=1, source_target_pairs={{0,32},{32,64},{64,96},{96,0},{1,33},{33,65},{65,97},{97,1},{2,34}... | collective-permute-start | bytes 1572872 | tf_op jit(solution)/shard_map/ppermute | solution.py:43
  107.4 24.5 %collective-permute-start.22 = (bf16[32,4,16,128]{3,2,1,0:T(8,128)(2,1)S(1)}, bf16[32,4,16,128]{3,2,1,0:T(8,128)(2,1)}, u32[]{:S(2)}, u32[]{:S(2)}) collective-permute-start(bf16[32,4,16,128]{3,2,1,0:T(8,128)(2,1)S(1)} %all-to-all-done.4.own), channel_id=1, source_target_pairs={{0,96},{32,0},{64,32},{96,64},{1,97},{33,1},{65,33},{97,65},{2,98}... | collective-permute-start | bytes 1572872 | tf_op jit(solution)/shard_map/ppermute | solution.py:43
  109.1 24.1 %collective-permute-start.17 = (bf16[32,4,16,128]{3,2,1,0:T(8,128)(2,1)S(1)}, bf16[32,4,16,128]{3,2,1,0:T(8,128)(2,1)}, u32[]{:S(2)}, u32[]{:S(2)}) collective-permute-start(bf16[32,4,16,128]{3,2,1,0:T(8,128)(2,1)S(1)} %all-to-all-done.3.own), channel_id=1, source_target_pairs={{0,32},{32,64},{64,96},{96,0},{1,33},{33,65},{65,97},{97,1},{2,34}... | collective-permute-start | bytes 1572872 | tf_op jit(solution)/shard_map/ppermute | solution.py:43
  109.4 30.9 %collective-permute-start.18 = (bf16[32,4,16,128]{3,2,1,0:T(8,128)(2,1)S(1)}, bf16[32,4,16,128]{3,2,1,0:T(8,128)(2,1)}, u32[]{:S(2)}, u32[]{:S(2)}) collective-permute-start(bf16[32,4,16,128]{3,2,1,0:T(8,128)(2,1)S(1)} %all-to-all-done.3.own), channel_id=1, source_target_pairs={{0,96},{32,0},{64,32},{96,64},{1,97},{33,1},{65,33},{97,65},{2,98}... | collective-permute-start | bytes 1572872 | tf_op jit(solution)/shard_map/ppermute | solution.py:43
  112.4 32.0 %collective-permute-start.13 = (bf16[32,4,16,128]{3,2,1,0:T(8,128)(2,1)S(1)}, bf16[32,4,16,128]{3,2,1,0:T(8,128)(2,1)S(1)}, u32[]{:S(2)}, u32[]{:S(2)}) collective-permute-start(bf16[32,4,16,128]{3,2,1,0:T(8,128)(2,1)S(1)} %all-to-all-done.2.own), channel_id=1, source_target_pairs={{0,32},{32,64},{64,96},{96,0},{1,33},{33,65},{65,97},{97,1},{2,34}... | collective-permute-start | bytes 1572872 | tf_op jit(solution)/shard_map/ppermute | solution.py:43
  121.1 19.1 %all-to-all-start = ((bf16[32,4,16,128]{3,2,1,0:T(8,128)(2,1)}), bf16[32,4,16,128]{3,2,1,0:T(8,128)(2,1)S(1)}, u32[]{:S(2)}, u32[]{:S(2)}) async-start(bf16[32,4,16,128]{3,2,1,0:T(8,128)(2,1)} %bitcast.15), calls=%async_computation | async-start | bytes 1048576 | tf_op jit(solution)/shard_map/all_to_all | solution.py:259
  128.5 21.2 %collective-permute-start.14 = (bf16[32,4,16,128]{3,2,1,0:T(8,128)(2,1)S(1)}, bf16[32,4,16,128]{3,2,1,0:T(8,128)(2,1)}, u32[]{:S(2)}, u32[]{:S(2)}) collective-permute-start(bf16[32,4,16,128]{3,2,1,0:T(8,128)(2,1)S(1)} %all-to-all-done.2.own), channel_id=1, source_target_pairs={{0,96},{32,0},{64,32},{96,64},{1,97},{33,1},{65,33},{97,65},{2,98}... | collective-permute-start | bytes 1572872 | tf_op jit(solution)/shard_map/ppermute | solution.py:43
  131.8 23.7 %collective-permute-start.9 = (bf16[32,4,16,128]{3,2,1,0:T(8,128)(2,1)S(1)}, bf16[32,4,16,128]{3,2,1,0:T(8,128)(2,1)S(1)}, u32[]{:S(2)}, u32[]{:S(2)}) collective-permute-start(bf16[32,4,16,128]{3,2,1,0:T(8,128)(2,1)S(1)} %all-to-all-done.1.own), channel_id=1, source_target_pairs={{0,32},{32,64},{64,96},{96,0},{1,33},{33,65},{65,97},{97,1},{2,34}... | collective-permute-start | bytes 1572872 | tf_op jit(solution)/shard_map/ppermute | solution.py:43
  133.2 23.9 %collective-permute-start.10 = (bf16[32,4,16,128]{3,2,1,0:T(8,128)(2,1)S(1)}, bf16[32,4,16,128]{3,2,1,0:T(8,128)(2,1)}, u32[]{:S(2)}, u32[]{:S(2)}) collective-permute-start(bf16[32,4,16,128]{3,2,1,0:T(8,128)(2,1)S(1)} %all-to-all-done.1.own), channel_id=1, source_target_pairs={{0,96},{32,0},{64,32},{96,64},{1,97},{33,1},{65,33},{97,65},{2,98}... | collective-permute-start | bytes 1572872 | tf_op jit(solution)/shard_map/ppermute | solution.py:43
  140.3 26.5 %collective-permute-start.5 = (bf16[32,4,16,128]{3,2,1,0:T(8,128)(2,1)S(1)}, bf16[32,4,16,128]{3,2,1,0:T(8,128)(2,1)S(1)}, u32[]{:S(2)}, u32[]{:S(2)}) collective-permute-start(bf16[32,4,16,128]{3,2,1,0:T(8,128)(2,1)S(1)} %all-to-all-done.own), channel_id=1, source_target_pairs={{0,32},{32,64},{64,96},{96,0},{1,33},{33,65},{65,97},{97,1},{2,34}... | collective-permute-start | bytes 1572872 | tf_op jit(solution)/shard_map/ppermute | solution.py:43
  144.3 24.0 %collective-permute-start.6 = (bf16[32,4,16,128]{3,2,1,0:T(8,128)(2,1)S(1)}, bf16[32,4,16,128]{3,2,1,0:T(8,128)(2,1)S(1)}, u32[]{:S(2)}, u32[]{:S(2)}) collective-permute-start(bf16[32,4,16,128]{3,2,1,0:T(8,128)(2,1)S(1)} %all-to-all-done.own), channel_id=1, source_target_pairs={{0,96},{32,0},{64,32},{96,64},{1,97},{33,1},{65,33},{97,65},{2,98}... | collective-permute-start | bytes 1572872 | tf_op jit(solution)/shard_map/ppermute | solution.py:43
  149.8 24.6 %collective-permute-start.23 = (bf16[16,4,16,128]{3,2,1,0:T(8,128)(2,1)S(1)}, bf16[16,4,16,128]{3,2,1,0:T(8,128)(2,1)S(1)}, u32[]{:S(2)}, u32[]{:S(2)}) collective-permute-start(bf16[16,4,16,128]{3,2,1,0:T(8,128)(2,1)S(1)} %slice.64), channel_id=1, source_target_pairs={{0,32},{32,64},{64,96},{96,0},{1,33},{33,65},{65,97},{97,1},{2,34}... | collective-permute-start | bytes 786440 | tf_op jit(solution)/shard_map/ppermute | solution.py:43
  155.5 21.5 %collective-permute-start.24 = (bf16[16,4,16,128]{3,2,1,0:T(8,128)(2,1)S(1)}, bf16[16,4,16,128]{3,2,1,0:T(8,128)(2,1)S(1)}, u32[]{:S(2)}, u32[]{:S(2)}) collective-permute-start(bf16[16,4,16,128]{3,2,1,0:T(8,128)(2,1)S(1)} %slice.65), channel_id=1, source_target_pairs={{0,96},{32,0},{64,32},{96,64},{1,97},{33,1},{65,33},{97,65},{2,98}... | collective-permute-start | bytes 786440 | tf_op jit(solution)/shard_map/ppermute | solution.py:43
  157.1 20.9 %collective-permute-start.19 = (bf16[16,4,16,128]{3,2,1,0:T(8,128)(2,1)S(1)}, bf16[16,4,16,128]{3,2,1,0:T(8,128)(2,1)S(1)}, u32[]{:S(2)}, u32[]{:S(2)}) collective-permute-start(bf16[16,4,16,128]{3,2,1,0:T(8,128)(2,1)S(1)} %slice.62), channel_id=1, source_target_pairs={{0,32},{32,64},{64,96},{96,0},{1,33},{33,65},{65,97},{97,1},{2,34}... | collective-permute-start | bytes 786440 | tf_op jit(solution)/shard_map/ppermute | solution.py:43
  174.3 21.6 %collective-permute-start.16 = (bf16[16,4,16,128]{3,2,1,0:T(8,128)(2,1)}, bf16[16,4,16,128]{3,2,1,0:T(8,128)(2,1)}, u32[]{:S(2)}, u32[]{:S(2)}) collective-permute-start(bf16[16,4,16,128]{3,2,1,0:T(8,128)(2,1)} %slice.61), channel_id=1, source_target_pairs={{0,96},{32,0},{64,32},{96,64},{1,97},{33,1},{65,33},{97,65},{2,98}... | collective-permute-start | bytes 786440 | tf_op jit(solution)/shard_map/ppermute | solution.py:43
  177.1 24.1 %collective-permute-start.11 = (bf16[16,4,16,128]{3,2,1,0:T(8,128)(2,1)}, bf16[16,4,16,128]{3,2,1,0:T(8,128)(2,1)}, u32[]{:S(2)}, u32[]{:S(2)}) collective-permute-start(bf16[16,4,16,128]{3,2,1,0:T(8,128)(2,1)} %slice.58), channel_id=1, source_target_pairs={{0,32},{32,64},{64,96},{96,0},{1,33},{33,65},{65,97},{97,1},{2,34}... | collective-permute-start | bytes 786440 | tf_op jit(solution)/shard_map/ppermute | solution.py:43
  178.0 23.2 %collective-permute-start.12 = (bf16[16,4,16,128]{3,2,1,0:T(8,128)(2,1)}, bf16[16,4,16,128]{3,2,1,0:T(8,128)(2,1)}, u32[]{:S(2)}, u32[]{:S(2)}) collective-permute-start(bf16[16,4,16,128]{3,2,1,0:T(8,128)(2,1)} %slice.59), channel_id=1, source_target_pairs={{0,96},{32,0},{64,32},{96,64},{1,97},{33,1},{65,33},{97,65},{2,98}... | collective-permute-start | bytes 786440 | tf_op jit(solution)/shard_map/ppermute | solution.py:43
  180.3 26.2 %collective-permute-start.7 = (bf16[16,4,16,128]{3,2,1,0:T(8,128)(2,1)}, bf16[16,4,16,128]{3,2,1,0:T(8,128)(2,1)}, u32[]{:S(2)}, u32[]{:S(2)}) collective-permute-start(bf16[16,4,16,128]{3,2,1,0:T(8,128)(2,1)} %slice.56), channel_id=1, source_target_pairs={{0,32},{32,64},{64,96},{96,0},{1,33},{33,65},{65,97},{97,1},{2,34}... | collective-permute-start | bytes 786440 | tf_op jit(solution)/shard_map/ppermute | solution.py:43
  183.7 22.8 %collective-permute-start.8 = (bf16[16,4,16,128]{3,2,1,0:T(8,128)(2,1)}, bf16[16,4,16,128]{3,2,1,0:T(8,128)(2,1)}, u32[]{:S(2)}, u32[]{:S(2)}) collective-permute-start(bf16[16,4,16,128]{3,2,1,0:T(8,128)(2,1)} %slice.57), channel_id=1, source_target_pairs={{0,96},{32,0},{64,32},{96,64},{1,97},{33,1},{65,33},{97,65},{2,98}... | collective-permute-start | bytes 786440 | tf_op jit(solution)/shard_map/ppermute | solution.py:43
  (21 other events, 478.6 us)

commit v2 on v0

v2 whole, which is shorter than its diff:
```python
import math

import jax
import jax.numpy as jnp
import ml_dtypes
import numpy as np
from jax import lax
from jax.experimental import pallas as pl
from jax.experimental.pallas import tpu as pltpu
from jax.sharding import PartitionSpec as P

CH = 1024
TAPS = 4
BAND_LO = 256
CAP = 20
CORES = 2
BLOCKS = 4
PIECES = (8, 12)
EARLY = ((0, 4),)
LATE = ((0, 1), (4, 3))
STEP = 2
AHEAD = (0, 3, 1, 2)
VMEM = 60 * 1024 * 1024
WEIGHT = pl.CostEstimate(flops=10**13, bytes_accessed=2 * 10**10, transcendentals=0)


def prototype():
    total = TAPS * CH
    position = np.arange(total).astype(np.float32)
    offset = (position - total / 2 + 0.5) / CH
    taper = 0.5 - 0.5 * np.cos(2 * np.pi * (position + 0.5) / total)
    coeffs = np.sinc(offset) * taper
    coeffs = coeffs * np.sqrt(CH / np.sum(coeffs * coeffs))
    return coeffs.reshape(TAPS, CH).astype(np.float32)


def tables(band):
    sample = np.arange(CH)
    channel = np.arange(band) + BAND_LO
    phase = (channel[:, None] * sample[None, :] % CH).astype(np.float32) * np.float32(2 * np.pi / CH)
    cosine = np.cos(phase).astype(ml_dtypes.bfloat16)
    sine = np.sin(phase).astype(ml_dtypes.bfloat16)
    return np.concatenate([cosine, sine], 1)


def after(value, *earlier):
    return lax.optimization_barrier((value,) + earlier)[0]


def pick_kernel(place, voltage, *rest):
    outs, sems = rest[:-1], rest[-1]
    core = place[0]
    half = voltage.shape[1] // CORES
    copies = []
    for k, out in enumerate(outs):
        width = out.shape[2]
        first = core * width if width < voltage.shape[2] else 0
        base = (1 - core if k + 1 == len(outs) else core) * half
        source = voltage.at[
            :, pl.ds(pl.multiple_of(base, half), half), pl.ds(pl.multiple_of(first, CH), width)
        ]
        copies.append(pltpu.make_async_copy(source, out, sems.at[k]))
    for copy in copies:
        copy.start()
    for copy in copies:
        copy.wait()


def pick(place, voltage, count, width):
    half = voltage.shape[1] // CORES
    return pl.pallas_call(
        pick_kernel,
        out_shape=[jax.ShapeDtypeStruct((2, half, width), jnp.bfloat16)] * count,
        in_specs=[pl.BlockSpec(memory_space=pltpu.SMEM), pl.BlockSpec(memory_space=pl.ANY)],
        out_specs=[pl.BlockSpec(memory_space=pltpu.VMEM)] * count,
        scratch_shapes=[pltpu.SemaphoreType.DMA((count,))],
        compiler_params=pltpu.CompilerParams(vmem_limit_bytes=VMEM),
        cost_estimate=WEIGHT,
        name="pick",
    )(place, voltage)


def channelize_kernel(windows, pieces, place, voltage, other, *rest):
    second = len(windows) == 2
    halo = rest[: 2 * second]
    rest = rest[2 * second :]
    coeffs, table = rest[:2]
    outs = rest[2:-5]
    held, weighted, chosen, spread, sems = rest[-5:]
    core = place[0]
    half = voltage.shape[1] // CORES
    own_rows = pl.ds(pl.multiple_of(core * half, half), half)
    tail = TAPS - 1
    fetch = pltpu.make_async_copy(table, chosen, sems.at[4])
    fetch.start()

    def load(parts):
        copies = []
        for source, first, count, at in parts:
            if source is voltage:
                block = voltage.at[:, own_rows, pl.ds(first * CH, count * CH)]
            else:
                block = source.at[:, :, pl.ds(first * CH, count * CH)]
            target = held.at[:, :, pl.ds(at * CH, count * CH)]
            copies.append(pltpu.make_async_copy(block, target, sems.at[len(copies)]))
        for copy in copies:
            copy.start()
        for copy in copies:
            copy.wait()

    def load_for(low, high, nearer):
        if second:
            previous, following = nearer
            load(
                [
                    (previous, 1, 1, 0),
                    (low, 0, tail, 1),
                    (high, 0, BLOCKS, BLOCKS),
                    (following, 0, 2, 2 * BLOCKS),
                ]
            )
        else:
            load([(low, 0, BLOCKS, 0), (high, 0, tail, BLOCKS)])

    @pl.when(core == 0)
    def _():
        load_for(voltage, other, halo[::-1])

    @pl.when(core != 0)
    def _():
        load_for(other, voltage, halo)

    keep = place[2].astype(jnp.float32)
    rows = 16
    width = 256

    def step(index, carry):
        at = pl.ds(pl.multiple_of(index * rows, rows), rows)
        for z in range(2):
            for start in range(0, CH, width):
                taps = [coeffs[p : p + 1, pl.ds(start, width)] for p in range(TAPS)]
                s = 0
                for window, (base, count) in enumerate(windows):
                    blocks = [
                        held[z, at, pl.ds((base + b) * CH + start, width)].astype(jnp.float32)
                        for b in range(count + TAPS - 1)
                    ]
                    for k in range(count):
                        total = blocks[k] * taps[0]
                        for p in range(1, TAPS):
                            tap = taps[p] * keep if second and window == 0 else taps[p]
                            total = total + blocks[k + p] * tap
                        weighted[z, s, at, pl.ds(start, width)] = total.astype(jnp.bfloat16)
                        s += 1
        return carry

    lax.fori_loop(0, half // rows, step, 0)
    fetch.wait()
    owners = outs[0].shape[0]
    places = [(out, j) for out in outs for j in range(out.shape[1])]
    columns = BLOCKS * half
    samples = weighted[...].reshape(2 * columns, CH)
    base = 0
    for slots in pieces:
        number = owners * slots
        at = pl.ds(base, number)
        out, first = places[base // owners]
        both = jnp.concatenate([chosen[at, :CH], chosen[at, CH:]], 0)
        product = lax.dot_general(
            both, samples, (((1,), (1,)), ((), ())), preferred_element_type=jnp.float32
        )
        parts = (
            product[:number, :columns] + product[number:, columns:],
            product[:number, columns:] - product[number:, :columns],
        )
        for z in range(2):
            for s in range(BLOCKS):
                spread[pl.ds(z * BLOCKS + s, number, stride=2 * BLOCKS), :] = parts[z][
                    :, s * half : (s + 1) * half
                ]
        out[:, first : first + slots] = (
            spread[pl.ds(0, number * 2 * BLOCKS), :]
            .reshape(owners, slots, 2 * BLOCKS, half)
            .astype(jnp.bfloat16)
        )
        base += number


def channelize(place, voltage, other, halo, table, windows, pieces, sent, owners):
    half = voltage.shape[1] // CORES
    operands = (voltage, other) + halo
    span = sum(count + TAPS - 1 for _, count in windows)
    anywhere = pl.BlockSpec(memory_space=pl.ANY)
    vmem = pl.BlockSpec(memory_space=pltpu.VMEM)

    def kernel(*refs):
        channelize_kernel(windows, pieces, *refs)

    return pl.pallas_call(
        kernel,
        out_shape=[
            jax.ShapeDtypeStruct((owners, slots, 2 * BLOCKS, half), jnp.bfloat16)
            for slots in sent
        ],
        in_specs=[pl.BlockSpec(memory_space=pltpu.SMEM)]
        + [anywhere] * len(operands)
        + [vmem, anywhere],
        out_specs=[vmem] * len(sent),
        scratch_shapes=[
            pltpu.VMEM((2, half, span * CH), jnp.bfloat16),
            pltpu.VMEM((2, BLOCKS, half, CH), jnp.bfloat16),
            pltpu.VMEM(table.shape, jnp.bfloat16),
            pltpu.VMEM((owners * max(pieces) * 2 * BLOCKS, half), jnp.float32),
            pltpu.SemaphoreType.DMA((5,)),
        ],
        compiler_params=pltpu.CompilerParams(vmem_limit_bytes=VMEM),
        cost_estimate=WEIGHT,
        name="channelize",
    )(place, *operands, jnp.asarray(prototype()), table)


def gathered(part, j):
    count, _, rows, lanes = part.shape
    wide = part[:, j].astype(jnp.float32).reshape(count // CORES, CORES, rows, lanes)
    return jnp.concatenate([wide[:, core] for core in range(CORES)], 2)


def correlate_kernel(parts_of, place, *refs):
    out = refs[-1]
    me = place[1]
    group = out.shape[2]
    groups = out.shape[3] // group
    sources = []
    at = 0
    for count in parts_of:
        sources.append(refs[at : at + count])
        at += count
    scale = CORES / (2 * BLOCKS * refs[0].shape[0])
    row = lax.broadcasted_iota(jnp.int32, (1, 2 * BLOCKS, group), 1)
    sign = jnp.where(row < BLOCKS, -1.0, 1.0)
    for j in range(out.shape[0]):
        for ahead, source in zip(AHEAD, sources):
            wide = jnp.concatenate([gathered(piece, j) for piece in source], 0)
            if ahead == 0:
                mine = wide * scale
                turned = pltpu.roll(mine, BLOCKS, 1) * sign
                lhs = jnp.concatenate([mine, turned], 2)
                lhs = lhs.reshape(-1, 2 * group).astype(jnp.bfloat16)
                lhs = jnp.transpose(lhs)
            product = lax.dot_general(
                lhs,
                wide.reshape(-1, group).astype(jnp.bfloat16),
                (((1,), (0,)), ((), ())),
                preferred_element_type=jnp.float32,
            ).astype(jnp.bfloat16)
            at = pl.ds(pl.multiple_of(lax.rem(me + ahead, groups) * group, group), group)
            for z in range(2):
                out[j, z, :, at] = product[z * group : (z + 1) * group]


def correlate(place, sources, first, slots, shape, result):
    in_specs = []
    operands = []
    for ahead, source in zip(AHEAD, sources):
        for part, starts, axis in source:
            skip = (first - starts) // STEP
            if axis is None:
                block = (part.shape[0], STEP) + part.shape[2:]
            else:
                block = [None if k == axis else part.shape[k] for k in range(part.ndim)]
                block[2] = STEP
            groups = None if axis is None else part.shape[axis]

            def index(j, place, ahead=ahead, skip=skip, axis=axis, groups=groups):
                if axis is None:
                    return 0, skip + j, 0, 0
                which = lax.rem(place[1] + ahead, groups)
                return (which, 0, skip + j, 0, 0) if axis == 0 else (0, which, skip + j, 0, 0)

            in_specs.append(pl.BlockSpec(tuple(block), index))
            operands.append(part)
    parts_of = tuple(len(source) for source in sources)
    aliases = {}
    if result is not None:
        in_specs.append(pl.BlockSpec(memory_space=pl.ANY))
        aliases = {len(operands) + 1: 0}
        operands.append(result)

    def kernel(*refs):
        correlate_kernel(parts_of, *refs)

    return pl.pallas_call(
        kernel,
        out_shape=jax.ShapeDtypeStruct(shape, jnp.bfloat16),
        grid_spec=pltpu.PrefetchScalarGridSpec(
            num_scalar_prefetch=1,
            grid=(slots // STEP,),
            in_specs=in_specs,
            out_specs=pl.BlockSpec(
                (STEP,) + shape[1:], lambda j, place: (first // STEP + j, 0, 0, 0)
            ),
        ),
        input_output_aliases=aliases,
        compiler_params=pltpu.CompilerParams(
            dimension_semantics=("arbitrary",), vmem_limit_bytes=VMEM
        ),
        cost_estimate=WEIGHT,
        name="correlate",
    )(place, *operands)


def body(voltage, flags, owner_slot):
    owners = lax.axis_size("freq")
    groups = lax.axis_size("feed")
    chips = owners // CORES
    band = owner_slot.shape[0]
    feeds = voltage.shape[1]
    position = lax.axis_index("freq")
    place = jnp.stack(
        [position % CORES, lax.axis_index("feed"), (position >= CORES).astype(jnp.int32)]
    ).astype(jnp.int32)

    (given,) = pick(place, voltage, 1, voltage.shape[2])
    other = lax.ppermute(given, "freq", [(k, k ^ 1) for k in range(owners)])
    edges = pick(place, after(voltage, given), 2, 2 * CH)
    halo = []
    for k, edge in enumerate(edges):
        down = [(CORES * (c + 1), CORES * c + k) for c in range(chips - 1)]
        up = [(CORES * c + 1, CORES * ((c + 1) % chips) + 1 - k) for c in range(chips)]
        halo.append(lax.ppermute(edge, "freq", down + up))
    kept = flags[0].astype(jnp.float32) * (1.0 / math.sqrt(CH))
    slot = []
    first = 0
    for slots in PIECES:
        row = np.arange(owners * slots)
        slot.append(row // slots * CAP + first + row % slots)
        first += slots
    slot = jnp.asarray(np.concatenate(slot), jnp.int32)
    select = jnp.where(owner_slot[None, :] == slot[:, None], kept[None, :], 0.0)
    table = jnp.dot(
        select.astype(jnp.bfloat16), jnp.asarray(tables(band)), preferred_element_type=jnp.float32
    ).astype(jnp.bfloat16)

    def ring(value, steps):
        return lax.ppermute(value, "feed", [(k, (k + steps) % groups) for k in range(groups)])

    def exchanged(spectra):
        return lax.all_to_all(spectra, "freq", 0, 0, tiled=True)

    def far(left, right):
        middle = owners // 2
        return ring(left[:middle], 1), ring(right[middle:], -1)

    small, large = PIECES
    a0, a1 = channelize(place, after(voltage, *edges), other, (), table, EARLY, PIECES, PIECES, owners)
    all_a0 = lax.all_gather(a0, "feed")
    own_a1 = exchanged(a1)
    b0, b1 = channelize(place, voltage, other, tuple(halo), table, LATE, PIECES, PIECES, owners)
    b0, b1 = channelize(place, voltage, other, tuple(halo), table, LATE, PIECES, PIECES, owners)
    own_a1 = after(own_a1, b1)
    left_a1, right_a1 = ring(own_a1, 1), ring(own_a1, -1)
    far_a1 = far(left_a1, right_a1)
    own_b1 = exchanged(after(b1, own_a1, all_a0))
    own_b0 = exchanged(after(b0, own_b1, *far_a1))
    left_b1, right_b1 = ring(own_b1, 1), ring(own_b1, -1)
    left_b0, right_b0 = ring(own_b0, 1), ring(own_b0, -1)
    all_a0 = exchanged(after(jnp.swapaxes(all_a0, 0, 1), left_b1, right_b1))
    far_b1 = far(left_b1, right_b1)
    far_b0 = far(left_b0, right_b0)

    shape = (CAP, 2, feeds, feeds * groups)

    def whole(parts, first):
        return [
            [(part, first, None) for part in (group if isinstance(group, tuple) else (group,))]
            for group in parts
        ]

    early = whole((own_a1, left_a1, right_a1, far_a1), small)
    late = whole((own_b1, left_b1, right_b1, far_b1), small)
    sources = [one + two for one, two in zip(early, late)]
    result = correlate(place, sources, small, large, shape, None)
    late = whole((own_b0, left_b0, right_b0, far_b0), 0)
    sources = [[(all_a0, 0, 1)] + two for two in late]
    return correlate(place, sources, 0, small, shape, result)


def solution(mesh):
    placed = (P(None, "feed", "freq"), P("feed", None), P())
    return jax.shard_map(
        body, mesh=mesh, in_specs=placed, out_specs=P("freq", None, "feed", None), check_vma=False
    )
```

time: 513 us -> 179 us (0.35); the launches traced: 503 us -> 178 us
  waiting for transfers between devices: 255 us -> 40.4 us
  matrix products: 89.6 us -> 3.07 us
  local copies, waits for them, and re-layouts: 92.6 us -> 9.79 us
  Pallas kernels: 0 us -> 45.9 us
  other arithmetic: 41.7 us -> 0.64 us
  starting transfers between devices: 8.95 us -> 44.3 us
  blocking collectives: 0 us -> 20.4 us
    all_to_all x1 -> x3, waiting for transfers between devices: 132 us -> 15.5 us  [exchanged(): return lax.all_to_all(spectra, 'freq', 0, 0, tiled=True)]
    all_gather x1, waiting for transfers between devices: 118 us -> 12.9 us  [body(): all_a0 = lax.all_gather(a0, 'feed')]
    dot_general x7 -> x1, matrix products: 89.6 us -> 3.07 us  [body(): jnp.dot(select.astype(jnp.bfloat16), jnp.asarray(tables(band)), preferred...]
    pallas_call x0 -> x6, Pallas kernels: none -> 45.9 us  [the longest x2 20.1 us: correlate(): pl.pallas_call(kernel, out_shape=jax.ShapeDtypeStruct(shape, jnp.bfloat16...]
    reshape x2 -> x0, local copies, waits for them, and re-layouts: 33.9 us -> none  [body(): placed.reshape((CAP, owners) + complete.shape[1:])]
    convert_element_type x3 -> x0, other arithmetic: 26.2 us -> none  [the longest x1 16.2 us: correlate(): return (jnp.stack([real_vis, imag_vis], 1) * inverse).astype(jnp.bfloat16)]
    all_to_all x1 -> x3, starting transfers between devices: 7.66 us -> 28.7 us  [exchanged(): return lax.all_to_all(spectra, 'freq', 0, 0, tiled=True)]
    all_to_all x0 -> x1, blocking collectives: none -> 20.4 us  [exchanged(): return lax.all_to_all(spectra, 'freq', 0, 0, tiled=True)]
  transfers between devices with their start and end apart: 3 -> 19, of which waited for: 3 -> 8; matrix products, arithmetic and copies ran while one was open for 0% -> 7% of each run, Pallas kernels for 0% -> 19%
where the time goes in v2:
time: 179 us; the launch traced here: 178 us
  Pallas kernels  45.9 us (26%)
  starting transfers between devices  44.3 us (25%)
  waiting for transfers between devices  40.4 us (23%)
  blocking collectives  20.4 us (11%)
  between operations  13.6 us (8%)
  local copies, waits for them, and re-layouts  9.79 us (5%)
  matrix products  3.07 us (2%)
    all_to_all x3, starting transfers between devices, exchanged(): return lax.all_to_all(spectra, 'freq', 0, 0, tiled=True)  28.7 us
    all_to_all x1, blocking collectives, exchanged(): return lax.all_to_all(spectra, 'freq', 0, 0, tiled=True)  20.4 us
    pallas_call x2, Pallas kernels, correlate(): pl.pallas_call(kernel, out_shape=jax.ShapeDtypeStruct(shape, jnp.bfloat16...  20.1 us
    pallas_call x2, Pallas kernels, channelize(): pl.pallas_call(kernel, out_shape=[jax.ShapeDtypeStruct((owners, slots, 2...  18.4 us
    all_to_all x3, waiting for transfers between devices, exchanged(): return lax.all_to_all(spectra, 'freq', 0, 0, tiled=True)  15.5 us
    ppermute x12, starting transfers between devices, ring(): lax.ppermute(value, 'feed', [(k, (k + steps) % groups) for k in range(gro...  13 us
    all_gather x1, waiting for transfers between devices, body(): all_a0 = lax.all_gather(a0, 'feed')  12.9 us
    slice x6, local copies, waits for them, and re-layouts, far(): return (ring(left[:middle], 1), ring(right[middle:], -1))  7.91 us
  transfers between devices with their start and end apart: 19, of which 8 were waited for; matrix products, arithmetic and copies ran while one was open for 7% of the time, Pallas kernels for 19%

profile of v2, /device:TPU:0, one launch (start us, length us, event | category | flops | bytes accessed | tf_op | source)
XLA Modules:
  0.0 178.0 jit_solution(3414561365414505876)
XLA Ops:
  7.2 3.6 %pick.2 = bf16[2,128,4096]{2,1,0:T(8,128)(2,1)} custom-call(s32[3]{0:T(128)} %pad_add_fusion.place.refs_0_, bf16[2,256,4096]{2,1,0:T(8,128)(2,1)} %refs_1_.2), custom_call_target="tpu_custom_call" | custom-call | flops 9999999827968 | bytes 20000000000 | tf_op jit(solution)/shard_map/pick/pallas_call | solution.py:71
  10.9 3.8 %pick.3 = (bf16[2,128,2048]{2,1,0:T(8,128)(2,1)}, bf16[2,128,2048]{2,1,0:T(8,128)(2,1)}) custom-call(s32[3]{0:T(128)} %pad_add_fusion.place.refs_0_, bf16[2,256,4096]{2,1,0:T(8,128)(2,1)} %refs_1_.2), custom_call_target="tpu_custom_call" | custom-call | flops 9999999827968 | bytes 20000000000 | tf_op jit(solution)/shard_map/pick/pallas_call | solution.py:71
  17.4 3.1 %convolution_convert_fusion.refs_4_.refs_6_ = bf16[640,2048]{1,0:T(8,128)(2,1)} fusion(bf16[512,2048]{1,0:T(8,128)(2,1)S(1)} %copy-done.7, f32[512]{0:T(512)S(1)} %bitcast.10, s32[512]{0:T(512)S(1)} %copy-done.6, s32[640]{0:T(1024)S(1)} %copy-done.8), kind=kOutput, calls=%fused_computation | convolution fusion | flops 1344143360 | bytes 4725248 | tf_op jit(solution)/shard_map/dot_general | solution.py:340
  20.4 8.9 %channelize.2 = (bf16[32,8,8,128]{3,2,1,0:T(8,128)(2,1)}, bf16[32,12,8,128]{3,2,1,0:T(8,128)(2,1)}) custom-call(s32[3]{0:T(128)} %pad_add_fusion.place.refs_0_, bf16[2,256,4096]{2,1,0:T(8,128)(2,1)} %refs_1_.2, bf16[2,128,4096]{2,1,0:T(8,128)(2,1)} %collective-permute-done.refs_2_, f32[4,1024]{1,0:T(4,128)} %constant.34.clone.refs_3_.refs_5_, ...), custom_call_target="tpu_custom_call" | custom-call | flops 9999999827968 | bytes 20000000000 | tf_op jit(solution)/shard_map/channelize/pallas_call | solution.py:199
  29.4 13.3 %all-to-all-start = ((bf16[32,12,8,128]{3,2,1,0:T(8,128)(2,1)}), bf16[32,12,8,128]{3,2,1,0:T(8,128)(2,1)}, u32[]{:S(2)}, u32[]{:S(2)}) async-start(bf16[32,12,8,128]{3,2,1,0:T(8,128)(2,1)} %get-tuple-element.23), calls=%async_computation | async-start | bytes 1572864 | tf_op jit(solution)/shard_map/all_to_all | solution.py:348
  42.7 4.6 %collective-permute-done.2.refs_4_ = bf16[2,128,2048]{2,1,0:T(8,128)(2,1)} collective-permute-done((bf16[2,128,2048]{2,1,0:T(8,128)(2,1)}, bf16[2,128,2048]{2,1,0:T(8,128)(2,1)}, u32[]{:S(2)}, u32[]{:S(2)}) %collective-permute-start.2) | collective-permute-done | bytes 1048608 | tf_op jit(solution)/shard_map/ppermute | solution.py:330
  47.3 9.5 %channelize.3 = (bf16[32,8,8,128]{3,2,1,0:T(8,128)(2,1)}, bf16[32,12,8,128]{3,2,1,0:T(8,128)(2,1)}) custom-call(s32[3]{0:T(128)} %pad_add_fusion.place.refs_0_, bf16[2,256,4096]{2,1,0:T(8,128)(2,1)} %refs_1_.2, bf16[2,128,4096]{2,1,0:T(8,128)(2,1)} %collective-permute-done.refs_2_, bf16[2,128,2048]{2,1,0:T(8,128)(2,1)} %collective-permute-done.1.refs_3_, ...), custom_call_target="tpu_custom_call" | custom-call | flops 9999999827968 | bytes 20000000000 | tf_op jit(solution)/shard_map/channelize/pallas_call | solution.py:199
  57.2 2.8 %collective-permute-start.7 = (bf16[32,12,8,128]{3,2,1,0:T(8,128)(2,1)}, bf16[32,12,8,128]{3,2,1,0:T(8,128)(2,1)}, u32[]{:S(2)}, u32[]{:S(2)}) collective-permute-start(bf16[32,12,8,128]{3,2,1,0:T(8,128)(2,1)} %all-to-all-done.refs_1_), channel_id=1, source_target_pairs={{0,96},{32,0},{64,32},{96,64},{1,97},{33,1},{65,33},{97,65},{2,98}... | collective-permute-start | bytes 2359304 | tf_op jit(solution)/shard_map/ppermute | solution.py:345
  60.0 12.9 %all-gather.3.cloned.1.call-done = bf16[128,8,8,128]{3,2,1,0:T(8,128)(2,1)} async-done(((bf16[32,8,8,128]{3,2,1,0:T(8,128)(2,1)}), bf16[128,8,8,128]{3,2,1,0:T(8,128)(2,1)}) %all-gather.3.cloned.1.call-update) | async-done | bytes 2097168 | tf_op jit(solution)/shard_map/all_gather | solution.py:356
  72.9 10.6 %all-to-all-start.1 = ((bf16[32,12,8,128]{3,2,1,0:T(8,128)(2,1)}), bf16[32,12,8,128]{3,2,1,0:T(8,128)(2,1)S(1)}, u32[]{:S(2)}, u32[]{:S(2)}) async-start(bf16[32,12,8,128]{3,2,1,0:T(8,128)(2,1)} %get-tuple-element.25), calls=%async_computation.1 | async-start | bytes 1572864 | tf_op jit(solution)/shard_map/all_to_all | solution.py:348
  85.9 1.8 slice.24
  88.5 9.5 %all-to-all-done.1.refs_2_ = bf16[32,12,8,128]{3,2,1,0:T(8,128)(2,1)S(1)} async-done(((bf16[32,12,8,128]{3,2,1,0:T(8,128)(2,1)}), bf16[32,12,8,128]{3,2,1,0:T(8,128)(2,1)S(1)}, u32[]{:S(2)}, u32[]{:S(2)}) %all-to-all-start.1) | async-done | bytes 786464 | tf_op jit(solution)/shard_map/all_to_all | solution.py:348
  98.2 1.9 %collective-permute-start.3 = (bf16[32,12,8,128]{3,2,1,0:T(8,128)(2,1)S(1)}, bf16[32,12,8,128]{3,2,1,0:T(8,128)(2,1)S(1)}, u32[]{:S(2)}, u32[]{:S(2)}) collective-permute-start(bf16[32,12,8,128]{3,2,1,0:T(8,128)(2,1)S(1)} %all-to-all-done.1.refs_2_), channel_id=1, source_target_pairs={{0,32},{32,64},{64,96},{96,0},{1,33},{33,65},{65,97},{97,1},{2,34}... | collective-permute-start | bytes 2359304 | tf_op jit(solution)/shard_map/ppermute | solution.py:345
  100.1 20.4 %all_to_all.20.refs_2_ = bf16[32,8,8,128]{3,2,1,0:T(8,128)(2,1)S(1)} all-to-all(bf16[32,8,8,128]{3,2,1,0:T(8,128)(2,1)} %get-tuple-element.28), channel_id=1, replica_groups=mesh['feed'=4,'freq'=32] {'freq'}, dimensions={0} | all-to-all | bytes 1048576 | tf_op jit(solution)/shard_map/all_to_all | solution.py:348
  128.0 4.8 %all-to-all-start.2 = ((bf16[32,4,8,8,128]{4,3,2,1,0:T(8,128)(2,1)}), bf16[32,4,8,8,128]{4,3,2,1,0:T(8,128)(2,1)}, u32[]{:S(2)}, u32[]{:S(2)}) async-start(bf16[32,4,8,8,128]{4,3,2,1,0:T(8,128)(2,1)} %bitcast.8), calls=%async_computation.2 | async-start | bytes 4194304 | tf_op jit(solution)/shard_map/all_to_all | solution.py:348
  132.8 2.5 %collective-permute-done.10.refs_6_ = bf16[32,8,8,128]{3,2,1,0:T(8,128)(2,1)} collective-permute-done((bf16[32,8,8,128]{3,2,1,0:T(8,128)(2,1)S(1)}, bf16[32,8,8,128]{3,2,1,0:T(8,128)(2,1)}, u32[]{:S(2)}, u32[]{:S(2)}) %collective-permute-start.10) | collective-permute-done | bytes 524320 | tf_op jit(solution)/shard_map/ppermute | solution.py:345
  135.3 1.7 slice.27
  137.0 1.6 collective-permute-start.12
  138.6 1.7 slice.26
  140.7 3.1 %collective-permute-done.14.refs_10_ = bf16[16,12,8,128]{3,2,1,0:T(8,128)(2,1)} collective-permute-done((bf16[16,12,8,128]{3,2,1,0:T(8,128)(2,1)}, bf16[16,12,8,128]{3,2,1,0:T(8,128)(2,1)}, u32[]{:S(2)}, u32[]{:S(2)}) %collective-permute-start.14) | collective-permute-done | bytes 393248 | tf_op jit(solution)/shard_map/ppermute | solution.py:345
  143.7 1.7 collective-permute-done.13.refs_9_
  145.4 11.6 %correlate.2.refs_10_ = bf16[20,2,256,1024]{3,2,1,0:T(8,128)(2,1)} custom-call(s32[3]{0:T(128)} %pad_add_fusion.place.refs_0_, bf16[32,12,8,128]{3,2,1,0:T(8,128)(2,1)} %all-to-all-done.refs_1_, bf16[32,12,8,128]{3,2,1,0:T(8,128)(2,1)} %copy-done.1, bf16[32,12,8,128]{3,2,1,0:T(8,128)(2,1)} %collective-permute-done.5.refs_3_, ...), custom_call_target="tpu_custom_call" | custom-call | flops 9999999827968 | bytes 20000000000 | tf_op jit(solution)/shard_map/correlate/pallas_call | solution.py:292
  157.1 5.7 %all-to-all-done.2.refs_1_.refs_3_.refs_5_.refs_7_ = bf16[32,4,8,8,128]{4,3,2,1,0:T(8,128)(2,1)} async-done(((bf16[32,4,8,8,128]{4,3,2,1,0:T(8,128)(2,1)}), bf16[32,4,8,8,128]{4,3,2,1,0:T(8,128)(2,1)}, u32[]{:S(2)}, u32[]{:S(2)}) %all-to-all-start.2) | async-done | bytes 2097184 | tf_op jit(solution)/shard_map/all_to_all | solution.py:348
  162.7 8.5 %correlate.3 = bf16[20,2,256,1024]{3,2,1,0:T(8,128)(2,1)} custom-call(s32[3]{0:T(128)} %pad_add_fusion.place.refs_0_, bf16[32,4,8,8,128]{4,3,2,1,0:T(8,128)(2,1)} %all-to-all-done.2.refs_1_.refs_3_.refs_5_.refs_7_, bf16[32,8,8,128]{3,2,1,0:T(8,128)(2,1)} %copy-done.2, ...), custom_call_target="tpu_custom_call", output_to_operand_aliasing={{}: (10, {})} | custom-call | flops 9999999827968 | bytes 20000000000 | tf_op jit(solution)/shard_map/correlate/pallas_call | solution.py:292
  (50 shorter events, 15.2 us)
Async XLA Ops:
  6.5 66.3 %all-gather.3.cloned.1.call-start = ((), (), s32[]{:S(2)}) async-start(), calls=%async_computation.4 | async-start | bytes 2621440 | tf_op jit(solution)/shard_map/all_gather | solution.py:356
  10.8 9.6 %collective-permute-start = (bf16[2,128,4096]{2,1,0:T(8,128)(2,1)}, bf16[2,128,4096]{2,1,0:T(8,128)(2,1)}, u32[]{:S(2)}, u32[]{:S(2)}) collective-permute-start(bf16[2,128,4096]{2,1,0:T(8,128)(2,1)} %pick.2), channel_id=1, source_target_pairs={{0,1},{1,0},{2,3},{3,2},{4,5},{5,4},{6,7},{7,6},{8,9},{9,8},{10,11... | collective-permute-start | bytes 6291464 | tf_op jit(solution)/shard_map/ppermute | solution.py:324
  10.9 6.4 %copy-start.6 = (s32[512]{0:T(512)S(1)}, s32[512]{0:T(512)}, u32[]{:S(2)}) copy-start(s32[512]{0:T(512)} %param.9) | copy-start | bytes 6148
  10.9 6.4 %copy-start.7 = (bf16[512,2048]{1,0:T(8,128)(2,1)S(1)}, bf16[512,2048]{1,0:T(8,128)(2,1)}, u32[]{:S(2)}) copy-start(bf16[512,2048]{1,0:T(8,128)(2,1)} %constant.33.clone) | copy-start | bytes 6291460
  14.7 28.0 %collective-permute-start.1 = (bf16[2,128,2048]{2,1,0:T(8,128)(2,1)}, bf16[2,128,2048]{2,1,0:T(8,128)(2,1)}, u32[]{:S(2)}, u32[]{:S(2)}) collective-permute-start(bf16[2,128,2048]{2,1,0:T(8,128)(2,1)} %get-tuple-element.18), channel_id=1, source_target_pairs={{2,0},{4,2},{6,4},{8,6},{10,8},{12,10},{14,12},{16,14},{18,16},{20... | collective-permute-start | bytes 3145736 | tf_op jit(solution)/shard_map/ppermute | solution.py:330
  16.0 31.3 %collective-permute-start.2 = (bf16[2,128,2048]{2,1,0:T(8,128)(2,1)}, bf16[2,128,2048]{2,1,0:T(8,128)(2,1)}, u32[]{:S(2)}, u32[]{:S(2)}) collective-permute-start(bf16[2,128,2048]{2,1,0:T(8,128)(2,1)} %get-tuple-element.19), channel_id=1, source_target_pairs={{2,1},{4,3},{6,5},{8,7},{10,9},{12,11},{14,13},{16,15},{18,17},{20... | collective-permute-start | bytes 3145736 | tf_op jit(solution)/shard_map/ppermute | solution.py:330
  29.4 27.9 %all-to-all-start = ((bf16[32,12,8,128]{3,2,1,0:T(8,128)(2,1)}), bf16[32,12,8,128]{3,2,1,0:T(8,128)(2,1)}, u32[]{:S(2)}, u32[]{:S(2)}) async-start(bf16[32,12,8,128]{3,2,1,0:T(8,128)(2,1)} %get-tuple-element.23), calls=%async_computation | async-start | bytes 1572864 | tf_op jit(solution)/shard_map/all_to_all | solution.py:348
  57.2 26.2 %collective-permute-start.7 = (bf16[32,12,8,128]{3,2,1,0:T(8,128)(2,1)}, bf16[32,12,8,128]{3,2,1,0:T(8,128)(2,1)}, u32[]{:S(2)}, u32[]{:S(2)}) collective-permute-start(bf16[32,12,8,128]{3,2,1,0:T(8,128)(2,1)} %all-to-all-done.refs_1_), channel_id=1, source_target_pairs={{0,96},{32,0},{64,32},{96,64},{1,97},{33,1},{65,33},{97,65},{2,98}... | collective-permute-start | bytes 2359304 | tf_op jit(solution)/shard_map/ppermute | solution.py:345
  60.0 25.9 %collective-permute-start.5 = (bf16[32,12,8,128]{3,2,1,0:T(8,128)(2,1)}, bf16[32,12,8,128]{3,2,1,0:T(8,128)(2,1)}, u32[]{:S(2)}, u32[]{:S(2)}) collective-permute-start(bf16[32,12,8,128]{3,2,1,0:T(8,128)(2,1)} %all-to-all-done.refs_1_), channel_id=1, source_target_pairs={{0,32},{32,64},{64,96},{96,0},{1,33},{33,65},{65,97},{97,1},{2,34}... | collective-permute-start | bytes 2359304 | tf_op jit(solution)/shard_map/ppermute | solution.py:345
  72.9 25.2 %all-to-all-start.1 = ((bf16[32,12,8,128]{3,2,1,0:T(8,128)(2,1)}), bf16[32,12,8,128]{3,2,1,0:T(8,128)(2,1)S(1)}, u32[]{:S(2)}, u32[]{:S(2)}) async-start(bf16[32,12,8,128]{3,2,1,0:T(8,128)(2,1)} %get-tuple-element.25), calls=%async_computation.1 | async-start | bytes 1572864 | tf_op jit(solution)/shard_map/all_to_all | solution.py:348
  83.5 43.0 %copy-start = (bf16[128,8,8,128]{3,2,1,0:T(8,128)(2,1)S(1)}, bf16[128,8,8,128]{3,2,1,0:T(8,128)(2,1)}, u32[]{:S(2)}) copy-start(bf16[128,8,8,128]{3,2,1,0:T(8,128)(2,1)} %all-gather.3.cloned.1.call-done) | copy-start | bytes 6291460
  84.7 15.4 %collective-permute-start.8 = (bf16[16,12,8,128]{3,2,1,0:T(8,128)(2,1)S(1)}, bf16[16,12,8,128]{3,2,1,0:T(8,128)(2,1)}, u32[]{:S(2)}, u32[]{:S(2)}) collective-permute-start(bf16[16,12,8,128]{3,2,1,0:T(8,128)(2,1)S(1)} %slice.25), channel_id=1, source_target_pairs={{0,96},{32,0},{64,32},{96,64},{1,97},{33,1},{65,33},{97,65},{2,98}... | collective-permute-start | bytes 1179656 | tf_op jit(solution)/shard_map/ppermute | solution.py:345
  87.6 12.4 %collective-permute-start.6 = (bf16[16,12,8,128]{3,2,1,0:T(8,128)(2,1)}, bf16[16,12,8,128]{3,2,1,0:T(8,128)(2,1)}, u32[]{:S(2)}, u32[]{:S(2)}) collective-permute-start(bf16[16,12,8,128]{3,2,1,0:T(8,128)(2,1)} %slice.24), channel_id=1, source_target_pairs={{0,32},{32,64},{64,96},{96,0},{1,33},{33,65},{65,97},{97,1},{2,34}... | collective-permute-start | bytes 1179656 | tf_op jit(solution)/shard_map/ppermute | solution.py:345
  98.0 30.0 %copy-start.1 = (bf16[32,12,8,128]{3,2,1,0:T(8,128)(2,1)}, bf16[32,12,8,128]{3,2,1,0:T(8,128)(2,1)S(1)}, u32[]{:S(2)}) copy-start(bf16[32,12,8,128]{3,2,1,0:T(8,128)(2,1)S(1)} %all-to-all-done.1.refs_2_) | copy-start | bytes 2359300
  98.0 24.4 %collective-permute-start.4 = (bf16[32,12,8,128]{3,2,1,0:T(8,128)(2,1)S(1)}, bf16[32,12,8,128]{3,2,1,0:T(8,128)(2,1)S(1)}, u32[]{:S(2)}, u32[]{:S(2)}) collective-permute-start(bf16[32,12,8,128]{3,2,1,0:T(8,128)(2,1)S(1)} %all-to-all-done.1.refs_2_), channel_id=1, source_target_pairs={{0,96},{32,0},{64,32},{96,64},{1,97},{33,1},{65,33},{97,65},{2,98}... | collective-permute-start | bytes 2359304 | tf_op jit(solution)/shard_map/ppermute | solution.py:345
  98.2 26.7 %collective-permute-start.3 = (bf16[32,12,8,128]{3,2,1,0:T(8,128)(2,1)S(1)}, bf16[32,12,8,128]{3,2,1,0:T(8,128)(2,1)S(1)}, u32[]{:S(2)}, u32[]{:S(2)}) collective-permute-start(bf16[32,12,8,128]{3,2,1,0:T(8,128)(2,1)S(1)} %all-to-all-done.1.refs_2_), channel_id=1, source_target_pairs={{0,32},{32,64},{64,96},{96,0},{1,33},{33,65},{65,97},{97,1},{2,34}... | collective-permute-start | bytes 2359304 | tf_op jit(solution)/shard_map/ppermute | solution.py:345
  120.4 7.6 %copy-start.2 = (bf16[32,8,8,128]{3,2,1,0:T(8,128)(2,1)}, bf16[32,8,8,128]{3,2,1,0:T(8,128)(2,1)S(1)}, u32[]{:S(2)}) copy-start(bf16[32,8,8,128]{3,2,1,0:T(8,128)(2,1)S(1)} %all_to_all.20.refs_2_) | copy-start | bytes 1572868
  120.4 14.9 %collective-permute-start.10 = (bf16[32,8,8,128]{3,2,1,0:T(8,128)(2,1)S(1)}, bf16[32,8,8,128]{3,2,1,0:T(8,128)(2,1)}, u32[]{:S(2)}, u32[]{:S(2)}) collective-permute-start(bf16[32,8,8,128]{3,2,1,0:T(8,128)(2,1)S(1)} %all_to_all.20.refs_2_), channel_id=1, source_target_pairs={{0,96},{32,0},{64,32},{96,64},{1,97},{33,1},{65,33},{97,65},{2,98}... | collective-permute-start | bytes 1572872 | tf_op jit(solution)/shard_map/ppermute | solution.py:345
  120.9 17.8 %collective-permute-start.9 = (bf16[32,8,8,128]{3,2,1,0:T(8,128)(2,1)S(1)}, bf16[32,8,8,128]{3,2,1,0:T(8,128)(2,1)}, u32[]{:S(2)}, u32[]{:S(2)}) collective-permute-start(bf16[32,8,8,128]{3,2,1,0:T(8,128)(2,1)S(1)} %all_to_all.20.refs_2_), channel_id=1, source_target_pairs={{0,32},{32,64},{64,96},{96,0},{1,33},{33,65},{65,97},{97,1},{2,34}... | collective-permute-start | bytes 1572872 | tf_op jit(solution)/shard_map/ppermute | solution.py:345
  123.3 20.4 %collective-permute-start.14 = (bf16[16,12,8,128]{3,2,1,0:T(8,128)(2,1)}, bf16[16,12,8,128]{3,2,1,0:T(8,128)(2,1)}, u32[]{:S(2)}, u32[]{:S(2)}) collective-permute-start(bf16[16,12,8,128]{3,2,1,0:T(8,128)(2,1)} %slice.29), channel_id=1, source_target_pairs={{0,96},{32,0},{64,32},{96,64},{1,97},{33,1},{65,33},{97,65},{2,98}... | collective-permute-start | bytes 1179656 | tf_op jit(solution)/shard_map/ppermute | solution.py:345
  126.0 19.4 %collective-permute-start.13 = (bf16[16,12,8,128]{3,2,1,0:T(8,128)(2,1)}, bf16[16,12,8,128]{3,2,1,0:T(8,128)(2,1)}, u32[]{:S(2)}, u32[]{:S(2)}) collective-permute-start(bf16[16,12,8,128]{3,2,1,0:T(8,128)(2,1)} %slice.28), channel_id=1, source_target_pairs={{0,32},{32,64},{64,96},{96,0},{1,33},{33,65},{65,97},{97,1},{2,34}... | collective-permute-start | bytes 1179656 | tf_op jit(solution)/shard_map/ppermute | solution.py:345
  128.0 34.7 %all-to-all-start.2 = ((bf16[32,4,8,8,128]{4,3,2,1,0:T(8,128)(2,1)}), bf16[32,4,8,8,128]{4,3,2,1,0:T(8,128)(2,1)}, u32[]{:S(2)}, u32[]{:S(2)}) async-start(bf16[32,4,8,8,128]{4,3,2,1,0:T(8,128)(2,1)} %bitcast.8), calls=%async_computation.2 | async-start | bytes 4194304 | tf_op jit(solution)/shard_map/all_to_all | solution.py:348
  137.0 20.1 %collective-permute-start.12 = (bf16[16,8,8,128]{3,2,1,0:T(8,128)(2,1)}, bf16[16,8,8,128]{3,2,1,0:T(8,128)(2,1)}, u32[]{:S(2)}, u32[]{:S(2)}) collective-permute-start(bf16[16,8,8,128]{3,2,1,0:T(8,128)(2,1)} %slice.27), channel_id=1, source_target_pairs={{0,96},{32,0},{64,32},{96,64},{1,97},{33,1},{65,33},{97,65},{2,98}... | collective-permute-start | bytes 786440 | tf_op jit(solution)/shard_map/ppermute | solution.py:345
  140.3 16.8 %collective-permute-start.11 = (bf16[16,8,8,128]{3,2,1,0:T(8,128)(2,1)}, bf16[16,8,8,128]{3,2,1,0:T(8,128)(2,1)}, u32[]{:S(2)}, u32[]{:S(2)}) collective-permute-start(bf16[16,8,8,128]{3,2,1,0:T(8,128)(2,1)} %slice.26), channel_id=1, source_target_pairs={{0,32},{32,64},{64,96},{96,0},{1,33},{33,65},{65,97},{97,1},{2,34}... | collective-permute-start | bytes 786440 | tf_op jit(solution)/shard_map/ppermute | solution.py:345
  (4 other events, 16.4 us)
Sparse Core Ops, SparseCore 0:
  29.5 43.3 all-gather.2

commit v3 on v2

--- a/solution.py
+++ b/solution.py
@@ -18,7 +18,7 @@
 PIECES = (8, 12)
 EARLY = ((0, 4),)
 LATE = ((0, 1), (4, 3))
-STEP = 2
+STEP = 4
 AHEAD = (0, 3, 1, 2)
 VMEM = 60 * 1024 * 1024
 WEIGHT = pl.CostEstimate(flops=10**13, bytes_accessed=2 * 10**10, transcendentals=0)
@@ -45,6 +45,10 @@
 
 def after(value, *earlier):
     return lax.optimization_barrier((value,) + earlier)[0]
+
+
+def after_all(values, earlier):
+    return lax.optimization_barrier(tuple(values) + tuple(earlier))[: len(values)]
 
 
 def pick_kernel(place, voltage, *rest):
@@ -217,6 +221,31 @@
         cost_estimate=WEIGHT,
         name="channelize",
     )(place, *operands, jnp.asarray(prototype()), table)
+
+
+def pack_kernel(*refs):
+    out = refs[-1]
+    slots = refs[0].shape[1]
+    for k, ref in enumerate(refs[:4]):
+        out[:, k * slots : (k + 1) * slots] = ref[...]
+
+
+def pack(parts, wait):
+    count, slots, rows, lanes = parts[0].shape
+    step = count // 8
+    block = pl.BlockSpec((step, slots, rows, lanes), lambda k: (k, 0, 0, 0))
+    return pl.pallas_call(
+        pack_kernel,
+        grid=(count // step,),
+        out_shape=jax.ShapeDtypeStruct((count, len(parts) * slots, rows, lanes), jnp.bfloat16),
+        in_specs=[block] * len(parts),
+        out_specs=pl.BlockSpec((step, len(parts) * slots, rows, lanes), lambda k: (k, 0, 0, 0)),
+        compiler_params=pltpu.CompilerParams(
+            dimension_semantics=("arbitrary",), vmem_limit_bytes=VMEM
+        ),
+        cost_estimate=WEIGHT,
+        name="pack",
+    )(*after_all(parts, wait))
 
 
 def gathered(part, j):
@@ -304,7 +333,7 @@
         compiler_params=pltpu.CompilerParams(
             dimension_semantics=("arbitrary",), vmem_limit_bytes=VMEM
         ),
-        cost_estimate=WEIGHT,
+        cost_estimate=pl.CostEstimate(flops=10**10, bytes_accessed=4 * 10**7, transcendentals=0),
         name="correlate",
     )(place, *operands)
 
@@ -353,35 +382,39 @@
 
     small, large = PIECES
     a0, a1 = channelize(place, after(voltage, *edges), other, (), table, EARLY, PIECES, PIECES, owners)
-    all_a0 = lax.all_gather(a0, "feed")
+    left_a0, right_a0, far_a0 = ring(a0, 1), ring(a0, -1), ring(a0, 2)
     own_a1 = exchanged(a1)
-    b0, b1 = channelize(place, voltage, other, tuple(halo), table, LATE, PIECES, PIECES, owners)
-    b0, b1 = channelize(place, voltage, other, tuple(halo), table, LATE, PIECES, PIECES, owners)
-    own_a1 = after(own_a1, b1)
+    (b,) = channelize(place, voltage, other, tuple(halo), table, LATE, PIECES, (CAP,), owners)
+    (b,) = channelize(place, voltage, other, tuple(halo), table, LATE, PIECES, (CAP,), owners)
+    own_a1 = after(own_a1, b, left_a0, right_a0, far_a0)
     left_a1, right_a1 = ring(own_a1, 1), ring(own_a1, -1)
     far_a1 = far(left_a1, right_a1)
-    own_b1 = exchanged(after(b1, own_a1, all_a0))
-    own_b0 = exchanged(after(b0, own_b1, *far_a1))
+    own_b = exchanged(after(b, own_a1))
+    all_a0 = pack((a0, left_a0, right_a0, far_a0), (left_a1, right_a1))
+    own_b = after(own_b, all_a0)
+    ready_b = after(own_b, *far_a1)
+    own_b1 = ready_b[:, small:]
+    own_b0 = ready_b[:, :small]
     left_b1, right_b1 = ring(own_b1, 1), ring(own_b1, -1)
     left_b0, right_b0 = ring(own_b0, 1), ring(own_b0, -1)
-    all_a0 = exchanged(after(jnp.swapaxes(all_a0, 0, 1), left_b1, right_b1))
+    all_a0 = exchanged(after(all_a0, ready_b))
     far_b1 = far(left_b1, right_b1)
     far_b0 = far(left_b0, right_b0)
 
     shape = (CAP, 2, feeds, feeds * groups)
 
-    def whole(parts, first):
-        return [
+    def whole(own, parts, first):
+        return [[own]] + [
             [(part, first, None) for part in (group if isinstance(group, tuple) else (group,))]
             for group in parts
         ]
 
-    early = whole((own_a1, left_a1, right_a1, far_a1), small)
-    late = whole((own_b1, left_b1, right_b1, far_b1), small)
+    early = whole((own_a1, small, None), (left_a1, right_a1, far_a1), small)
+    late = whole((own_b, 0, None), (left_b1, right_b1, far_b1), small)
     sources = [one + two for one, two in zip(early, late)]
     result = correlate(place, sources, small, large, shape, None)
-    late = whole((own_b0, left_b0, right_b0, far_b0), 0)
-    sources = [[(all_a0, 0, 1)] + two for two in late]
+    late = whole((own_b, 0, None), (left_b0, right_b0, far_b0), 0)
+    sources = [[(all_a0, -small * k, None)] + two for k, two in enumerate(late)]
     return correlate(place, sources, 0, small, shape, result)
 
 

time: 179 us -> 155 us (0.87)
  blocking collectives: 20.4 us -> 0 us
  between operations: 13.6 us -> 0.28 us
  starting transfers between devices: 44.3 us -> 50.5 us
  Pallas kernels: 45.9 us -> 50 us
    ppermute x12 -> x15, waiting for transfers between devices: 7.32 us -> 34.5 us  [ring(): lax.ppermute(value, 'feed', [(k, (k + steps) % groups) for k in range(gro...]
    all_to_all x1 -> x0, blocking collectives: 20.4 us -> none  [exchanged(): return lax.all_to_all(spectra, 'freq', 0, 0, tiled=True)]
    all_gather x1 -> x0, waiting for transfers between devices: 12.9 us -> none  [body(): all_a0 = lax.all_gather(a0, 'feed')]
    all_to_all x3, waiting for transfers between devices: 15.5 us -> 4.77 us  [exchanged(): return lax.all_to_all(spectra, 'freq', 0, 0, tiled=True)]
    ppermute x12 -> x15, starting transfers between devices: 13 us -> 19.8 us  [ring(): lax.ppermute(value, 'feed', [(k, (k + steps) % groups) for k in range(gro...]
    pallas_call x0 -> x1, Pallas kernels: none -> 5.62 us  [pack(): pl.pallas_call(pack_kernel, grid=(count // step,), out_shape=jax.ShapeDty...]
    ppermute x2, waiting for transfers between devices: 4.62 us -> 0.29 us  [body(): halo.append(lax.ppermute(edge, 'freq', down + up))]
    slice x6, local copies, waits for them, and re-layouts: 7.91 us -> 4.53 us  [far(): return (ring(left[:middle], 1), ring(right[middle:], -1))]
  transfers between devices with their start and end apart: 19 -> 21, of which waited for: 8 -> 11; matrix products, arithmetic and copies ran while one was open for 7% -> 6% of each run, Pallas kernels for 19% -> 25%
where the time goes in v3:
time: 155 us; the launch traced here: 154 us
  starting transfers between devices  50.5 us (33%)
  Pallas kernels  50 us (32%)
  waiting for transfers between devices  39.6 us (26%)
  local copies, waits for them, and re-layouts  9.7 us (6%)
  matrix products  3.07 us (2%)
    ppermute x15, waiting for transfers between devices, ring(): lax.ppermute(value, 'feed', [(k, (k + steps) % groups) for k in range(gro...  34.5 us
    all_to_all x3, starting transfers between devices, exchanged(): return lax.all_to_all(spectra, 'freq', 0, 0, tiled=True)  28.1 us
    ppermute x15, starting transfers between devices, ring(): lax.ppermute(value, 'feed', [(k, (k + steps) % groups) for k in range(gro...  19.8 us
    pallas_call x2, Pallas kernels, channelize(): pl.pallas_call(kernel, out_shape=[jax.ShapeDtypeStruct((owners, slots, 2...  18.6 us
    pallas_call x2, Pallas kernels, correlate(): pl.pallas_call(kernel, out_shape=jax.ShapeDtypeStruct(shape, jnp.bfloat16...  18.4 us
    pallas_call x2, Pallas kernels, pick(): pl.pallas_call(pick_kernel, out_shape=[jax.ShapeDtypeStruct((2, half, wid...  7.36 us
    pallas_call x1, Pallas kernels, pack(): pl.pallas_call(pack_kernel, grid=(count // step,), out_shape=jax.ShapeDty...  5.62 us
    all_to_all x3, waiting for transfers between devices, exchanged(): return lax.all_to_all(spectra, 'freq', 0, 0, tiled=True)  4.77 us
  transfers between devices with their start and end apart: 21, of which 11 were waited for; matrix products, arithmetic and copies ran while one was open for 6% of the time, Pallas kernels for 25%

profile of v3, /device:TPU:0, one launch (start us, length us, event | category | flops | bytes accessed | tf_op | source)
XLA Modules:
  0.0 153.8 jit_solution(1893658128717820117)
XLA Ops:
  0.7 3.6 %pick.2 = bf16[2,128,4096]{2,1,0:T(8,128)(2,1)} custom-call(s32[3]{0:T(128)} %pad_add_fusion.place.refs_0_, bf16[2,256,4096]{2,1,0:T(8,128)(2,1)} %refs_1_.2), custom_call_target="tpu_custom_call" | custom-call | flops 9999999827968 | bytes 20000000000 | tf_op jit(solution)/shard_map/pick/pallas_call | solution.py:75
  4.4 3.7 %pick.3 = (bf16[2,128,2048]{2,1,0:T(8,128)(2,1)}, bf16[2,128,2048]{2,1,0:T(8,128)(2,1)}) custom-call(s32[3]{0:T(128)} %pad_add_fusion.place.refs_0_, bf16[2,256,4096]{2,1,0:T(8,128)(2,1)} %refs_1_.2), custom_call_target="tpu_custom_call" | custom-call | flops 9999999827968 | bytes 20000000000 | tf_op jit(solution)/shard_map/pick/pallas_call | solution.py:75
  10.8 3.1 %convolution_convert_fusion.refs_4_.refs_6_ = bf16[640,2048]{1,0:T(8,128)(2,1)} fusion(bf16[512,2048]{1,0:T(8,128)(2,1)S(1)} %copy-done.10, f32[512]{0:T(512)S(1)} %bitcast.5, s32[512]{0:T(512)S(1)} %copy-done.9, s32[640]{0:T(1024)S(1)} %copy-done.11), kind=kOutput, calls=%fused_computation | convolution fusion | flops 1344143360 | bytes 4725248 | tf_op jit(solution)/shard_map/dot_general | solution.py:369
  13.9 9.0 %channelize.2 = (bf16[32,8,8,128]{3,2,1,0:T(8,128)(2,1)}, bf16[32,12,8,128]{3,2,1,0:T(8,128)(2,1)}) custom-call(s32[3]{0:T(128)} %pad_add_fusion.place.refs_0_, bf16[2,256,4096]{2,1,0:T(8,128)(2,1)} %refs_1_.2, bf16[2,128,4096]{2,1,0:T(8,128)(2,1)} %collective-permute-done.refs_2_, f32[4,1024]{1,0:T(4,128)} %constant.34.clone.refs_3_.refs_5_, ...), custom_call_target="tpu_custom_call" | custom-call | flops 9999999827968 | bytes 20000000000 | tf_op jit(solution)/shard_map/channelize/pallas_call | solution.py:203
  22.9 3.2 %collective-permute-start.3 = (bf16[32,8,8,128]{3,2,1,0:T(8,128)(2,1)}, bf16[32,8,8,128]{3,2,1,0:T(8,128)(2,1)}, u32[]{:S(2)}, u32[]{:S(2)}) collective-permute-start(bf16[32,8,8,128]{3,2,1,0:T(8,128)(2,1)} %get-tuple-element.27.refs_0_), channel_id=1, source_target_pairs={{0,64},{32,96},{64,0},{96,32},{1,65},{33,97},{65,1},{97,33},{2,66}... | collective-permute-start | bytes 1572872 | tf_op jit(solution)/shard_map/ppermute | solution.py:374
  28.1 12.4 %all-to-all-start = ((bf16[32,12,8,128]{3,2,1,0:T(8,128)(2,1)}), bf16[32,12,8,128]{3,2,1,0:T(8,128)(2,1)}, u32[]{:S(2)}, u32[]{:S(2)}) async-start(bf16[32,12,8,128]{3,2,1,0:T(8,128)(2,1)} %get-tuple-element.25), calls=%async_computation | async-start | bytes 1572864 | tf_op jit(solution)/shard_map/all_to_all | solution.py:377
  40.7 9.7 %channelize.3 = bf16[32,20,8,128]{3,2,1,0:T(8,128)(2,1)} custom-call(s32[3]{0:T(128)} %pad_add_fusion.place.refs_0_, bf16[2,256,4096]{2,1,0:T(8,128)(2,1)} %refs_1_.2, bf16[2,128,4096]{2,1,0:T(8,128)(2,1)} %collective-permute-done.refs_2_, bf16[2,128,2048]{2,1,0:T(8,128)(2,1)} %collective-permute-done.4.refs_3_, ...), custom_call_target="tpu_custom_call" | custom-call | flops 9999999827968 | bytes 20000000000 | tf_op jit(solution)/shard_map/channelize/pallas_call | solution.py:203
  50.7 4.3 %all-to-all-done.refs_1_ = bf16[32,12,8,128]{3,2,1,0:T(8,128)(2,1)} async-done(((bf16[32,12,8,128]{3,2,1,0:T(8,128)(2,1)}), bf16[32,12,8,128]{3,2,1,0:T(8,128)(2,1)}, u32[]{:S(2)}, u32[]{:S(2)}) %all-to-all-start) | async-done | bytes 786464 | tf_op jit(solution)/shard_map/all_to_all | solution.py:377
  55.0 2.4 %collective-permute-start.7 = (bf16[32,12,8,128]{3,2,1,0:T(8,128)(2,1)}, bf16[32,12,8,128]{3,2,1,0:T(8,128)(2,1)S(1)}, u32[]{:S(2)}, u32[]{:S(2)}) collective-permute-start(bf16[32,12,8,128]{3,2,1,0:T(8,128)(2,1)} %all-to-all-done.refs_1_), channel_id=1, source_target_pairs={{0,96},{32,0},{64,32},{96,64},{1,97},{33,1},{65,33},{97,65},{2,98}... | collective-permute-start | bytes 2359304 | tf_op jit(solution)/shard_map/ppermute | solution.py:374
  57.4 7.8 %all-to-all-start.1 = ((bf16[32,20,8,128]{3,2,1,0:T(8,128)(2,1)}), bf16[32,20,8,128]{3,2,1,0:T(8,128)(2,1)}, u32[]{:S(2)}, u32[]{:S(2)}) async-start(bf16[32,20,8,128]{3,2,1,0:T(8,128)(2,1)} %channelize.3), calls=%async_computation.1 | async-start | bytes 2621440 | tf_op jit(solution)/shard_map/all_to_all | solution.py:377
  65.2 9.4 %collective-permute-done.7.refs_5_ = bf16[32,12,8,128]{3,2,1,0:T(8,128)(2,1)S(1)} collective-permute-done((bf16[32,12,8,128]{3,2,1,0:T(8,128)(2,1)}, bf16[32,12,8,128]{3,2,1,0:T(8,128)(2,1)S(1)}, u32[]{:S(2)}, u32[]{:S(2)}) %collective-permute-start.7) | collective-permute-done | bytes 786464 | tf_op jit(solution)/shard_map/ppermute | solution.py:374
  75.4 3.6 %collective-permute-start.9 = (bf16[16,12,8,128]{3,2,1,0:T(8,128)(2,1)}, bf16[16,12,8,128]{3,2,1,0:T(8,128)(2,1)}, u32[]{:S(2)}, u32[]{:S(2)}) collective-permute-start(bf16[16,12,8,128]{3,2,1,0:T(8,128)(2,1)} %slice.33), channel_id=1, source_target_pairs={{0,96},{32,0},{64,32},{96,64},{1,97},{33,1},{65,33},{97,65},{2,98}... | collective-permute-start | bytes 1179656 | tf_op jit(solution)/shard_map/ppermute | solution.py:374
  79.8 5.6 %pack.1 = bf16[32,32,8,128]{3,2,1,0:T(8,128)(2,1)} custom-call(bf16[32,8,8,128]{3,2,1,0:T(8,128)(2,1)} %get-tuple-element.27.refs_0_, bf16[32,8,8,128]{3,2,1,0:T(8,128)(2,1)} %collective-permute-done.1.refs_1_, bf16[32,8,8,128]{3,2,1,0:T(8,128)(2,1)} %collective-permute-done.2.refs_2_, bf16[32,8,8,128]{3,2,1,0:T(8,128)(2,1)} %collective-permute-done.3.refs_3_), custom_call_target="tpu_custom_call" | custom-call | flops 9999999827968 | bytes 20000000000 | tf_op jit(solution)/shard_map/pack/pallas_call | solution.py:237
  87.0 4.2 %collective-permute-done.8.refs_7_ = bf16[16,12,8,128]{3,2,1,0:T(8,128)(2,1)} collective-permute-done((bf16[16,12,8,128]{3,2,1,0:T(8,128)(2,1)}, bf16[16,12,8,128]{3,2,1,0:T(8,128)(2,1)}, u32[]{:S(2)}, u32[]{:S(2)}) %collective-permute-start.8) | collective-permute-done | bytes 393248 | tf_op jit(solution)/shard_map/ppermute | solution.py:374
  92.6 2.0 %collective-permute-start.14 = (bf16[32,12,8,128]{3,2,1,0:T(8,128)(2,1)S(1)}, bf16[32,12,8,128]{3,2,1,0:T(8,128)(2,1)}, u32[]{:S(2)}, u32[]{:S(2)}) collective-permute-start(bf16[32,12,8,128]{3,2,1,0:T(8,128)(2,1)S(1)} %slice.29), channel_id=1, source_target_pairs={{0,32},{32,64},{64,96},{96,0},{1,33},{33,65},{65,97},{97,1},{2,34}... | collective-permute-start | bytes 2359304 | tf_op jit(solution)/shard_map/ppermute | solution.py:374
  94.6 7.9 %all-to-all-start.2 = ((bf16[32,32,8,128]{3,2,1,0:T(8,128)(2,1)}), bf16[32,32,8,128]{3,2,1,0:T(8,128)(2,1)S(1)}, u32[]{:S(2)}, u32[]{:S(2)}) async-start(bf16[32,32,8,128]{3,2,1,0:T(8,128)(2,1)} %pack.1), calls=%async_computation.2 | async-start | bytes 4194304 | tf_op jit(solution)/shard_map/all_to_all | solution.py:377
  103.6 1.5 %collective-permute-start.11 = (bf16[32,8,8,128]{3,2,1,0:T(8,128)(2,1)S(1)}, bf16[32,8,8,128]{3,2,1,0:T(8,128)(2,1)S(1)}, u32[]{:S(2)}, u32[]{:S(2)}) collective-permute-start(bf16[32,8,8,128]{3,2,1,0:T(8,128)(2,1)S(1)} %slice.26), channel_id=1, source_target_pairs={{0,96},{32,0},{64,32},{96,64},{1,97},{33,1},{65,33},{97,65},{2,98}... | collective-permute-start | bytes 1572872 | tf_op jit(solution)/shard_map/ppermute | solution.py:374
  105.9 7.2 %collective-permute-done.15.refs_6_ = bf16[32,12,8,128]{3,2,1,0:T(8,128)(2,1)} collective-permute-done((bf16[32,12,8,128]{3,2,1,0:T(8,128)(2,1)S(1)}, bf16[32,12,8,128]{3,2,1,0:T(8,128)(2,1)}, u32[]{:S(2)}, u32[]{:S(2)}) %collective-permute-start.15) | collective-permute-done | bytes 786464 | tf_op jit(solution)/shard_map/ppermute | solution.py:374
  115.9 1.5 collective-permute-start.16
  117.3 6.9 %collective-permute-done.11.refs_6_ = bf16[32,8,8,128]{3,2,1,0:T(8,128)(2,1)S(1)} collective-permute-done((bf16[32,8,8,128]{3,2,1,0:T(8,128)(2,1)S(1)}, bf16[32,8,8,128]{3,2,1,0:T(8,128)(2,1)S(1)}, u32[]{:S(2)}, u32[]{:S(2)}) %collective-permute-start.11) | collective-permute-done | bytes 524320 | tf_op jit(solution)/shard_map/ppermute | solution.py:374
  125.8 1.4 collective-permute-start.12
  127.2 5.2 %collective-permute-done.17.refs_10_ = bf16[16,12,8,128]{3,2,1,0:T(8,128)(2,1)S(1)} collective-permute-done((bf16[16,12,8,128]{3,2,1,0:T(8,128)(2,1)S(1)}, bf16[16,12,8,128]{3,2,1,0:T(8,128)(2,1)S(1)}, u32[]{:S(2)}, u32[]{:S(2)}) %collective-permute-start.17) | collective-permute-done | bytes 393248 | tf_op jit(solution)/shard_map/ppermute | solution.py:374
  133.3 10.7 %correlate.2.refs_10_ = bf16[20,2,256,1024]{3,2,1,0:T(8,128)(2,1)} custom-call(s32[3]{0:T(128)} %pad_add_fusion.place.refs_0_, bf16[32,12,8,128]{3,2,1,0:T(8,128)(2,1)} %all-to-all-done.refs_1_, bf16[32,20,8,128]{3,2,1,0:T(8,128)(2,1)} %all-to-all-done.1.refs_2_, bf16[32,12,8,128]{3,2,1,0:T(8,128)(2,1)} %copy-done.6, ...), custom_call_target="tpu_custom_call" | custom-call | flops 10000000000 | bytes 40000000 | tf_op jit(solution)/shard_map/correlate/pallas_call | solution.py:321
  146.2 7.7 %correlate.3 = bf16[20,2,256,1024]{3,2,1,0:T(8,128)(2,1)} custom-call(s32[3]{0:T(128)} %pad_add_fusion.place.refs_0_, bf16[32,32,8,128]{3,2,1,0:T(8,128)(2,1)} %copy-done, bf16[32,20,8,128]{3,2,1,0:T(8,128)(2,1)} %all-to-all-done.1.refs_2_, bf16[32,32,8,128]{3,2,1,0:T(8,128)(2,1)} %copy-done, ...), custom_call_target="tpu_custom_call", output_to_operand_aliasing={{}: (10, {})} | custom-call | flops 10000000000 | bytes 40000000 | tf_op jit(solution)/shard_map/correlate/pallas_call | solution.py:321
  (60 shorter events, 19.5 us)
Async XLA Ops:
  4.3 9.6 %collective-permute-start = (bf16[2,128,4096]{2,1,0:T(8,128)(2,1)}, bf16[2,128,4096]{2,1,0:T(8,128)(2,1)}, u32[]{:S(2)}, u32[]{:S(2)}) collective-permute-start(bf16[2,128,4096]{2,1,0:T(8,128)(2,1)} %pick.2), channel_id=1, source_target_pairs={{0,1},{1,0},{2,3},{3,2},{4,5},{5,4},{6,7},{7,6},{8,9},{9,8},{10,11... | collective-permute-start | bytes 6291464 | tf_op jit(solution)/shard_map/ppermute | solution.py:353
  8.2 32.3 %collective-permute-start.4 = (bf16[2,128,2048]{2,1,0:T(8,128)(2,1)}, bf16[2,128,2048]{2,1,0:T(8,128)(2,1)}, u32[]{:S(2)}, u32[]{:S(2)}) collective-permute-start(bf16[2,128,2048]{2,1,0:T(8,128)(2,1)} %get-tuple-element.21), channel_id=1, source_target_pairs={{2,0},{4,2},{6,4},{8,6},{10,8},{12,10},{14,12},{16,14},{18,16},{20... | collective-permute-start | bytes 3145736 | tf_op jit(solution)/shard_map/ppermute | solution.py:359
  9.5 31.3 %collective-permute-start.5 = (bf16[2,128,2048]{2,1,0:T(8,128)(2,1)}, bf16[2,128,2048]{2,1,0:T(8,128)(2,1)}, u32[]{:S(2)}, u32[]{:S(2)}) collective-permute-start(bf16[2,128,2048]{2,1,0:T(8,128)(2,1)} %get-tuple-element.22), channel_id=1, source_target_pairs={{2,1},{4,3},{6,5},{8,7},{10,9},{12,11},{14,13},{16,15},{18,17},{20... | collective-permute-start | bytes 3145736 | tf_op jit(solution)/shard_map/ppermute | solution.py:359
  22.9 27.6 %collective-permute-start.3 = (bf16[32,8,8,128]{3,2,1,0:T(8,128)(2,1)}, bf16[32,8,8,128]{3,2,1,0:T(8,128)(2,1)}, u32[]{:S(2)}, u32[]{:S(2)}) collective-permute-start(bf16[32,8,8,128]{3,2,1,0:T(8,128)(2,1)} %get-tuple-element.27.refs_0_), channel_id=1, source_target_pairs={{0,64},{32,96},{64,0},{96,32},{1,65},{33,97},{65,1},{97,33},{2,66}... | collective-permute-start | bytes 1572872 | tf_op jit(solution)/shard_map/ppermute | solution.py:374
  26.1 24.4 %collective-permute-start.2 = (bf16[32,8,8,128]{3,2,1,0:T(8,128)(2,1)}, bf16[32,8,8,128]{3,2,1,0:T(8,128)(2,1)}, u32[]{:S(2)}, u32[]{:S(2)}) collective-permute-start(bf16[32,8,8,128]{3,2,1,0:T(8,128)(2,1)} %get-tuple-element.27.refs_0_), channel_id=1, source_target_pairs={{0,96},{32,0},{64,32},{96,64},{1,97},{33,1},{65,33},{97,65},{2,98}... | collective-permute-start | bytes 1572872 | tf_op jit(solution)/shard_map/ppermute | solution.py:374
  27.2 23.5 %collective-permute-start.1 = (bf16[32,8,8,128]{3,2,1,0:T(8,128)(2,1)}, bf16[32,8,8,128]{3,2,1,0:T(8,128)(2,1)}, u32[]{:S(2)}, u32[]{:S(2)}) collective-permute-start(bf16[32,8,8,128]{3,2,1,0:T(8,128)(2,1)} %get-tuple-element.27.refs_0_), channel_id=1, source_target_pairs={{0,32},{32,64},{64,96},{96,0},{1,33},{33,65},{65,97},{97,1},{2,34}... | collective-permute-start | bytes 1572872 | tf_op jit(solution)/shard_map/ppermute | solution.py:374
  28.1 26.9 %all-to-all-start = ((bf16[32,12,8,128]{3,2,1,0:T(8,128)(2,1)}), bf16[32,12,8,128]{3,2,1,0:T(8,128)(2,1)}, u32[]{:S(2)}, u32[]{:S(2)}) async-start(bf16[32,12,8,128]{3,2,1,0:T(8,128)(2,1)} %get-tuple-element.25), calls=%async_computation | async-start | bytes 1572864 | tf_op jit(solution)/shard_map/all_to_all | solution.py:377
  55.0 19.6 %collective-permute-start.7 = (bf16[32,12,8,128]{3,2,1,0:T(8,128)(2,1)}, bf16[32,12,8,128]{3,2,1,0:T(8,128)(2,1)S(1)}, u32[]{:S(2)}, u32[]{:S(2)}) collective-permute-start(bf16[32,12,8,128]{3,2,1,0:T(8,128)(2,1)} %all-to-all-done.refs_1_), channel_id=1, source_target_pairs={{0,96},{32,0},{64,32},{96,64},{1,97},{33,1},{65,33},{97,65},{2,98}... | collective-permute-start | bytes 2359304 | tf_op jit(solution)/shard_map/ppermute | solution.py:374
  57.4 21.6 %collective-permute-start.6 = (bf16[32,12,8,128]{3,2,1,0:T(8,128)(2,1)}, bf16[32,12,8,128]{3,2,1,0:T(8,128)(2,1)S(1)}, u32[]{:S(2)}, u32[]{:S(2)}) collective-permute-start(bf16[32,12,8,128]{3,2,1,0:T(8,128)(2,1)} %all-to-all-done.refs_1_), channel_id=1, source_target_pairs={{0,32},{32,64},{64,96},{96,0},{1,33},{33,65},{65,97},{97,1},{2,34}... | collective-permute-start | bytes 2359304 | tf_op jit(solution)/shard_map/ppermute | solution.py:374
  57.4 28.6 %all-to-all-start.1 = ((bf16[32,20,8,128]{3,2,1,0:T(8,128)(2,1)}), bf16[32,20,8,128]{3,2,1,0:T(8,128)(2,1)}, u32[]{:S(2)}, u32[]{:S(2)}) async-start(bf16[32,20,8,128]{3,2,1,0:T(8,128)(2,1)} %channelize.3), calls=%async_computation.1 | async-start | bytes 2621440 | tf_op jit(solution)/shard_map/all_to_all | solution.py:377
  74.6 10.9 %copy-start.5 = (bf16[32,12,8,128]{3,2,1,0:T(8,128)(2,1)}, bf16[32,12,8,128]{3,2,1,0:T(8,128)(2,1)S(1)}, u32[]{:S(2)}) copy-start(bf16[32,12,8,128]{3,2,1,0:T(8,128)(2,1)S(1)} %collective-permute-done.7.refs_5_) | copy-start | bytes 2359300
  75.4 11.6 %collective-permute-start.9 = (bf16[16,12,8,128]{3,2,1,0:T(8,128)(2,1)}, bf16[16,12,8,128]{3,2,1,0:T(8,128)(2,1)}, u32[]{:S(2)}, u32[]{:S(2)}) collective-permute-start(bf16[16,12,8,128]{3,2,1,0:T(8,128)(2,1)} %slice.33), channel_id=1, source_target_pairs={{0,96},{32,0},{64,32},{96,64},{1,97},{33,1},{65,33},{97,65},{2,98}... | collective-permute-start | bytes 1179656 | tf_op jit(solution)/shard_map/ppermute | solution.py:374
  79.8 11.5 %collective-permute-start.8 = (bf16[16,12,8,128]{3,2,1,0:T(8,128)(2,1)}, bf16[16,12,8,128]{3,2,1,0:T(8,128)(2,1)}, u32[]{:S(2)}, u32[]{:S(2)}) collective-permute-start(bf16[16,12,8,128]{3,2,1,0:T(8,128)(2,1)} %slice.32), channel_id=1, source_target_pairs={{0,32},{32,64},{64,96},{96,0},{1,33},{33,65},{65,97},{97,1},{2,34}... | collective-permute-start | bytes 1179656 | tf_op jit(solution)/shard_map/ppermute | solution.py:374
  92.5 20.7 %collective-permute-start.15 = (bf16[32,12,8,128]{3,2,1,0:T(8,128)(2,1)S(1)}, bf16[32,12,8,128]{3,2,1,0:T(8,128)(2,1)}, u32[]{:S(2)}, u32[]{:S(2)}) collective-permute-start(bf16[32,12,8,128]{3,2,1,0:T(8,128)(2,1)S(1)} %slice.29), channel_id=1, source_target_pairs={{0,96},{32,0},{64,32},{96,64},{1,97},{33,1},{65,33},{97,65},{2,98}... | collective-permute-start | bytes 2359304 | tf_op jit(solution)/shard_map/ppermute | solution.py:374
  92.6 22.3 %collective-permute-start.14 = (bf16[32,12,8,128]{3,2,1,0:T(8,128)(2,1)S(1)}, bf16[32,12,8,128]{3,2,1,0:T(8,128)(2,1)}, u32[]{:S(2)}, u32[]{:S(2)}) collective-permute-start(bf16[32,12,8,128]{3,2,1,0:T(8,128)(2,1)S(1)} %slice.29), channel_id=1, source_target_pairs={{0,32},{32,64},{64,96},{96,0},{1,33},{33,65},{65,97},{97,1},{2,34}... | collective-permute-start | bytes 2359304 | tf_op jit(solution)/shard_map/ppermute | solution.py:374
  94.6 49.5 %all-to-all-start.2 = ((bf16[32,32,8,128]{3,2,1,0:T(8,128)(2,1)}), bf16[32,32,8,128]{3,2,1,0:T(8,128)(2,1)S(1)}, u32[]{:S(2)}, u32[]{:S(2)}) async-start(bf16[32,32,8,128]{3,2,1,0:T(8,128)(2,1)} %pack.1), calls=%async_computation.2 | async-start | bytes 4194304 | tf_op jit(solution)/shard_map/all_to_all | solution.py:377
  103.6 20.7 %collective-permute-start.11 = (bf16[32,8,8,128]{3,2,1,0:T(8,128)(2,1)S(1)}, bf16[32,8,8,128]{3,2,1,0:T(8,128)(2,1)S(1)}, u32[]{:S(2)}, u32[]{:S(2)}) collective-permute-start(bf16[32,8,8,128]{3,2,1,0:T(8,128)(2,1)S(1)} %slice.26), channel_id=1, source_target_pairs={{0,96},{32,0},{64,32},{96,64},{1,97},{33,1},{65,33},{97,65},{2,98}... | collective-permute-start | bytes 1572872 | tf_op jit(solution)/shard_map/ppermute | solution.py:374
  105.1 19.8 %collective-permute-start.10 = (bf16[32,8,8,128]{3,2,1,0:T(8,128)(2,1)S(1)}, bf16[32,8,8,128]{3,2,1,0:T(8,128)(2,1)S(1)}, u32[]{:S(2)}, u32[]{:S(2)}) collective-permute-start(bf16[32,8,8,128]{3,2,1,0:T(8,128)(2,1)S(1)} %slice.26), channel_id=1, source_target_pairs={{0,32},{32,64},{64,96},{96,0},{1,33},{33,65},{65,97},{97,1},{2,34}... | collective-permute-start | bytes 1572872 | tf_op jit(solution)/shard_map/ppermute | solution.py:374
  114.1 18.3 %collective-permute-start.17 = (bf16[16,12,8,128]{3,2,1,0:T(8,128)(2,1)S(1)}, bf16[16,12,8,128]{3,2,1,0:T(8,128)(2,1)S(1)}, u32[]{:S(2)}, u32[]{:S(2)}) collective-permute-start(bf16[16,12,8,128]{3,2,1,0:T(8,128)(2,1)S(1)} %slice.37), channel_id=1, source_target_pairs={{0,96},{32,0},{64,32},{96,64},{1,97},{33,1},{65,33},{97,65},{2,98}... | collective-permute-start | bytes 1179656 | tf_op jit(solution)/shard_map/ppermute | solution.py:374
  115.9 17.4 %collective-permute-start.16 = (bf16[16,12,8,128]{3,2,1,0:T(8,128)(2,1)S(1)}, bf16[16,12,8,128]{3,2,1,0:T(8,128)(2,1)}, u32[]{:S(2)}, u32[]{:S(2)}) collective-permute-start(bf16[16,12,8,128]{3,2,1,0:T(8,128)(2,1)S(1)} %slice.36), channel_id=1, source_target_pairs={{0,32},{32,64},{64,96},{96,0},{1,33},{33,65},{65,97},{97,1},{2,34}... | collective-permute-start | bytes 1179656 | tf_op jit(solution)/shard_map/ppermute | solution.py:374
  124.3 19.8 %copy-start.1 = (bf16[32,8,8,128]{3,2,1,0:T(8,128)(2,1)}, bf16[32,8,8,128]{3,2,1,0:T(8,128)(2,1)S(1)}, u32[]{:S(2)}) copy-start(bf16[32,8,8,128]{3,2,1,0:T(8,128)(2,1)S(1)} %collective-permute-done.11.refs_6_) | copy-start | bytes 1572868
  124.3 19.8 %collective-permute-start.13 = (bf16[16,8,8,128]{3,2,1,0:T(8,128)(2,1)S(1)}, bf16[16,8,8,128]{3,2,1,0:T(8,128)(2,1)S(1)}, u32[]{:S(2)}, u32[]{:S(2)}) collective-permute-start(bf16[16,8,8,128]{3,2,1,0:T(8,128)(2,1)S(1)} %slice.35), channel_id=1, source_target_pairs={{0,96},{32,0},{64,32},{96,64},{1,97},{33,1},{65,33},{97,65},{2,98}... | collective-permute-start | bytes 786440 | tf_op jit(solution)/shard_map/ppermute | solution.py:374
  125.0 19.0 %copy-start.2 = (bf16[32,8,8,128]{3,2,1,0:T(8,128)(2,1)}, bf16[32,8,8,128]{3,2,1,0:T(8,128)(2,1)S(1)}, u32[]{:S(2)}) copy-start(bf16[32,8,8,128]{3,2,1,0:T(8,128)(2,1)S(1)} %collective-permute-done.10.refs_4_) | copy-start | bytes 1572868
  125.8 18.3 %collective-permute-start.12 = (bf16[16,8,8,128]{3,2,1,0:T(8,128)(2,1)}, bf16[16,8,8,128]{3,2,1,0:T(8,128)(2,1)S(1)}, u32[]{:S(2)}, u32[]{:S(2)}) collective-permute-start(bf16[16,8,8,128]{3,2,1,0:T(8,128)(2,1)} %slice.34), channel_id=1, source_target_pairs={{0,32},{32,64},{64,96},{96,0},{1,33},{33,65},{65,97},{97,1},{2,34}... | collective-permute-start | bytes 786440 | tf_op jit(solution)/shard_map/ppermute | solution.py:374
  (9 other events, 35.6 us)

commit v4 on v3

--- a/solution.py
+++ b/solution.py
@@ -254,6 +254,70 @@
     return jnp.concatenate([wide[:, core] for core in range(CORES)], 2)
 
 
+def left_operand(mine, scale):
+    group = mine.shape[2]
+    row = lax.broadcasted_iota(jnp.int32, (1, 2 * BLOCKS, group), 1)
+    sign = jnp.where(row < BLOCKS, -1.0, 1.0)
+    mine = mine * scale
+    turned = pltpu.roll(mine, BLOCKS, 1) * sign
+    both = jnp.concatenate([mine, turned], 2)
+    return jnp.transpose(both.reshape(-1, 2 * group).astype(jnp.bfloat16))
+
+
+def correlate_far_kernel(counts, place, *refs):
+    out = refs[-1]
+    group = out.shape[2]
+    own, far = refs[: counts[0]], refs[counts[0] : sum(counts)]
+    scale = CORES / (2 * BLOCKS * refs[0].shape[0])
+    for j in range(out.shape[0]):
+        mine = jnp.concatenate([gathered(piece, j) for piece in own], 0)
+        wide = jnp.concatenate([gathered(piece, j) for piece in far], 0)
+        product = lax.dot_general(
+            left_operand(mine, scale),
+            wide.reshape(-1, group).astype(jnp.bfloat16),
+            (((1,), (0,)), ((), ())),
+            preferred_element_type=jnp.float32,
+        ).astype(jnp.bfloat16)
+        for z in range(2):
+            out[j, z] = product[z * group : (z + 1) * group]
+
+
+def correlate_far(place, sources, first, slots, shape, result):
+    in_specs = []
+    operands = []
+    group = shape[2]
+    for source in sources:
+        for part, starts, _ in source:
+            skip = (first - starts) // STEP
+            block = (part.shape[0], STEP) + part.shape[2:]
+            in_specs.append(pl.BlockSpec(block, lambda j, place, skip=skip: (0, skip + j, 0, 0)))
+            operands.append(part)
+    counts = tuple(len(source) for source in sources)
+
+    def kernel(*refs):
+        correlate_far_kernel(counts, *refs)
+
+    def column(j, place):
+        return first // STEP + j, 0, 0, lax.rem(place[1] + 2, shape[3] // group)
+
+    return pl.pallas_call(
+        kernel,
+        out_shape=jax.ShapeDtypeStruct(shape, jnp.bfloat16),
+        grid_spec=pltpu.PrefetchScalarGridSpec(
+            num_scalar_prefetch=1,
+            grid=(slots // STEP,),
+            in_specs=in_specs + [pl.BlockSpec(memory_space=pl.ANY)],
+            out_specs=pl.BlockSpec((STEP, 2, group, group), column),
+        ),
+        input_output_aliases={len(operands) + 1: 0},
+        compiler_params=pltpu.CompilerParams(
+            dimension_semantics=("arbitrary",), vmem_limit_bytes=VMEM
+        ),
+        cost_estimate=pl.CostEstimate(flops=10**10, bytes_accessed=4 * 10**7, transcendentals=0),
+        name="correlate_far",
+    )(place, *operands, result)
+
+
 def correlate_kernel(parts_of, place, *refs):
     out = refs[-1]
     me = place[1]
@@ -265,17 +329,11 @@
         sources.append(refs[at : at + count])
         at += count
     scale = CORES / (2 * BLOCKS * refs[0].shape[0])
-    row = lax.broadcasted_iota(jnp.int32, (1, 2 * BLOCKS, group), 1)
-    sign = jnp.where(row < BLOCKS, -1.0, 1.0)
     for j in range(out.shape[0]):
         for ahead, source in zip(AHEAD, sources):
             wide = jnp.concatenate([gathered(piece, j) for piece in source], 0)
             if ahead == 0:
-                mine = wide * scale
-                turned = pltpu.roll(mine, BLOCKS, 1) * sign
-                lhs = jnp.concatenate([mine, turned], 2)
-                lhs = lhs.reshape(-1, 2 * group).astype(jnp.bfloat16)
-                lhs = jnp.transpose(lhs)
+                lhs = left_operand(wide, scale)
             product = lax.dot_general(
                 lhs,
                 wide.reshape(-1, group).astype(jnp.bfloat16),
@@ -333,7 +391,7 @@
         compiler_params=pltpu.CompilerParams(
             dimension_semantics=("arbitrary",), vmem_limit_bytes=VMEM
         ),
-        cost_estimate=pl.CostEstimate(flops=10**10, bytes_accessed=4 * 10**7, transcendentals=0),
+        cost_estimate=pl.CostEstimate(flops=10**9, bytes_accessed=4 * 10**6, transcendentals=0),
         name="correlate",
     )(place, *operands)
 
@@ -399,9 +457,6 @@
     left_b0, right_b0 = ring(own_b0, 1), ring(own_b0, -1)
     all_a0 = exchanged(after(all_a0, ready_b))
     far_b1 = far(left_b1, right_b1)
-    far_b0 = far(left_b0, right_b0)
-
-    shape = (CAP, 2, feeds, feeds * groups)
 
     def whole(own, parts, first):
         return [[own]] + [
@@ -409,10 +464,14 @@
             for group in parts
         ]
 
+    shape = (CAP, 2, feeds, feeds * groups)
     early = whole((own_a1, small, None), (left_a1, right_a1, far_a1), small)
     late = whole((own_b, 0, None), (left_b1, right_b1, far_b1), small)
     sources = [one + two for one, two in zip(early, late)]
-    result = correlate(place, sources, small, large, shape, None)
+    result = correlate(place, sources[:3], small, large, shape, None)
+    left_b0, right_b0, result = after_all((left_b0, right_b0, result), ())
+    far_b0 = far(left_b0, right_b0)
+    result = correlate_far(place, [sources[0], sources[3]], small, large, shape, result)
     late = whole((own_b, 0, None), (left_b0, right_b0, far_b0), 0)
     sources = [[(all_a0, -small * k, None)] + two for k, two in enumerate(late)]
     return correlate(place, sources, 0, small, shape, result)

time: 155 us -> 151 us (0.974)
  waiting for transfers between devices: 39.6 us -> 29.7 us
  Pallas kernels: 50 us -> 54.2 us
    ppermute x15, waiting for transfers between devices: 34.5 us -> 24.7 us  [ring(): lax.ppermute(value, 'feed', [(k, (k + steps) % groups) for k in range(gro...]
    pallas_call x0 -> x1, Pallas kernels: none -> 5.78 us  [correlate_far(): pl.pallas_call(kernel, out_shape=jax.ShapeDtypeStruct(shape, jnp.bfloat16...]
  transfers between devices with their start and end apart: 21 -> 21, of which waited for: 11 -> 10; matrix products, arithmetic and copies ran while one was open for 6% -> 7% of each run, Pallas kernels for 25% -> 29%
where the time goes in v4:
time: 151 us; the launch traced here: 149 us
  Pallas kernels  54.2 us (36%)
  starting transfers between devices  50 us (33%)
  waiting for transfers between devices  29.7 us (20%)
  local copies, waits for them, and re-layouts  11.2 us (7%)
  matrix products  3.08 us (2%)
    all_to_all x3, starting transfers between devices, exchanged(): return lax.all_to_all(spectra, 'freq', 0, 0, tiled=True)  28.1 us
    ppermute x15, waiting for transfers between devices, ring(): lax.ppermute(value, 'feed', [(k, (k + steps) % groups) for k in range(gro...  24.7 us
    ppermute x15, starting transfers between devices, ring(): lax.ppermute(value, 'feed', [(k, (k + steps) % groups) for k in range(gro...  19.3 us
    pallas_call x2, Pallas kernels, channelize(): pl.pallas_call(kernel, out_shape=[jax.ShapeDtypeStruct((owners, slots, 2...  18.7 us
    pallas_call x2, Pallas kernels, correlate(): pl.pallas_call(kernel, out_shape=jax.ShapeDtypeStruct(shape, jnp.bfloat16...  16.9 us
    pallas_call x2, Pallas kernels, pick(): pl.pallas_call(pick_kernel, out_shape=[jax.ShapeDtypeStruct((2, half, wid...  7.26 us
    pallas_call x1, Pallas kernels, correlate_far(): pl.pallas_call(kernel, out_shape=jax.ShapeDtypeStruct(shape, jnp.bfloat16...  5.78 us
    pallas_call x1, Pallas kernels, pack(): pl.pallas_call(pack_kernel, grid=(count // step,), out_shape=jax.ShapeDty...  5.62 us
  transfers between devices with their start and end apart: 21, of which 10 were waited for; matrix products, arithmetic and copies ran while one was open for 7% of the time, Pallas kernels for 29%

profile of v4, /device:TPU:0, one launch (start us, length us, event | category | flops | bytes accessed | tf_op | source)
XLA Modules:
  0.0 149.2 jit_solution(12678978158145158600)
XLA Ops:
  0.7 3.6 %pick.2 = bf16[2,128,4096]{2,1,0:T(8,128)(2,1)} custom-call(s32[3]{0:T(128)} %pad_add_fusion.place.refs_0_, bf16[2,256,4096]{2,1,0:T(8,128)(2,1)} %refs_1_.2), custom_call_target="tpu_custom_call" | custom-call | flops 9999999827968 | bytes 20000000000 | tf_op jit(solution)/shard_map/pick/pallas_call | solution.py:75
  4.4 3.7 %pick.3 = (bf16[2,128,2048]{2,1,0:T(8,128)(2,1)}, bf16[2,128,2048]{2,1,0:T(8,128)(2,1)}) custom-call(s32[3]{0:T(128)} %pad_add_fusion.place.refs_0_, bf16[2,256,4096]{2,1,0:T(8,128)(2,1)} %refs_1_.2), custom_call_target="tpu_custom_call" | custom-call | flops 9999999827968 | bytes 20000000000 | tf_op jit(solution)/shard_map/pick/pallas_call | solution.py:75
  10.7 3.1 %convolution_convert_fusion.refs_4_.refs_6_ = bf16[640,2048]{1,0:T(8,128)(2,1)} fusion(bf16[512,2048]{1,0:T(8,128)(2,1)S(1)} %copy-done.10, f32[512]{0:T(512)S(1)} %bitcast.5, s32[512]{0:T(512)S(1)} %copy-done.9, s32[640]{0:T(1024)S(1)} %copy-done.11), kind=kOutput, calls=%fused_computation | convolution fusion | flops 1344143360 | bytes 4725248 | tf_op jit(solution)/shard_map/dot_general | solution.py:427
  13.8 9.0 %channelize.2 = (bf16[32,8,8,128]{3,2,1,0:T(8,128)(2,1)}, bf16[32,12,8,128]{3,2,1,0:T(8,128)(2,1)}) custom-call(s32[3]{0:T(128)} %pad_add_fusion.place.refs_0_, bf16[2,256,4096]{2,1,0:T(8,128)(2,1)} %refs_1_.2, bf16[2,128,4096]{2,1,0:T(8,128)(2,1)} %collective-permute-done.refs_2_, f32[4,1024]{1,0:T(4,128)} %constant.34.clone.refs_3_.refs_5_, ...), custom_call_target="tpu_custom_call" | custom-call | flops 9999999827968 | bytes 20000000000 | tf_op jit(solution)/shard_map/channelize/pallas_call | solution.py:203
  22.8 3.2 %collective-permute-start.3 = (bf16[32,8,8,128]{3,2,1,0:T(8,128)(2,1)}, bf16[32,8,8,128]{3,2,1,0:T(8,128)(2,1)}, u32[]{:S(2)}, u32[]{:S(2)}) collective-permute-start(bf16[32,8,8,128]{3,2,1,0:T(8,128)(2,1)} %get-tuple-element.30.refs_0_), channel_id=1, source_target_pairs={{0,64},{32,96},{64,0},{96,32},{1,65},{33,97},{65,1},{97,33},{2,66}... | collective-permute-start | bytes 1572872 | tf_op jit(solution)/shard_map/ppermute | solution.py:432
  28.0 12.4 %all-to-all-start = ((bf16[32,12,8,128]{3,2,1,0:T(8,128)(2,1)}), bf16[32,12,8,128]{3,2,1,0:T(8,128)(2,1)}, u32[]{:S(2)}, u32[]{:S(2)}) async-start(bf16[32,12,8,128]{3,2,1,0:T(8,128)(2,1)} %get-tuple-element.28), calls=%async_computation | async-start | bytes 1572864 | tf_op jit(solution)/shard_map/all_to_all | solution.py:435
  40.6 9.7 %channelize.3 = bf16[32,20,8,128]{3,2,1,0:T(8,128)(2,1)} custom-call(s32[3]{0:T(128)} %pad_add_fusion.place.refs_0_, bf16[2,256,4096]{2,1,0:T(8,128)(2,1)} %refs_1_.2, bf16[2,128,4096]{2,1,0:T(8,128)(2,1)} %collective-permute-done.refs_2_, bf16[2,128,2048]{2,1,0:T(8,128)(2,1)} %collective-permute-done.4.refs_3_, ...), custom_call_target="tpu_custom_call" | custom-call | flops 9999999827968 | bytes 20000000000 | tf_op jit(solution)/shard_map/channelize/pallas_call | solution.py:203
  50.6 4.3 %all-to-all-done.refs_1_ = bf16[32,12,8,128]{3,2,1,0:T(8,128)(2,1)} async-done(((bf16[32,12,8,128]{3,2,1,0:T(8,128)(2,1)}), bf16[32,12,8,128]{3,2,1,0:T(8,128)(2,1)}, u32[]{:S(2)}, u32[]{:S(2)}) %all-to-all-start) | async-done | bytes 786464 | tf_op jit(solution)/shard_map/all_to_all | solution.py:435
  54.9 2.4 %collective-permute-start.7 = (bf16[32,12,8,128]{3,2,1,0:T(8,128)(2,1)}, bf16[32,12,8,128]{3,2,1,0:T(8,128)(2,1)S(1)}, u32[]{:S(2)}, u32[]{:S(2)}) collective-permute-start(bf16[32,12,8,128]{3,2,1,0:T(8,128)(2,1)} %all-to-all-done.refs_1_), channel_id=1, source_target_pairs={{0,96},{32,0},{64,32},{96,64},{1,97},{33,1},{65,33},{97,65},{2,98}... | collective-permute-start | bytes 2359304 | tf_op jit(solution)/shard_map/ppermute | solution.py:432
  57.3 7.8 %all-to-all-start.1 = ((bf16[32,20,8,128]{3,2,1,0:T(8,128)(2,1)}), bf16[32,20,8,128]{3,2,1,0:T(8,128)(2,1)}, u32[]{:S(2)}, u32[]{:S(2)}) async-start(bf16[32,20,8,128]{3,2,1,0:T(8,128)(2,1)} %channelize.3), calls=%async_computation.1 | async-start | bytes 2621440 | tf_op jit(solution)/shard_map/all_to_all | solution.py:435
  65.1 9.4 %collective-permute-done.7.refs_5_ = bf16[32,12,8,128]{3,2,1,0:T(8,128)(2,1)S(1)} collective-permute-done((bf16[32,12,8,128]{3,2,1,0:T(8,128)(2,1)}, bf16[32,12,8,128]{3,2,1,0:T(8,128)(2,1)S(1)}, u32[]{:S(2)}, u32[]{:S(2)}) %collective-permute-start.7) | collective-permute-done | bytes 786464 | tf_op jit(solution)/shard_map/ppermute | solution.py:432
  75.4 3.6 %collective-permute-start.9 = (bf16[16,12,8,128]{3,2,1,0:T(8,128)(2,1)}, bf16[16,12,8,128]{3,2,1,0:T(8,128)(2,1)}, u32[]{:S(2)}, u32[]{:S(2)}) collective-permute-start(bf16[16,12,8,128]{3,2,1,0:T(8,128)(2,1)} %slice.33), channel_id=1, source_target_pairs={{0,96},{32,0},{64,32},{96,64},{1,97},{33,1},{65,33},{97,65},{2,98}... | collective-permute-start | bytes 1179656 | tf_op jit(solution)/shard_map/ppermute | solution.py:432
  79.8 5.6 %pack.1 = bf16[32,32,8,128]{3,2,1,0:T(8,128)(2,1)} custom-call(bf16[32,8,8,128]{3,2,1,0:T(8,128)(2,1)} %get-tuple-element.30.refs_0_, bf16[32,8,8,128]{3,2,1,0:T(8,128)(2,1)} %collective-permute-done.1.refs_1_, bf16[32,8,8,128]{3,2,1,0:T(8,128)(2,1)} %collective-permute-done.2.refs_2_, bf16[32,8,8,128]{3,2,1,0:T(8,128)(2,1)} %collective-permute-done.3.refs_3_), custom_call_target="tpu_custom_call" | custom-call | flops 9999999827968 | bytes 20000000000 | tf_op jit(solution)/shard_map/pack/pallas_call | solution.py:237
  87.0 4.2 %collective-permute-done.8.refs_3_ = bf16[16,12,8,128]{3,2,1,0:T(8,128)(2,1)} collective-permute-done((bf16[16,12,8,128]{3,2,1,0:T(8,128)(2,1)}, bf16[16,12,8,128]{3,2,1,0:T(8,128)(2,1)}, u32[]{:S(2)}, u32[]{:S(2)}) %collective-permute-start.8) | collective-permute-done | bytes 393248 | tf_op jit(solution)/shard_map/ppermute | solution.py:432
  91.2 2.1 %slice.27 = bf16[32,12,8,128]{3,2,1,0:T(8,128)(2,1)} slice(bf16[32,20,8,128]{3,2,1,0:T(8,128)(2,1)} %all-to-all-done.1.refs_2_), slice={[0:32], [8:20], [0:8], [0:128]} | slice | bytes 1572864 | tf_op jit(solution)/shard_map/slice | solution.py:454
  93.3 2.0 %collective-permute-start.12 = (bf16[32,12,8,128]{3,2,1,0:T(8,128)(2,1)}, bf16[32,12,8,128]{3,2,1,0:T(8,128)(2,1)}, u32[]{:S(2)}, u32[]{:S(2)}) collective-permute-start(bf16[32,12,8,128]{3,2,1,0:T(8,128)(2,1)} %slice.27), channel_id=1, source_target_pairs={{0,32},{32,64},{64,96},{96,0},{1,33},{33,65},{65,97},{97,1},{2,34}... | collective-permute-start | bytes 2359304 | tf_op jit(solution)/shard_map/ppermute | solution.py:432
  95.3 7.9 %all-to-all-start.2 = ((bf16[32,32,8,128]{3,2,1,0:T(8,128)(2,1)}), bf16[32,32,8,128]{3,2,1,0:T(8,128)(2,1)S(1)}, u32[]{:S(2)}, u32[]{:S(2)}) async-start(bf16[32,32,8,128]{3,2,1,0:T(8,128)(2,1)} %pack.1), calls=%async_computation.2 | async-start | bytes 4194304 | tf_op jit(solution)/shard_map/all_to_all | solution.py:435
  103.3 1.9 %slice.26 = bf16[32,8,8,128]{3,2,1,0:T(8,128)(2,1)} slice(bf16[32,20,8,128]{3,2,1,0:T(8,128)(2,1)} %all-to-all-done.1.refs_2_), slice={[0:32], [0:8], [0:8], [0:128]} | slice | bytes 1048576 | tf_op jit(solution)/shard_map/slice | solution.py:455
  107.2 6.4 %collective-permute-done.13.refs_6_ = bf16[32,12,8,128]{3,2,1,0:T(8,128)(2,1)S(1)} collective-permute-done((bf16[32,12,8,128]{3,2,1,0:T(8,128)(2,1)}, bf16[32,12,8,128]{3,2,1,0:T(8,128)(2,1)S(1)}, u32[]{:S(2)}, u32[]{:S(2)}) %collective-permute-start.13) | collective-permute-done | bytes 786464 | tf_op jit(solution)/shard_map/ppermute | solution.py:432
  118.2 9.2 %correlate.2.refs_7_ = bf16[20,2,256,1024]{3,2,1,0:T(8,128)(2,1)} custom-call(s32[3]{0:T(128)} %pad_add_fusion.place.refs_0_, bf16[32,12,8,128]{3,2,1,0:T(8,128)(2,1)} %all-to-all-done.refs_1_, bf16[32,20,8,128]{3,2,1,0:T(8,128)(2,1)} %all-to-all-done.1.refs_2_, bf16[32,12,8,128]{3,2,1,0:T(8,128)(2,1)} %copy-done.2, ...), custom_call_target="tpu_custom_call" | custom-call | flops 1000000000 | bytes 4000000 | tf_op jit(solution)/shard_map/correlate/pallas_call | solution.py:379
  128.3 1.8 %collective-permute-start.15 = (bf16[16,8,8,128]{3,2,1,0:T(8,128)(2,1)}, bf16[16,8,8,128]{3,2,1,0:T(8,128)(2,1)S(1)}, u32[]{:S(2)}, u32[]{:S(2)}) collective-permute-start(bf16[16,8,8,128]{3,2,1,0:T(8,128)(2,1)} %slice.29), channel_id=1, source_target_pairs={{0,96},{32,0},{64,32},{96,64},{1,97},{33,1},{65,33},{97,65},{2,98}... | collective-permute-start | bytes 786440 | tf_op jit(solution)/shard_map/ppermute | solution.py:432
  130.4 3.0 %collective-permute-done.17.refs_6_ = bf16[16,12,8,128]{3,2,1,0:T(8,128)(2,1)} collective-permute-done((bf16[16,12,8,128]{3,2,1,0:T(8,128)(2,1)}, bf16[16,12,8,128]{3,2,1,0:T(8,128)(2,1)}, u32[]{:S(2)}, u32[]{:S(2)}) %collective-permute-start.17) | collective-permute-done | bytes 393248 | tf_op jit(solution)/shard_map/ppermute | solution.py:432
  133.6 5.8 %correlate_far.1.refs_10_ = bf16[20,2,256,1024]{3,2,1,0:T(8,128)(2,1)} custom-call(s32[3]{0:T(128)} %pad_add_fusion.place.refs_0_, bf16[32,12,8,128]{3,2,1,0:T(8,128)(2,1)} %all-to-all-done.refs_1_, bf16[32,20,8,128]{3,2,1,0:T(8,128)(2,1)} %all-to-all-done.1.refs_2_, ...), custom_call_target="tpu_custom_call", output_to_operand_aliasing={{}: (7, {})} | custom-call | flops 10000000000 | bytes 40000000 | tf_op jit(solution)/shard_map/correlate_far/pallas_call | solution.py:303
  141.5 7.7 %correlate.3 = bf16[20,2,256,1024]{3,2,1,0:T(8,128)(2,1)} custom-call(s32[3]{0:T(128)} %pad_add_fusion.place.refs_0_, bf16[32,32,8,128]{3,2,1,0:T(8,128)(2,1)} %copy-done, bf16[32,20,8,128]{3,2,1,0:T(8,128)(2,1)} %all-to-all-done.1.refs_2_, bf16[32,32,8,128]{3,2,1,0:T(8,128)(2,1)} %copy-done, ...), custom_call_target="tpu_custom_call", output_to_operand_aliasing={{}: (10, {})} | custom-call | flops 1000000000 | bytes 4000000 | tf_op jit(solution)/shard_map/correlate/pallas_call | solution.py:379
  (61 shorter events, 19.3 us)
Async XLA Ops:
  4.2 9.6 %collective-permute-start = (bf16[2,128,4096]{2,1,0:T(8,128)(2,1)}, bf16[2,128,4096]{2,1,0:T(8,128)(2,1)}, u32[]{:S(2)}, u32[]{:S(2)}) collective-permute-start(bf16[2,128,4096]{2,1,0:T(8,128)(2,1)} %pick.2), channel_id=1, source_target_pairs={{0,1},{1,0},{2,3},{3,2},{4,5},{5,4},{6,7},{7,6},{8,9},{9,8},{10,11... | collective-permute-start | bytes 6291464 | tf_op jit(solution)/shard_map/ppermute | solution.py:411
  8.1 32.3 %collective-permute-start.4 = (bf16[2,128,2048]{2,1,0:T(8,128)(2,1)}, bf16[2,128,2048]{2,1,0:T(8,128)(2,1)}, u32[]{:S(2)}, u32[]{:S(2)}) collective-permute-start(bf16[2,128,2048]{2,1,0:T(8,128)(2,1)} %get-tuple-element.24), channel_id=1, source_target_pairs={{2,0},{4,2},{6,4},{8,6},{10,8},{12,10},{14,12},{16,14},{18,16},{20... | collective-permute-start | bytes 3145736 | tf_op jit(solution)/shard_map/ppermute | solution.py:417
  9.4 31.3 %collective-permute-start.5 = (bf16[2,128,2048]{2,1,0:T(8,128)(2,1)}, bf16[2,128,2048]{2,1,0:T(8,128)(2,1)}, u32[]{:S(2)}, u32[]{:S(2)}) collective-permute-start(bf16[2,128,2048]{2,1,0:T(8,128)(2,1)} %get-tuple-element.25), channel_id=1, source_target_pairs={{2,1},{4,3},{6,5},{8,7},{10,9},{12,11},{14,13},{16,15},{18,17},{20... | collective-permute-start | bytes 3145736 | tf_op jit(solution)/shard_map/ppermute | solution.py:417
  22.8 27.5 %collective-permute-start.3 = (bf16[32,8,8,128]{3,2,1,0:T(8,128)(2,1)}, bf16[32,8,8,128]{3,2,1,0:T(8,128)(2,1)}, u32[]{:S(2)}, u32[]{:S(2)}) collective-permute-start(bf16[32,8,8,128]{3,2,1,0:T(8,128)(2,1)} %get-tuple-element.30.refs_0_), channel_id=1, source_target_pairs={{0,64},{32,96},{64,0},{96,32},{1,65},{33,97},{65,1},{97,33},{2,66}... | collective-permute-start | bytes 1572872 | tf_op jit(solution)/shard_map/ppermute | solution.py:432
  26.0 24.4 %collective-permute-start.2 = (bf16[32,8,8,128]{3,2,1,0:T(8,128)(2,1)}, bf16[32,8,8,128]{3,2,1,0:T(8,128)(2,1)}, u32[]{:S(2)}, u32[]{:S(2)}) collective-permute-start(bf16[32,8,8,128]{3,2,1,0:T(8,128)(2,1)} %get-tuple-element.30.refs_0_), channel_id=1, source_target_pairs={{0,96},{32,0},{64,32},{96,64},{1,97},{33,1},{65,33},{97,65},{2,98}... | collective-permute-start | bytes 1572872 | tf_op jit(solution)/shard_map/ppermute | solution.py:432
  27.1 23.5 %collective-permute-start.1 = (bf16[32,8,8,128]{3,2,1,0:T(8,128)(2,1)}, bf16[32,8,8,128]{3,2,1,0:T(8,128)(2,1)}, u32[]{:S(2)}, u32[]{:S(2)}) collective-permute-start(bf16[32,8,8,128]{3,2,1,0:T(8,128)(2,1)} %get-tuple-element.30.refs_0_), channel_id=1, source_target_pairs={{0,32},{32,64},{64,96},{96,0},{1,33},{33,65},{65,97},{97,1},{2,34}... | collective-permute-start | bytes 1572872 | tf_op jit(solution)/shard_map/ppermute | solution.py:432
  28.0 26.9 %all-to-all-start = ((bf16[32,12,8,128]{3,2,1,0:T(8,128)(2,1)}), bf16[32,12,8,128]{3,2,1,0:T(8,128)(2,1)}, u32[]{:S(2)}, u32[]{:S(2)}) async-start(bf16[32,12,8,128]{3,2,1,0:T(8,128)(2,1)} %get-tuple-element.28), calls=%async_computation | async-start | bytes 1572864 | tf_op jit(solution)/shard_map/all_to_all | solution.py:435
  54.9 19.6 %collective-permute-start.7 = (bf16[32,12,8,128]{3,2,1,0:T(8,128)(2,1)}, bf16[32,12,8,128]{3,2,1,0:T(8,128)(2,1)S(1)}, u32[]{:S(2)}, u32[]{:S(2)}) collective-permute-start(bf16[32,12,8,128]{3,2,1,0:T(8,128)(2,1)} %all-to-all-done.refs_1_), channel_id=1, source_target_pairs={{0,96},{32,0},{64,32},{96,64},{1,97},{33,1},{65,33},{97,65},{2,98}... | collective-permute-start | bytes 2359304 | tf_op jit(solution)/shard_map/ppermute | solution.py:432
  57.3 21.7 %collective-permute-start.6 = (bf16[32,12,8,128]{3,2,1,0:T(8,128)(2,1)}, bf16[32,12,8,128]{3,2,1,0:T(8,128)(2,1)S(1)}, u32[]{:S(2)}, u32[]{:S(2)}) collective-permute-start(bf16[32,12,8,128]{3,2,1,0:T(8,128)(2,1)} %all-to-all-done.refs_1_), channel_id=1, source_target_pairs={{0,32},{32,64},{64,96},{96,0},{1,33},{33,65},{65,97},{97,1},{2,34}... | collective-permute-start | bytes 2359304 | tf_op jit(solution)/shard_map/ppermute | solution.py:432
  57.3 28.6 %all-to-all-start.1 = ((bf16[32,20,8,128]{3,2,1,0:T(8,128)(2,1)}), bf16[32,20,8,128]{3,2,1,0:T(8,128)(2,1)}, u32[]{:S(2)}, u32[]{:S(2)}) async-start(bf16[32,20,8,128]{3,2,1,0:T(8,128)(2,1)} %channelize.3), calls=%async_computation.1 | async-start | bytes 2621440 | tf_op jit(solution)/shard_map/all_to_all | solution.py:435
  74.5 10.9 %copy-start.1 = (bf16[32,12,8,128]{3,2,1,0:T(8,128)(2,1)}, bf16[32,12,8,128]{3,2,1,0:T(8,128)(2,1)S(1)}, u32[]{:S(2)}) copy-start(bf16[32,12,8,128]{3,2,1,0:T(8,128)(2,1)S(1)} %collective-permute-done.7.refs_5_) | copy-start | bytes 2359300
  75.4 11.6 %collective-permute-start.9 = (bf16[16,12,8,128]{3,2,1,0:T(8,128)(2,1)}, bf16[16,12,8,128]{3,2,1,0:T(8,128)(2,1)}, u32[]{:S(2)}, u32[]{:S(2)}) collective-permute-start(bf16[16,12,8,128]{3,2,1,0:T(8,128)(2,1)} %slice.33), channel_id=1, source_target_pairs={{0,96},{32,0},{64,32},{96,64},{1,97},{33,1},{65,33},{97,65},{2,98}... | collective-permute-start | bytes 1179656 | tf_op jit(solution)/shard_map/ppermute | solution.py:432
  79.8 11.5 %collective-permute-start.8 = (bf16[16,12,8,128]{3,2,1,0:T(8,128)(2,1)}, bf16[16,12,8,128]{3,2,1,0:T(8,128)(2,1)}, u32[]{:S(2)}, u32[]{:S(2)}) collective-permute-start(bf16[16,12,8,128]{3,2,1,0:T(8,128)(2,1)} %slice.32), channel_id=1, source_target_pairs={{0,32},{32,64},{64,96},{96,0},{1,33},{33,65},{65,97},{97,1},{2,34}... | collective-permute-start | bytes 1179656 | tf_op jit(solution)/shard_map/ppermute | solution.py:432
  93.3 20.3 %collective-permute-start.13 = (bf16[32,12,8,128]{3,2,1,0:T(8,128)(2,1)}, bf16[32,12,8,128]{3,2,1,0:T(8,128)(2,1)S(1)}, u32[]{:S(2)}, u32[]{:S(2)}) collective-permute-start(bf16[32,12,8,128]{3,2,1,0:T(8,128)(2,1)} %slice.27), channel_id=1, source_target_pairs={{0,96},{32,0},{64,32},{96,64},{1,97},{33,1},{65,33},{97,65},{2,98}... | collective-permute-start | bytes 2359304 | tf_op jit(solution)/shard_map/ppermute | solution.py:432
  93.3 21.7 %collective-permute-start.12 = (bf16[32,12,8,128]{3,2,1,0:T(8,128)(2,1)}, bf16[32,12,8,128]{3,2,1,0:T(8,128)(2,1)}, u32[]{:S(2)}, u32[]{:S(2)}) collective-permute-start(bf16[32,12,8,128]{3,2,1,0:T(8,128)(2,1)} %slice.27), channel_id=1, source_target_pairs={{0,32},{32,64},{64,96},{96,0},{1,33},{33,65},{65,97},{97,1},{2,34}... | collective-permute-start | bytes 2359304 | tf_op jit(solution)/shard_map/ppermute | solution.py:432
  95.3 44.1 %all-to-all-start.2 = ((bf16[32,32,8,128]{3,2,1,0:T(8,128)(2,1)}), bf16[32,32,8,128]{3,2,1,0:T(8,128)(2,1)S(1)}, u32[]{:S(2)}, u32[]{:S(2)}) async-start(bf16[32,32,8,128]{3,2,1,0:T(8,128)(2,1)} %pack.1), calls=%async_computation.2 | async-start | bytes 4194304 | tf_op jit(solution)/shard_map/all_to_all | solution.py:435
  105.2 22.3 %collective-permute-start.11 = (bf16[32,8,8,128]{3,2,1,0:T(8,128)(2,1)}, bf16[32,8,8,128]{3,2,1,0:T(8,128)(2,1)S(1)}, u32[]{:S(2)}, u32[]{:S(2)}) collective-permute-start(bf16[32,8,8,128]{3,2,1,0:T(8,128)(2,1)} %slice.26), channel_id=1, source_target_pairs={{0,96},{32,0},{64,32},{96,64},{1,97},{33,1},{65,33},{97,65},{2,98}... | collective-permute-start | bytes 1572872 | tf_op jit(solution)/shard_map/ppermute | solution.py:432
  106.4 21.1 %collective-permute-start.10 = (bf16[32,8,8,128]{3,2,1,0:T(8,128)(2,1)}, bf16[32,8,8,128]{3,2,1,0:T(8,128)(2,1)S(1)}, u32[]{:S(2)}, u32[]{:S(2)}) collective-permute-start(bf16[32,8,8,128]{3,2,1,0:T(8,128)(2,1)} %slice.26), channel_id=1, source_target_pairs={{0,32},{32,64},{64,96},{96,0},{1,33},{33,65},{65,97},{97,1},{2,34}... | collective-permute-start | bytes 1572872 | tf_op jit(solution)/shard_map/ppermute | solution.py:432
  114.4 18.9 %collective-permute-start.17 = (bf16[16,12,8,128]{3,2,1,0:T(8,128)(2,1)}, bf16[16,12,8,128]{3,2,1,0:T(8,128)(2,1)}, u32[]{:S(2)}, u32[]{:S(2)}) collective-permute-start(bf16[16,12,8,128]{3,2,1,0:T(8,128)(2,1)} %slice.35), channel_id=1, source_target_pairs={{0,96},{32,0},{64,32},{96,64},{1,97},{33,1},{65,33},{97,65},{2,98}... | collective-permute-start | bytes 1179656 | tf_op jit(solution)/shard_map/ppermute | solution.py:432
  116.7 16.9 %collective-permute-start.16 = (bf16[16,12,8,128]{3,2,1,0:T(8,128)(2,1)}, bf16[16,12,8,128]{3,2,1,0:T(8,128)(2,1)}, u32[]{:S(2)}, u32[]{:S(2)}) collective-permute-start(bf16[16,12,8,128]{3,2,1,0:T(8,128)(2,1)} %slice.34), channel_id=1, source_target_pairs={{0,32},{32,64},{64,96},{96,0},{1,33},{33,65},{65,97},{97,1},{2,34}... | collective-permute-start | bytes 1179656 | tf_op jit(solution)/shard_map/ppermute | solution.py:432
  127.4 11.9 %copy-start.4 = (bf16[32,8,8,128]{3,2,1,0:T(8,128)(2,1)}, bf16[32,8,8,128]{3,2,1,0:T(8,128)(2,1)S(1)}, u32[]{:S(2)}) copy-start(bf16[32,8,8,128]{3,2,1,0:T(8,128)(2,1)S(1)} %collective-permute-done.11.refs_6_) | copy-start | bytes 1572868
  127.5 11.9 %copy-start.5 = (bf16[32,8,8,128]{3,2,1,0:T(8,128)(2,1)}, bf16[32,8,8,128]{3,2,1,0:T(8,128)(2,1)S(1)}, u32[]{:S(2)}) copy-start(bf16[32,8,8,128]{3,2,1,0:T(8,128)(2,1)S(1)} %collective-permute-done.10.refs_4_) | copy-start | bytes 1572868
  128.3 11.1 %collective-permute-start.15 = (bf16[16,8,8,128]{3,2,1,0:T(8,128)(2,1)}, bf16[16,8,8,128]{3,2,1,0:T(8,128)(2,1)S(1)}, u32[]{:S(2)}, u32[]{:S(2)}) collective-permute-start(bf16[16,8,8,128]{3,2,1,0:T(8,128)(2,1)} %slice.29), channel_id=1, source_target_pairs={{0,96},{32,0},{64,32},{96,64},{1,97},{33,1},{65,33},{97,65},{2,98}... | collective-permute-start | bytes 786440 | tf_op jit(solution)/shard_map/ppermute | solution.py:432
  130.1 9.3 %collective-permute-start.14 = (bf16[16,8,8,128]{3,2,1,0:T(8,128)(2,1)S(1)}, bf16[16,8,8,128]{3,2,1,0:T(8,128)(2,1)S(1)}, u32[]{:S(2)}, u32[]{:S(2)}) collective-permute-start(bf16[16,8,8,128]{3,2,1,0:T(8,128)(2,1)S(1)} %slice.28), channel_id=1, source_target_pairs={{0,32},{32,64},{64,96},{96,0},{1,33},{33,65},{65,97},{97,1},{2,34}... | collective-permute-start | bytes 786440 | tf_op jit(solution)/shard_map/ppermute | solution.py:432
  (9 other events, 39.3 us)

commit v5 on v4

--- a/solution.py
+++ b/solution.py
@@ -450,12 +450,11 @@
     own_b = exchanged(after(b, own_a1))
     all_a0 = pack((a0, left_a0, right_a0, far_a0), (left_a1, right_a1))
     own_b = after(own_b, all_a0)
-    ready_b = after(own_b, *far_a1)
-    own_b1 = ready_b[:, small:]
-    own_b0 = ready_b[:, :small]
+    own_b1 = after(own_b[:, small:], *far_a1)
+    own_b0 = after(own_b[:, :small], *far_a1)
     left_b1, right_b1 = ring(own_b1, 1), ring(own_b1, -1)
     left_b0, right_b0 = ring(own_b0, 1), ring(own_b0, -1)
-    all_a0 = exchanged(after(all_a0, ready_b))
+    all_a0 = exchanged(after(all_a0, own_b1))
     far_b1 = far(left_b1, right_b1)
 
     def whole(own, parts, first):

time: 151 us -> 149 us (0.987)
  waiting for transfers between devices: 29.7 us -> 27.9 us
    ppermute x15, waiting for transfers between devices: 24.7 us -> 22.9 us  [ring(): lax.ppermute(value, 'feed', [(k, (k + steps) % groups) for k in range(gro...]
  transfers between devices with their start and end apart: 21 -> 21, of which waited for: 10 -> 9; matrix products, arithmetic and copies ran while one was open for 7% -> 8% of each run, Pallas kernels for 29% -> 29%
where the time goes in v5:
time: 149 us; the launch traced here: 148 us
  Pallas kernels  54.2 us (36%)
  starting transfers between devices  50.3 us (34%)
  waiting for transfers between devices  27.9 us (19%)
  local copies, waits for them, and re-layouts  11.2 us (8%)
  matrix products  3.08 us (2%)
    all_to_all x3, starting transfers between devices, exchanged(): return lax.all_to_all(spectra, 'freq', 0, 0, tiled=True)  28.1 us
    ppermute x15, waiting for transfers between devices, ring(): lax.ppermute(value, 'feed', [(k, (k + steps) % groups) for k in range(gro...  22.9 us
    ppermute x15, starting transfers between devices, ring(): lax.ppermute(value, 'feed', [(k, (k + steps) % groups) for k in range(gro...  19.6 us
    pallas_call x2, Pallas kernels, channelize(): pl.pallas_call(kernel, out_shape=[jax.ShapeDtypeStruct((owners, slots, 2...  18.7 us
    pallas_call x2, Pallas kernels, correlate(): pl.pallas_call(kernel, out_shape=jax.ShapeDtypeStruct(shape, jnp.bfloat16...  16.9 us
    pallas_call x2, Pallas kernels, pick(): pl.pallas_call(pick_kernel, out_shape=[jax.ShapeDtypeStruct((2, half, wid...  7.26 us
    pallas_call x1, Pallas kernels, correlate_far(): pl.pallas_call(kernel, out_shape=jax.ShapeDtypeStruct(shape, jnp.bfloat16...  5.78 us
    pallas_call x1, Pallas kernels, pack(): pl.pallas_call(pack_kernel, grid=(count // step,), out_shape=jax.ShapeDty...  5.62 us
  transfers between devices with their start and end apart: 21, of which 9 were waited for; matrix products, arithmetic and copies ran while one was open for 8% of the time, Pallas kernels for 29%

profile of v5, /device:TPU:0, one launch (start us, length us, event | category | flops | bytes accessed | tf_op | source)
XLA Modules:
  0.0 147.6 jit_solution(18395149397212350762)
XLA Ops:
  0.7 3.6 %pick.2 = bf16[2,128,4096]{2,1,0:T(8,128)(2,1)} custom-call(s32[3]{0:T(128)} %pad_add_fusion.place.refs_0_, bf16[2,256,4096]{2,1,0:T(8,128)(2,1)} %refs_1_.2), custom_call_target="tpu_custom_call" | custom-call | flops 9999999827968 | bytes 20000000000 | tf_op jit(solution)/shard_map/pick/pallas_call | solution.py:75
  4.4 3.7 %pick.3 = (bf16[2,128,2048]{2,1,0:T(8,128)(2,1)}, bf16[2,128,2048]{2,1,0:T(8,128)(2,1)}) custom-call(s32[3]{0:T(128)} %pad_add_fusion.place.refs_0_, bf16[2,256,4096]{2,1,0:T(8,128)(2,1)} %refs_1_.2), custom_call_target="tpu_custom_call" | custom-call | flops 9999999827968 | bytes 20000000000 | tf_op jit(solution)/shard_map/pick/pallas_call | solution.py:75
  10.7 3.1 %convolution_convert_fusion.refs_4_.refs_6_ = bf16[640,2048]{1,0:T(8,128)(2,1)} fusion(bf16[512,2048]{1,0:T(8,128)(2,1)S(1)} %copy-done.10, f32[512]{0:T(512)S(1)} %bitcast.5, s32[512]{0:T(512)S(1)} %copy-done.9, s32[640]{0:T(1024)S(1)} %copy-done.11), kind=kOutput, calls=%fused_computation | convolution fusion | flops 1344143360 | bytes 4725248 | tf_op jit(solution)/shard_map/dot_general | solution.py:427
  13.8 9.0 %channelize.2 = (bf16[32,8,8,128]{3,2,1,0:T(8,128)(2,1)}, bf16[32,12,8,128]{3,2,1,0:T(8,128)(2,1)}) custom-call(s32[3]{0:T(128)} %pad_add_fusion.place.refs_0_, bf16[2,256,4096]{2,1,0:T(8,128)(2,1)} %refs_1_.2, bf16[2,128,4096]{2,1,0:T(8,128)(2,1)} %collective-permute-done.refs_2_, f32[4,1024]{1,0:T(4,128)} %constant.34.clone.refs_3_.refs_5_, ...), custom_call_target="tpu_custom_call" | custom-call | flops 9999999827968 | bytes 20000000000 | tf_op jit(solution)/shard_map/channelize/pallas_call | solution.py:203
  22.8 3.2 %collective-permute-start.3 = (bf16[32,8,8,128]{3,2,1,0:T(8,128)(2,1)}, bf16[32,8,8,128]{3,2,1,0:T(8,128)(2,1)}, u32[]{:S(2)}, u32[]{:S(2)}) collective-permute-start(bf16[32,8,8,128]{3,2,1,0:T(8,128)(2,1)} %get-tuple-element.31.refs_0_), channel_id=1, source_target_pairs={{0,64},{32,96},{64,0},{96,32},{1,65},{33,97},{65,1},{97,33},{2,66}... | collective-permute-start | bytes 1572872 | tf_op jit(solution)/shard_map/ppermute | solution.py:432
  28.0 12.4 %all-to-all-start = ((bf16[32,12,8,128]{3,2,1,0:T(8,128)(2,1)}), bf16[32,12,8,128]{3,2,1,0:T(8,128)(2,1)}, u32[]{:S(2)}, u32[]{:S(2)}) async-start(bf16[32,12,8,128]{3,2,1,0:T(8,128)(2,1)} %get-tuple-element.29), calls=%async_computation | async-start | bytes 1572864 | tf_op jit(solution)/shard_map/all_to_all | solution.py:435
  40.6 9.7 %channelize.3 = bf16[32,20,8,128]{3,2,1,0:T(8,128)(2,1)} custom-call(s32[3]{0:T(128)} %pad_add_fusion.place.refs_0_, bf16[2,256,4096]{2,1,0:T(8,128)(2,1)} %refs_1_.2, bf16[2,128,4096]{2,1,0:T(8,128)(2,1)} %collective-permute-done.refs_2_, bf16[2,128,2048]{2,1,0:T(8,128)(2,1)} %collective-permute-done.4.refs_3_, ...), custom_call_target="tpu_custom_call" | custom-call | flops 9999999827968 | bytes 20000000000 | tf_op jit(solution)/shard_map/channelize/pallas_call | solution.py:203
  50.6 4.3 %all-to-all-done.refs_1_ = bf16[32,12,8,128]{3,2,1,0:T(8,128)(2,1)} async-done(((bf16[32,12,8,128]{3,2,1,0:T(8,128)(2,1)}), bf16[32,12,8,128]{3,2,1,0:T(8,128)(2,1)}, u32[]{:S(2)}, u32[]{:S(2)}) %all-to-all-start) | async-done | bytes 786464 | tf_op jit(solution)/shard_map/all_to_all | solution.py:435
  54.9 2.4 %collective-permute-start.7 = (bf16[32,12,8,128]{3,2,1,0:T(8,128)(2,1)}, bf16[32,12,8,128]{3,2,1,0:T(8,128)(2,1)S(1)}, u32[]{:S(2)}, u32[]{:S(2)}) collective-permute-start(bf16[32,12,8,128]{3,2,1,0:T(8,128)(2,1)} %all-to-all-done.refs_1_), channel_id=1, source_target_pairs={{0,96},{32,0},{64,32},{96,64},{1,97},{33,1},{65,33},{97,65},{2,98}... | collective-permute-start | bytes 2359304 | tf_op jit(solution)/shard_map/ppermute | solution.py:432
  57.3 7.8 %all-to-all-start.1 = ((bf16[32,20,8,128]{3,2,1,0:T(8,128)(2,1)}), bf16[32,20,8,128]{3,2,1,0:T(8,128)(2,1)}, u32[]{:S(2)}, u32[]{:S(2)}) async-start(bf16[32,20,8,128]{3,2,1,0:T(8,128)(2,1)} %channelize.3), calls=%async_computation.1 | async-start | bytes 2621440 | tf_op jit(solution)/shard_map/all_to_all | solution.py:435
  65.1 9.4 %collective-permute-done.7.refs_5_ = bf16[32,12,8,128]{3,2,1,0:T(8,128)(2,1)S(1)} collective-permute-done((bf16[32,12,8,128]{3,2,1,0:T(8,128)(2,1)}, bf16[32,12,8,128]{3,2,1,0:T(8,128)(2,1)S(1)}, u32[]{:S(2)}, u32[]{:S(2)}) %collective-permute-start.7) | collective-permute-done | bytes 786464 | tf_op jit(solution)/shard_map/ppermute | solution.py:432
  75.4 3.6 %collective-permute-start.9 = (bf16[16,12,8,128]{3,2,1,0:T(8,128)(2,1)}, bf16[16,12,8,128]{3,2,1,0:T(8,128)(2,1)}, u32[]{:S(2)}, u32[]{:S(2)}) collective-permute-start(bf16[16,12,8,128]{3,2,1,0:T(8,128)(2,1)} %slice.33), channel_id=1, source_target_pairs={{0,96},{32,0},{64,32},{96,64},{1,97},{33,1},{65,33},{97,65},{2,98}... | collective-permute-start | bytes 1179656 | tf_op jit(solution)/shard_map/ppermute | solution.py:432
  79.8 5.6 %pack.1 = bf16[32,32,8,128]{3,2,1,0:T(8,128)(2,1)} custom-call(bf16[32,8,8,128]{3,2,1,0:T(8,128)(2,1)} %get-tuple-element.31.refs_0_, bf16[32,8,8,128]{3,2,1,0:T(8,128)(2,1)} %collective-permute-done.1.refs_1_, bf16[32,8,8,128]{3,2,1,0:T(8,128)(2,1)} %collective-permute-done.2.refs_2_, bf16[32,8,8,128]{3,2,1,0:T(8,128)(2,1)} %collective-permute-done.3.refs_3_), custom_call_target="tpu_custom_call" | custom-call | flops 9999999827968 | bytes 20000000000 | tf_op jit(solution)/shard_map/pack/pallas_call | solution.py:237
  85.9 2.1 %slice.24 = bf16[32,12,8,128]{3,2,1,0:T(8,128)(2,1)} slice(bf16[32,20,8,128]{3,2,1,0:T(8,128)(2,1)} %all-to-all-done.1.refs_2_), slice={[0:32], [8:20], [0:8], [0:128]} | slice | bytes 1572864 | tf_op jit(solution)/shard_map/slice | solution.py:453
  87.9 3.3 %collective-permute-done.8.refs_3_ = bf16[16,12,8,128]{3,2,1,0:T(8,128)(2,1)} collective-permute-done((bf16[16,12,8,128]{3,2,1,0:T(8,128)(2,1)}, bf16[16,12,8,128]{3,2,1,0:T(8,128)(2,1)}, u32[]{:S(2)}, u32[]{:S(2)}) %collective-permute-start.8) | collective-permute-done | bytes 393248 | tf_op jit(solution)/shard_map/ppermute | solution.py:432
  91.2 2.0 %collective-permute-start.12 = (bf16[32,12,8,128]{3,2,1,0:T(8,128)(2,1)}, bf16[32,12,8,128]{3,2,1,0:T(8,128)(2,1)}, u32[]{:S(2)}, u32[]{:S(2)}) collective-permute-start(bf16[32,12,8,128]{3,2,1,0:T(8,128)(2,1)} %slice.24), channel_id=1, source_target_pairs={{0,32},{32,64},{64,96},{96,0},{1,33},{33,65},{65,97},{97,1},{2,34}... | collective-permute-start | bytes 2359304 | tf_op jit(solution)/shard_map/ppermute | solution.py:432
  93.2 7.9 %all-to-all-start.2 = ((bf16[32,32,8,128]{3,2,1,0:T(8,128)(2,1)}), bf16[32,32,8,128]{3,2,1,0:T(8,128)(2,1)S(1)}, u32[]{:S(2)}, u32[]{:S(2)}) async-start(bf16[32,32,8,128]{3,2,1,0:T(8,128)(2,1)} %pack.1), calls=%async_computation.2 | async-start | bytes 4194304 | tf_op jit(solution)/shard_map/all_to_all | solution.py:435
  101.2 1.9 %slice.27 = bf16[32,8,8,128]{3,2,1,0:T(8,128)(2,1)} slice(bf16[32,20,8,128]{3,2,1,0:T(8,128)(2,1)} %all-to-all-done.1.refs_2_), slice={[0:32], [0:8], [0:8], [0:128]} | slice | bytes 1048576 | tf_op jit(solution)/shard_map/slice | solution.py:454
  105.1 6.4 %collective-permute-done.13.refs_6_ = bf16[32,12,8,128]{3,2,1,0:T(8,128)(2,1)S(1)} collective-permute-done((bf16[32,12,8,128]{3,2,1,0:T(8,128)(2,1)}, bf16[32,12,8,128]{3,2,1,0:T(8,128)(2,1)S(1)}, u32[]{:S(2)}, u32[]{:S(2)}) %collective-permute-start.13) | collective-permute-done | bytes 786464 | tf_op jit(solution)/shard_map/ppermute | solution.py:432
  116.1 9.2 %correlate.2.refs_7_ = bf16[20,2,256,1024]{3,2,1,0:T(8,128)(2,1)} custom-call(s32[3]{0:T(128)} %pad_add_fusion.place.refs_0_, bf16[32,12,8,128]{3,2,1,0:T(8,128)(2,1)} %all-to-all-done.refs_1_, bf16[32,20,8,128]{3,2,1,0:T(8,128)(2,1)} %all-to-all-done.1.refs_2_, bf16[32,12,8,128]{3,2,1,0:T(8,128)(2,1)} %copy-done.2, ...), custom_call_target="tpu_custom_call" | custom-call | flops 1000000000 | bytes 4000000 | tf_op jit(solution)/shard_map/correlate/pallas_call | solution.py:379
  126.3 2.3 %collective-permute-start.15 = (bf16[16,8,8,128]{3,2,1,0:T(8,128)(2,1)}, bf16[16,8,8,128]{3,2,1,0:T(8,128)(2,1)S(1)}, u32[]{:S(2)}, u32[]{:S(2)}) collective-permute-start(bf16[16,8,8,128]{3,2,1,0:T(8,128)(2,1)} %slice.29), channel_id=1, source_target_pairs={{0,96},{32,0},{64,32},{96,64},{1,97},{33,1},{65,33},{97,65},{2,98}... | collective-permute-start | bytes 786440 | tf_op jit(solution)/shard_map/ppermute | solution.py:432
  128.6 2.6 %collective-permute-done.17.refs_6_ = bf16[16,12,8,128]{3,2,1,0:T(8,128)(2,1)} collective-permute-done((bf16[16,12,8,128]{3,2,1,0:T(8,128)(2,1)}, bf16[16,12,8,128]{3,2,1,0:T(8,128)(2,1)}, u32[]{:S(2)}, u32[]{:S(2)}) %collective-permute-start.17) | collective-permute-done | bytes 393248 | tf_op jit(solution)/shard_map/ppermute | solution.py:432
  132.1 5.8 %correlate_far.1.refs_10_ = bf16[20,2,256,1024]{3,2,1,0:T(8,128)(2,1)} custom-call(s32[3]{0:T(128)} %pad_add_fusion.place.refs_0_, bf16[32,12,8,128]{3,2,1,0:T(8,128)(2,1)} %all-to-all-done.refs_1_, bf16[32,20,8,128]{3,2,1,0:T(8,128)(2,1)} %all-to-all-done.1.refs_2_, ...), custom_call_target="tpu_custom_call", output_to_operand_aliasing={{}: (7, {})} | custom-call | flops 10000000000 | bytes 40000000 | tf_op jit(solution)/shard_map/correlate_far/pallas_call | solution.py:303
  140.0 7.7 %correlate.3 = bf16[20,2,256,1024]{3,2,1,0:T(8,128)(2,1)} custom-call(s32[3]{0:T(128)} %pad_add_fusion.place.refs_0_, bf16[32,32,8,128]{3,2,1,0:T(8,128)(2,1)} %copy-done, bf16[32,20,8,128]{3,2,1,0:T(8,128)(2,1)} %all-to-all-done.1.refs_2_, bf16[32,32,8,128]{3,2,1,0:T(8,128)(2,1)} %copy-done, ...), custom_call_target="tpu_custom_call", output_to_operand_aliasing={{}: (10, {})} | custom-call | flops 1000000000 | bytes 4000000 | tf_op jit(solution)/shard_map/correlate/pallas_call | solution.py:379
  (61 shorter events, 18.5 us)
Async XLA Ops:
  4.2 9.6 %collective-permute-start = (bf16[2,128,4096]{2,1,0:T(8,128)(2,1)}, bf16[2,128,4096]{2,1,0:T(8,128)(2,1)}, u32[]{:S(2)}, u32[]{:S(2)}) collective-permute-start(bf16[2,128,4096]{2,1,0:T(8,128)(2,1)} %pick.2), channel_id=1, source_target_pairs={{0,1},{1,0},{2,3},{3,2},{4,5},{5,4},{6,7},{7,6},{8,9},{9,8},{10,11... | collective-permute-start | bytes 6291464 | tf_op jit(solution)/shard_map/ppermute | solution.py:411
  8.1 32.3 %collective-permute-start.4 = (bf16[2,128,2048]{2,1,0:T(8,128)(2,1)}, bf16[2,128,2048]{2,1,0:T(8,128)(2,1)}, u32[]{:S(2)}, u32[]{:S(2)}) collective-permute-start(bf16[2,128,2048]{2,1,0:T(8,128)(2,1)} %get-tuple-element.25), channel_id=1, source_target_pairs={{2,0},{4,2},{6,4},{8,6},{10,8},{12,10},{14,12},{16,14},{18,16},{20... | collective-permute-start | bytes 3145736 | tf_op jit(solution)/shard_map/ppermute | solution.py:417
  9.4 31.3 %collective-permute-start.5 = (bf16[2,128,2048]{2,1,0:T(8,128)(2,1)}, bf16[2,128,2048]{2,1,0:T(8,128)(2,1)}, u32[]{:S(2)}, u32[]{:S(2)}) collective-permute-start(bf16[2,128,2048]{2,1,0:T(8,128)(2,1)} %get-tuple-element.26), channel_id=1, source_target_pairs={{2,1},{4,3},{6,5},{8,7},{10,9},{12,11},{14,13},{16,15},{18,17},{20... | collective-permute-start | bytes 3145736 | tf_op jit(solution)/shard_map/ppermute | solution.py:417
  22.8 27.5 %collective-permute-start.3 = (bf16[32,8,8,128]{3,2,1,0:T(8,128)(2,1)}, bf16[32,8,8,128]{3,2,1,0:T(8,128)(2,1)}, u32[]{:S(2)}, u32[]{:S(2)}) collective-permute-start(bf16[32,8,8,128]{3,2,1,0:T(8,128)(2,1)} %get-tuple-element.31.refs_0_), channel_id=1, source_target_pairs={{0,64},{32,96},{64,0},{96,32},{1,65},{33,97},{65,1},{97,33},{2,66}... | collective-permute-start | bytes 1572872 | tf_op jit(solution)/shard_map/ppermute | solution.py:432
  26.0 24.4 %collective-permute-start.2 = (bf16[32,8,8,128]{3,2,1,0:T(8,128)(2,1)}, bf16[32,8,8,128]{3,2,1,0:T(8,128)(2,1)}, u32[]{:S(2)}, u32[]{:S(2)}) collective-permute-start(bf16[32,8,8,128]{3,2,1,0:T(8,128)(2,1)} %get-tuple-element.31.refs_0_), channel_id=1, source_target_pairs={{0,96},{32,0},{64,32},{96,64},{1,97},{33,1},{65,33},{97,65},{2,98}... | collective-permute-start | bytes 1572872 | tf_op jit(solution)/shard_map/ppermute | solution.py:432
  27.1 23.5 %collective-permute-start.1 = (bf16[32,8,8,128]{3,2,1,0:T(8,128)(2,1)}, bf16[32,8,8,128]{3,2,1,0:T(8,128)(2,1)}, u32[]{:S(2)}, u32[]{:S(2)}) collective-permute-start(bf16[32,8,8,128]{3,2,1,0:T(8,128)(2,1)} %get-tuple-element.31.refs_0_), channel_id=1, source_target_pairs={{0,32},{32,64},{64,96},{96,0},{1,33},{33,65},{65,97},{97,1},{2,34}... | collective-permute-start | bytes 1572872 | tf_op jit(solution)/shard_map/ppermute | solution.py:432
  28.0 26.9 %all-to-all-start = ((bf16[32,12,8,128]{3,2,1,0:T(8,128)(2,1)}), bf16[32,12,8,128]{3,2,1,0:T(8,128)(2,1)}, u32[]{:S(2)}, u32[]{:S(2)}) async-start(bf16[32,12,8,128]{3,2,1,0:T(8,128)(2,1)} %get-tuple-element.29), calls=%async_computation | async-start | bytes 1572864 | tf_op jit(solution)/shard_map/all_to_all | solution.py:435
  54.9 19.6 %collective-permute-start.7 = (bf16[32,12,8,128]{3,2,1,0:T(8,128)(2,1)}, bf16[32,12,8,128]{3,2,1,0:T(8,128)(2,1)S(1)}, u32[]{:S(2)}, u32[]{:S(2)}) collective-permute-start(bf16[32,12,8,128]{3,2,1,0:T(8,128)(2,1)} %all-to-all-done.refs_1_), channel_id=1, source_target_pairs={{0,96},{32,0},{64,32},{96,64},{1,97},{33,1},{65,33},{97,65},{2,98}... | collective-permute-start | bytes 2359304 | tf_op jit(solution)/shard_map/ppermute | solution.py:432
  57.3 21.7 %collective-permute-start.6 = (bf16[32,12,8,128]{3,2,1,0:T(8,128)(2,1)}, bf16[32,12,8,128]{3,2,1,0:T(8,128)(2,1)S(1)}, u32[]{:S(2)}, u32[]{:S(2)}) collective-permute-start(bf16[32,12,8,128]{3,2,1,0:T(8,128)(2,1)} %all-to-all-done.refs_1_), channel_id=1, source_target_pairs={{0,32},{32,64},{64,96},{96,0},{1,33},{33,65},{65,97},{97,1},{2,34}... | collective-permute-start | bytes 2359304 | tf_op jit(solution)/shard_map/ppermute | solution.py:432
  57.3 28.6 %all-to-all-start.1 = ((bf16[32,20,8,128]{3,2,1,0:T(8,128)(2,1)}), bf16[32,20,8,128]{3,2,1,0:T(8,128)(2,1)}, u32[]{:S(2)}, u32[]{:S(2)}) async-start(bf16[32,20,8,128]{3,2,1,0:T(8,128)(2,1)} %channelize.3), calls=%async_computation.1 | async-start | bytes 2621440 | tf_op jit(solution)/shard_map/all_to_all | solution.py:435
  74.5 10.9 %copy-start.1 = (bf16[32,12,8,128]{3,2,1,0:T(8,128)(2,1)}, bf16[32,12,8,128]{3,2,1,0:T(8,128)(2,1)S(1)}, u32[]{:S(2)}) copy-start(bf16[32,12,8,128]{3,2,1,0:T(8,128)(2,1)S(1)} %collective-permute-done.7.refs_5_) | copy-start | bytes 2359300
  75.4 12.6 %collective-permute-start.9 = (bf16[16,12,8,128]{3,2,1,0:T(8,128)(2,1)}, bf16[16,12,8,128]{3,2,1,0:T(8,128)(2,1)}, u32[]{:S(2)}, u32[]{:S(2)}) collective-permute-start(bf16[16,12,8,128]{3,2,1,0:T(8,128)(2,1)} %slice.33), channel_id=1, source_target_pairs={{0,96},{32,0},{64,32},{96,64},{1,97},{33,1},{65,33},{97,65},{2,98}... | collective-permute-start | bytes 1179656 | tf_op jit(solution)/shard_map/ppermute | solution.py:432
  79.8 11.5 %collective-permute-start.8 = (bf16[16,12,8,128]{3,2,1,0:T(8,128)(2,1)}, bf16[16,12,8,128]{3,2,1,0:T(8,128)(2,1)}, u32[]{:S(2)}, u32[]{:S(2)}) collective-permute-start(bf16[16,12,8,128]{3,2,1,0:T(8,128)(2,1)} %slice.32), channel_id=1, source_target_pairs={{0,32},{32,64},{64,96},{96,0},{1,33},{33,65},{65,97},{97,1},{2,34}... | collective-permute-start | bytes 1179656 | tf_op jit(solution)/shard_map/ppermute | solution.py:432
  91.2 20.3 %collective-permute-start.13 = (bf16[32,12,8,128]{3,2,1,0:T(8,128)(2,1)}, bf16[32,12,8,128]{3,2,1,0:T(8,128)(2,1)S(1)}, u32[]{:S(2)}, u32[]{:S(2)}) collective-permute-start(bf16[32,12,8,128]{3,2,1,0:T(8,128)(2,1)} %slice.24), channel_id=1, source_target_pairs={{0,96},{32,0},{64,32},{96,64},{1,97},{33,1},{65,33},{97,65},{2,98}... | collective-permute-start | bytes 2359304 | tf_op jit(solution)/shard_map/ppermute | solution.py:432
  91.2 22.2 %collective-permute-start.12 = (bf16[32,12,8,128]{3,2,1,0:T(8,128)(2,1)}, bf16[32,12,8,128]{3,2,1,0:T(8,128)(2,1)}, u32[]{:S(2)}, u32[]{:S(2)}) collective-permute-start(bf16[32,12,8,128]{3,2,1,0:T(8,128)(2,1)} %slice.24), channel_id=1, source_target_pairs={{0,32},{32,64},{64,96},{96,0},{1,33},{33,65},{65,97},{97,1},{2,34}... | collective-permute-start | bytes 2359304 | tf_op jit(solution)/shard_map/ppermute | solution.py:432
  93.2 44.7 %all-to-all-start.2 = ((bf16[32,32,8,128]{3,2,1,0:T(8,128)(2,1)}), bf16[32,32,8,128]{3,2,1,0:T(8,128)(2,1)S(1)}, u32[]{:S(2)}, u32[]{:S(2)}) async-start(bf16[32,32,8,128]{3,2,1,0:T(8,128)(2,1)} %pack.1), calls=%async_computation.2 | async-start | bytes 4194304 | tf_op jit(solution)/shard_map/all_to_all | solution.py:435
  103.1 22.3 %collective-permute-start.11 = (bf16[32,8,8,128]{3,2,1,0:T(8,128)(2,1)}, bf16[32,8,8,128]{3,2,1,0:T(8,128)(2,1)S(1)}, u32[]{:S(2)}, u32[]{:S(2)}) collective-permute-start(bf16[32,8,8,128]{3,2,1,0:T(8,128)(2,1)} %slice.27), channel_id=1, source_target_pairs={{0,96},{32,0},{64,32},{96,64},{1,97},{33,1},{65,33},{97,65},{2,98}... | collective-permute-start | bytes 1572872 | tf_op jit(solution)/shard_map/ppermute | solution.py:432
  104.3 21.1 %collective-permute-start.10 = (bf16[32,8,8,128]{3,2,1,0:T(8,128)(2,1)}, bf16[32,8,8,128]{3,2,1,0:T(8,128)(2,1)S(1)}, u32[]{:S(2)}, u32[]{:S(2)}) collective-permute-start(bf16[32,8,8,128]{3,2,1,0:T(8,128)(2,1)} %slice.27), channel_id=1, source_target_pairs={{0,32},{32,64},{64,96},{96,0},{1,33},{33,65},{65,97},{97,1},{2,34}... | collective-permute-start | bytes 1572872 | tf_op jit(solution)/shard_map/ppermute | solution.py:432
  112.3 18.9 %collective-permute-start.17 = (bf16[16,12,8,128]{3,2,1,0:T(8,128)(2,1)}, bf16[16,12,8,128]{3,2,1,0:T(8,128)(2,1)}, u32[]{:S(2)}, u32[]{:S(2)}) collective-permute-start(bf16[16,12,8,128]{3,2,1,0:T(8,128)(2,1)} %slice.35), channel_id=1, source_target_pairs={{0,96},{32,0},{64,32},{96,64},{1,97},{33,1},{65,33},{97,65},{2,98}... | collective-permute-start | bytes 1179656 | tf_op jit(solution)/shard_map/ppermute | solution.py:432
  115.2 16.9 %collective-permute-start.16 = (bf16[16,12,8,128]{3,2,1,0:T(8,128)(2,1)}, bf16[16,12,8,128]{3,2,1,0:T(8,128)(2,1)}, u32[]{:S(2)}, u32[]{:S(2)}) collective-permute-start(bf16[16,12,8,128]{3,2,1,0:T(8,128)(2,1)} %slice.34), channel_id=1, source_target_pairs={{0,32},{32,64},{64,96},{96,0},{1,33},{33,65},{65,97},{97,1},{2,34}... | collective-permute-start | bytes 1179656 | tf_op jit(solution)/shard_map/ppermute | solution.py:432
  125.4 12.5 %copy-start.4 = (bf16[32,8,8,128]{3,2,1,0:T(8,128)(2,1)}, bf16[32,8,8,128]{3,2,1,0:T(8,128)(2,1)S(1)}, u32[]{:S(2)}) copy-start(bf16[32,8,8,128]{3,2,1,0:T(8,128)(2,1)S(1)} %collective-permute-done.11.refs_6_) | copy-start | bytes 1572868
  125.4 12.5 %copy-start.5 = (bf16[32,8,8,128]{3,2,1,0:T(8,128)(2,1)}, bf16[32,8,8,128]{3,2,1,0:T(8,128)(2,1)S(1)}, u32[]{:S(2)}) copy-start(bf16[32,8,8,128]{3,2,1,0:T(8,128)(2,1)S(1)} %collective-permute-done.10.refs_4_) | copy-start | bytes 1572868
  126.3 11.6 %collective-permute-start.15 = (bf16[16,8,8,128]{3,2,1,0:T(8,128)(2,1)}, bf16[16,8,8,128]{3,2,1,0:T(8,128)(2,1)S(1)}, u32[]{:S(2)}, u32[]{:S(2)}) collective-permute-start(bf16[16,8,8,128]{3,2,1,0:T(8,128)(2,1)} %slice.29), channel_id=1, source_target_pairs={{0,96},{32,0},{64,32},{96,64},{1,97},{33,1},{65,33},{97,65},{2,98}... | collective-permute-start | bytes 786440 | tf_op jit(solution)/shard_map/ppermute | solution.py:432
  128.6 9.3 %collective-permute-start.14 = (bf16[16,8,8,128]{3,2,1,0:T(8,128)(2,1)S(1)}, bf16[16,8,8,128]{3,2,1,0:T(8,128)(2,1)S(1)}, u32[]{:S(2)}, u32[]{:S(2)}) collective-permute-start(bf16[16,8,8,128]{3,2,1,0:T(8,128)(2,1)S(1)} %slice.28), channel_id=1, source_target_pairs={{0,32},{32,64},{64,96},{96,0},{1,33},{33,65},{65,97},{97,1},{2,34}... | collective-permute-start | bytes 786440 | tf_op jit(solution)/shard_map/ppermute | solution.py:432
  (9 other events, 39.3 us)

commit v6 on v5

--- a/solution.py
+++ b/solution.py
@@ -311,7 +311,7 @@
         ),
         input_output_aliases={len(operands) + 1: 0},
         compiler_params=pltpu.CompilerParams(
-            dimension_semantics=("arbitrary",), vmem_limit_bytes=VMEM
+            dimension_semantics=("arbitrary",), vmem_limit_bytes=VMEM // 2
         ),
         cost_estimate=pl.CostEstimate(flops=10**10, bytes_accessed=4 * 10**7, transcendentals=0),
         name="correlate_far",
@@ -389,7 +389,7 @@
         ),
         input_output_aliases=aliases,
         compiler_params=pltpu.CompilerParams(
-            dimension_semantics=("arbitrary",), vmem_limit_bytes=VMEM
+            dimension_semantics=("arbitrary",), vmem_limit_bytes=VMEM // 2
         ),
         cost_estimate=pl.CostEstimate(flops=10**9, bytes_accessed=4 * 10**6, transcendentals=0),
         name="correlate",

time: 149 us -> 149 us (level)
  waiting for transfers between devices: 27.9 us -> 32.2 us
  local copies, waits for them, and re-layouts: 11.2 us -> 8.75 us
  Pallas kernels: 54.2 us -> 52.1 us
    ppermute x15, waiting for transfers between devices: 22.9 us -> 27.1 us  [ring(): lax.ppermute(value, 'feed', [(k, (k + steps) % groups) for k in range(gro...]
    slice x6, local copies, waits for them, and re-layouts: 5.12 us -> 2.75 us  [far(): return (ring(left[:middle], 1), ring(right[middle:], -1))]
    pallas_call x2, Pallas kernels: 16.9 us -> 15.3 us  [correlate(): pl.pallas_call(kernel, out_shape=jax.ShapeDtypeStruct(shape, jnp.bfloat16...]
  transfers between devices with their start and end apart: 21 -> 21, of which waited for: 9 -> 10; matrix products, arithmetic and copies ran while one was open for 8% -> 6% of each run, Pallas kernels for 29% -> 28%
where the time goes in v6:
time: 149 us; the launch traced here: 147 us
  Pallas kernels  52.1 us (35%)
  starting transfers between devices  50.4 us (34%)
  waiting for transfers between devices  32.2 us (22%)
  local copies, waits for them, and re-layouts  8.75 us (6%)
  matrix products  3.08 us (2%)
    all_to_all x3, starting transfers between devices, exchanged(): return lax.all_to_all(spectra, 'freq', 0, 0, tiled=True)  28.1 us
    ppermute x15, waiting for transfers between devices, ring(): lax.ppermute(value, 'feed', [(k, (k + steps) % groups) for k in range(gro...  27.1 us
    ppermute x15, starting transfers between devices, ring(): lax.ppermute(value, 'feed', [(k, (k + steps) % groups) for k in range(gro...  19.7 us
    pallas_call x2, Pallas kernels, channelize(): pl.pallas_call(kernel, out_shape=[jax.ShapeDtypeStruct((owners, slots, 2...  18.7 us
    pallas_call x2, Pallas kernels, correlate(): pl.pallas_call(kernel, out_shape=jax.ShapeDtypeStruct(shape, jnp.bfloat16...  15.3 us
    pallas_call x2, Pallas kernels, pick(): pl.pallas_call(pick_kernel, out_shape=[jax.ShapeDtypeStruct((2, half, wid...  7.22 us
    pallas_call x1, Pallas kernels, pack(): pl.pallas_call(pack_kernel, grid=(count // step,), out_shape=jax.ShapeDty...  5.62 us
    pallas_call x1, Pallas kernels, correlate_far(): pl.pallas_call(kernel, out_shape=jax.ShapeDtypeStruct(shape, jnp.bfloat16...  5.25 us
  transfers between devices with their start and end apart: 21, of which 10 were waited for; matrix products, arithmetic and copies ran while one was open for 6% of the time, Pallas kernels for 28%

profile of v6, /device:TPU:0, one launch (start us, length us, event | category | flops | bytes accessed | tf_op | source)
XLA Modules:
  0.0 147.4 jit_solution(7630228634211514128)
XLA Ops:
  0.6 3.6 %pick.2 = bf16[2,128,4096]{2,1,0:T(8,128)(2,1)} custom-call(s32[3]{0:T(128)} %pad_add_fusion.place.refs_0_, bf16[2,256,4096]{2,1,0:T(8,128)(2,1)} %refs_1_.2), custom_call_target="tpu_custom_call" | custom-call | flops 9999999827968 | bytes 20000000000 | tf_op jit(solution)/shard_map/pick/pallas_call | solution.py:75
  4.3 3.7 %pick.3 = (bf16[2,128,2048]{2,1,0:T(8,128)(2,1)}, bf16[2,128,2048]{2,1,0:T(8,128)(2,1)}) custom-call(s32[3]{0:T(128)} %pad_add_fusion.place.refs_0_, bf16[2,256,4096]{2,1,0:T(8,128)(2,1)} %refs_1_.2), custom_call_target="tpu_custom_call" | custom-call | flops 9999999827968 | bytes 20000000000 | tf_op jit(solution)/shard_map/pick/pallas_call | solution.py:75
  10.6 3.1 %convolution_convert_fusion.refs_4_.refs_6_ = bf16[640,2048]{1,0:T(8,128)(2,1)} fusion(bf16[512,2048]{1,0:T(8,128)(2,1)S(1)} %copy-done.11, f32[512]{0:T(512)S(1)} %bitcast.5, s32[512]{0:T(512)S(1)} %copy-done.10, s32[640]{0:T(1024)S(1)} %copy-done.12), kind=kOutput, calls=%fused_computation | convolution fusion | flops 1344143360 | bytes 4725248 | tf_op jit(solution)/shard_map/dot_general | solution.py:427
  13.7 8.9 %channelize.2 = (bf16[32,8,8,128]{3,2,1,0:T(8,128)(2,1)}, bf16[32,12,8,128]{3,2,1,0:T(8,128)(2,1)}) custom-call(s32[3]{0:T(128)} %pad_add_fusion.place.refs_0_, bf16[2,256,4096]{2,1,0:T(8,128)(2,1)} %refs_1_.2, bf16[2,128,4096]{2,1,0:T(8,128)(2,1)} %collective-permute-done.refs_2_, f32[4,1024]{1,0:T(4,128)} %constant.34.clone.refs_3_.refs_5_, ...), custom_call_target="tpu_custom_call" | custom-call | flops 9999999827968 | bytes 20000000000 | tf_op jit(solution)/shard_map/channelize/pallas_call | solution.py:203
  22.6 3.2 %collective-permute-start.3 = (bf16[32,8,8,128]{3,2,1,0:T(8,128)(2,1)}, bf16[32,8,8,128]{3,2,1,0:T(8,128)(2,1)}, u32[]{:S(2)}, u32[]{:S(2)}) collective-permute-start(bf16[32,8,8,128]{3,2,1,0:T(8,128)(2,1)} %get-tuple-element.31.refs_0_), channel_id=1, source_target_pairs={{0,64},{32,96},{64,0},{96,32},{1,65},{33,97},{65,1},{97,33},{2,66}... | collective-permute-start | bytes 1572872 | tf_op jit(solution)/shard_map/ppermute | solution.py:432
  27.9 12.4 %all-to-all-start = ((bf16[32,12,8,128]{3,2,1,0:T(8,128)(2,1)}), bf16[32,12,8,128]{3,2,1,0:T(8,128)(2,1)}, u32[]{:S(2)}, u32[]{:S(2)}) async-start(bf16[32,12,8,128]{3,2,1,0:T(8,128)(2,1)} %get-tuple-element.29), calls=%async_computation | async-start | bytes 1572864 | tf_op jit(solution)/shard_map/all_to_all | solution.py:435
  40.5 9.7 %channelize.3 = bf16[32,20,8,128]{3,2,1,0:T(8,128)(2,1)} custom-call(s32[3]{0:T(128)} %pad_add_fusion.place.refs_0_, bf16[2,256,4096]{2,1,0:T(8,128)(2,1)} %refs_1_.2, bf16[2,128,4096]{2,1,0:T(8,128)(2,1)} %collective-permute-done.refs_2_, bf16[2,128,2048]{2,1,0:T(8,128)(2,1)} %collective-permute-done.4.refs_3_, ...), custom_call_target="tpu_custom_call" | custom-call | flops 9999999827968 | bytes 20000000000 | tf_op jit(solution)/shard_map/channelize/pallas_call | solution.py:203
  50.5 4.3 %all-to-all-done.refs_1_ = bf16[32,12,8,128]{3,2,1,0:T(8,128)(2,1)} async-done(((bf16[32,12,8,128]{3,2,1,0:T(8,128)(2,1)}), bf16[32,12,8,128]{3,2,1,0:T(8,128)(2,1)}, u32[]{:S(2)}, u32[]{:S(2)}) %all-to-all-start) | async-done | bytes 786464 | tf_op jit(solution)/shard_map/all_to_all | solution.py:435
  54.8 2.3 %collective-permute-start.7 = (bf16[32,12,8,128]{3,2,1,0:T(8,128)(2,1)}, bf16[32,12,8,128]{3,2,1,0:T(8,128)(2,1)S(1)}, u32[]{:S(2)}, u32[]{:S(2)}) collective-permute-start(bf16[32,12,8,128]{3,2,1,0:T(8,128)(2,1)} %all-to-all-done.refs_1_), channel_id=1, source_target_pairs={{0,96},{32,0},{64,32},{96,64},{1,97},{33,1},{65,33},{97,65},{2,98}... | collective-permute-start | bytes 2359304 | tf_op jit(solution)/shard_map/ppermute | solution.py:432
  57.1 7.8 %all-to-all-start.1 = ((bf16[32,20,8,128]{3,2,1,0:T(8,128)(2,1)}), bf16[32,20,8,128]{3,2,1,0:T(8,128)(2,1)}, u32[]{:S(2)}, u32[]{:S(2)}) async-start(bf16[32,20,8,128]{3,2,1,0:T(8,128)(2,1)} %channelize.3), calls=%async_computation.1 | async-start | bytes 2621440 | tf_op jit(solution)/shard_map/all_to_all | solution.py:435
  64.9 9.5 %collective-permute-done.7.refs_5_ = bf16[32,12,8,128]{3,2,1,0:T(8,128)(2,1)S(1)} collective-permute-done((bf16[32,12,8,128]{3,2,1,0:T(8,128)(2,1)}, bf16[32,12,8,128]{3,2,1,0:T(8,128)(2,1)S(1)}, u32[]{:S(2)}, u32[]{:S(2)}) %collective-permute-start.7) | collective-permute-done | bytes 786464 | tf_op jit(solution)/shard_map/ppermute | solution.py:432
  75.2 3.6 %collective-permute-start.9 = (bf16[16,12,8,128]{3,2,1,0:T(8,128)(2,1)}, bf16[16,12,8,128]{3,2,1,0:T(8,128)(2,1)}, u32[]{:S(2)}, u32[]{:S(2)}) collective-permute-start(bf16[16,12,8,128]{3,2,1,0:T(8,128)(2,1)} %slice.33), channel_id=1, source_target_pairs={{0,96},{32,0},{64,32},{96,64},{1,97},{33,1},{65,33},{97,65},{2,98}... | collective-permute-start | bytes 1179656 | tf_op jit(solution)/shard_map/ppermute | solution.py:432
  79.6 5.6 %pack.1 = bf16[32,32,8,128]{3,2,1,0:T(8,128)(2,1)} custom-call(bf16[32,8,8,128]{3,2,1,0:T(8,128)(2,1)} %get-tuple-element.31.refs_0_, bf16[32,8,8,128]{3,2,1,0:T(8,128)(2,1)} %collective-permute-done.1.refs_1_, bf16[32,8,8,128]{3,2,1,0:T(8,128)(2,1)} %collective-permute-done.2.refs_2_, bf16[32,8,8,128]{3,2,1,0:T(8,128)(2,1)} %collective-permute-done.3.refs_3_), custom_call_target="tpu_custom_call" | custom-call | flops 9999999827968 | bytes 20000000000 | tf_op jit(solution)/shard_map/pack/pallas_call | solution.py:237
  85.7 2.1 %slice.24 = bf16[32,12,8,128]{3,2,1,0:T(8,128)(2,1)} slice(bf16[32,20,8,128]{3,2,1,0:T(8,128)(2,1)} %all-to-all-done.1.refs_2_), slice={[0:32], [8:20], [0:8], [0:128]} | slice | bytes 1572864 | tf_op jit(solution)/shard_map/slice | solution.py:453
  87.8 3.3 %collective-permute-done.8.refs_3_ = bf16[16,12,8,128]{3,2,1,0:T(8,128)(2,1)} collective-permute-done((bf16[16,12,8,128]{3,2,1,0:T(8,128)(2,1)}, bf16[16,12,8,128]{3,2,1,0:T(8,128)(2,1)}, u32[]{:S(2)}, u32[]{:S(2)}) %collective-permute-start.8) | collective-permute-done | bytes 393248 | tf_op jit(solution)/shard_map/ppermute | solution.py:432
  91.1 2.0 %collective-permute-start.12 = (bf16[32,12,8,128]{3,2,1,0:T(8,128)(2,1)}, bf16[32,12,8,128]{3,2,1,0:T(8,128)(2,1)}, u32[]{:S(2)}, u32[]{:S(2)}) collective-permute-start(bf16[32,12,8,128]{3,2,1,0:T(8,128)(2,1)} %slice.24), channel_id=1, source_target_pairs={{0,32},{32,64},{64,96},{96,0},{1,33},{33,65},{65,97},{97,1},{2,34}... | collective-permute-start | bytes 2359304 | tf_op jit(solution)/shard_map/ppermute | solution.py:432
  93.1 7.9 %all-to-all-start.2 = ((bf16[32,32,8,128]{3,2,1,0:T(8,128)(2,1)}), bf16[32,32,8,128]{3,2,1,0:T(8,128)(2,1)S(1)}, u32[]{:S(2)}, u32[]{:S(2)}) async-start(bf16[32,32,8,128]{3,2,1,0:T(8,128)(2,1)} %pack.1), calls=%async_computation.2 | async-start | bytes 4194304 | tf_op jit(solution)/shard_map/all_to_all | solution.py:435
  102.3 1.5 collective-permute-start.11
  104.5 7.2 %collective-permute-done.13.refs_6_ = bf16[32,12,8,128]{3,2,1,0:T(8,128)(2,1)S(1)} collective-permute-done((bf16[32,12,8,128]{3,2,1,0:T(8,128)(2,1)}, bf16[32,12,8,128]{3,2,1,0:T(8,128)(2,1)S(1)}, u32[]{:S(2)}, u32[]{:S(2)}) %collective-permute-start.13) | collective-permute-done | bytes 786464 | tf_op jit(solution)/shard_map/ppermute | solution.py:432
  115.0 8.3 %correlate.2.refs_7_ = bf16[20,2,256,1024]{3,2,1,0:T(8,128)(2,1)} custom-call(s32[3]{0:T(128)S(1)} %copy-done.8, bf16[32,12,8,128]{3,2,1,0:T(8,128)(2,1)} %all-to-all-done.refs_1_, bf16[32,20,8,128]{3,2,1,0:T(8,128)(2,1)} %all-to-all-done.1.refs_2_, bf16[32,12,8,128]{3,2,1,0:T(8,128)(2,1)S(1)} %copy-done.3, ...), custom_call_target="tpu_custom_call" | custom-call | flops 1000000000 | bytes 4000000 | tf_op jit(solution)/shard_map/correlate/pallas_call | solution.py:379
  124.0 1.8 %collective-permute-start.15 = (bf16[16,8,8,128]{3,2,1,0:T(8,128)(2,1)S(1)}, bf16[16,8,8,128]{3,2,1,0:T(8,128)(2,1)S(1)}, u32[]{:S(2)}, u32[]{:S(2)}) collective-permute-start(bf16[16,8,8,128]{3,2,1,0:T(8,128)(2,1)S(1)} %slice.29), channel_id=1, source_target_pairs={{0,96},{32,0},{64,32},{96,64},{1,97},{33,1},{65,33},{97,65},{2,98}... | collective-permute-start | bytes 786440 | tf_op jit(solution)/shard_map/ppermute | solution.py:432
  126.1 5.1 %collective-permute-done.17.refs_6_ = bf16[16,12,8,128]{3,2,1,0:T(8,128)(2,1)S(1)} collective-permute-done((bf16[16,12,8,128]{3,2,1,0:T(8,128)(2,1)S(1)}, bf16[16,12,8,128]{3,2,1,0:T(8,128)(2,1)S(1)}, u32[]{:S(2)}, u32[]{:S(2)}) %collective-permute-start.17) | collective-permute-done | bytes 393248 | tf_op jit(solution)/shard_map/ppermute | solution.py:432
  132.4 5.2 %correlate_far.1.refs_10_ = bf16[20,2,256,1024]{3,2,1,0:T(8,128)(2,1)} custom-call(s32[3]{0:T(128)S(1)} %copy-done.8, bf16[32,12,8,128]{3,2,1,0:T(8,128)(2,1)} %all-to-all-done.refs_1_, bf16[32,20,8,128]{3,2,1,0:T(8,128)(2,1)} %all-to-all-done.1.refs_2_, bf16[16,12,8,128]{3,2,1,0:T(8,128)(2,1)} %collective-permute-done.8.refs_3_, ...), custom_call_target="tpu_custom_call", output_to_operand_aliasing={{}: (7, {})} | custom-call | flops 10000000000 | bytes 40000000 | tf_op jit(solution)/shard_map/correlate_far/pallas_call | solution.py:303
  140.4 7.0 %correlate.3 = bf16[20,2,256,1024]{3,2,1,0:T(8,128)(2,1)} custom-call(s32[3]{0:T(128)S(1)} %copy-done.8, bf16[32,32,8,128]{3,2,1,0:T(8,128)(2,1)S(1)} %all-to-all-done.2.refs_1_.refs_3_.refs_5_.refs_7_, bf16[32,20,8,128]{3,2,1,0:T(8,128)(2,1)} %all-to-all-done.1.refs_2_, ...), custom_call_target="tpu_custom_call", output_to_operand_aliasing={{}: (10, {})} | custom-call | flops 1000000000 | bytes 4000000 | tf_op jit(solution)/shard_map/correlate/pallas_call | solution.py:379
  (63 shorter events, 18.1 us)
Async XLA Ops:
  4.1 9.5 %collective-permute-start = (bf16[2,128,4096]{2,1,0:T(8,128)(2,1)}, bf16[2,128,4096]{2,1,0:T(8,128)(2,1)}, u32[]{:S(2)}, u32[]{:S(2)}) collective-permute-start(bf16[2,128,4096]{2,1,0:T(8,128)(2,1)} %pick.2), channel_id=1, source_target_pairs={{0,1},{1,0},{2,3},{3,2},{4,5},{5,4},{6,7},{7,6},{8,9},{9,8},{10,11... | collective-permute-start | bytes 6291464 | tf_op jit(solution)/shard_map/ppermute | solution.py:411
  8.0 32.3 %collective-permute-start.4 = (bf16[2,128,2048]{2,1,0:T(8,128)(2,1)}, bf16[2,128,2048]{2,1,0:T(8,128)(2,1)}, u32[]{:S(2)}, u32[]{:S(2)}) collective-permute-start(bf16[2,128,2048]{2,1,0:T(8,128)(2,1)} %get-tuple-element.25), channel_id=1, source_target_pairs={{2,0},{4,2},{6,4},{8,6},{10,8},{12,10},{14,12},{16,14},{18,16},{20... | collective-permute-start | bytes 3145736 | tf_op jit(solution)/shard_map/ppermute | solution.py:417
  9.3 31.3 %collective-permute-start.5 = (bf16[2,128,2048]{2,1,0:T(8,128)(2,1)}, bf16[2,128,2048]{2,1,0:T(8,128)(2,1)}, u32[]{:S(2)}, u32[]{:S(2)}) collective-permute-start(bf16[2,128,2048]{2,1,0:T(8,128)(2,1)} %get-tuple-element.26), channel_id=1, source_target_pairs={{2,1},{4,3},{6,5},{8,7},{10,9},{12,11},{14,13},{16,15},{18,17},{20... | collective-permute-start | bytes 3145736 | tf_op jit(solution)/shard_map/ppermute | solution.py:417
  22.6 27.6 %collective-permute-start.3 = (bf16[32,8,8,128]{3,2,1,0:T(8,128)(2,1)}, bf16[32,8,8,128]{3,2,1,0:T(8,128)(2,1)}, u32[]{:S(2)}, u32[]{:S(2)}) collective-permute-start(bf16[32,8,8,128]{3,2,1,0:T(8,128)(2,1)} %get-tuple-element.31.refs_0_), channel_id=1, source_target_pairs={{0,64},{32,96},{64,0},{96,32},{1,65},{33,97},{65,1},{97,33},{2,66}... | collective-permute-start | bytes 1572872 | tf_op jit(solution)/shard_map/ppermute | solution.py:432
  25.8 24.4 %collective-permute-start.2 = (bf16[32,8,8,128]{3,2,1,0:T(8,128)(2,1)}, bf16[32,8,8,128]{3,2,1,0:T(8,128)(2,1)}, u32[]{:S(2)}, u32[]{:S(2)}) collective-permute-start(bf16[32,8,8,128]{3,2,1,0:T(8,128)(2,1)} %get-tuple-element.31.refs_0_), channel_id=1, source_target_pairs={{0,96},{32,0},{64,32},{96,64},{1,97},{33,1},{65,33},{97,65},{2,98}... | collective-permute-start | bytes 1572872 | tf_op jit(solution)/shard_map/ppermute | solution.py:432
  27.0 23.5 %collective-permute-start.1 = (bf16[32,8,8,128]{3,2,1,0:T(8,128)(2,1)}, bf16[32,8,8,128]{3,2,1,0:T(8,128)(2,1)}, u32[]{:S(2)}, u32[]{:S(2)}) collective-permute-start(bf16[32,8,8,128]{3,2,1,0:T(8,128)(2,1)} %get-tuple-element.31.refs_0_), channel_id=1, source_target_pairs={{0,32},{32,64},{64,96},{96,0},{1,33},{33,65},{65,97},{97,1},{2,34}... | collective-permute-start | bytes 1572872 | tf_op jit(solution)/shard_map/ppermute | solution.py:432
  27.9 26.9 %all-to-all-start = ((bf16[32,12,8,128]{3,2,1,0:T(8,128)(2,1)}), bf16[32,12,8,128]{3,2,1,0:T(8,128)(2,1)}, u32[]{:S(2)}, u32[]{:S(2)}) async-start(bf16[32,12,8,128]{3,2,1,0:T(8,128)(2,1)} %get-tuple-element.29), calls=%async_computation | async-start | bytes 1572864 | tf_op jit(solution)/shard_map/all_to_all | solution.py:435
  54.8 19.6 %collective-permute-start.7 = (bf16[32,12,8,128]{3,2,1,0:T(8,128)(2,1)}, bf16[32,12,8,128]{3,2,1,0:T(8,128)(2,1)S(1)}, u32[]{:S(2)}, u32[]{:S(2)}) collective-permute-start(bf16[32,12,8,128]{3,2,1,0:T(8,128)(2,1)} %all-to-all-done.refs_1_), channel_id=1, source_target_pairs={{0,96},{32,0},{64,32},{96,64},{1,97},{33,1},{65,33},{97,65},{2,98}... | collective-permute-start | bytes 2359304 | tf_op jit(solution)/shard_map/ppermute | solution.py:432
  57.1 21.7 %collective-permute-start.6 = (bf16[32,12,8,128]{3,2,1,0:T(8,128)(2,1)}, bf16[32,12,8,128]{3,2,1,0:T(8,128)(2,1)S(1)}, u32[]{:S(2)}, u32[]{:S(2)}) collective-permute-start(bf16[32,12,8,128]{3,2,1,0:T(8,128)(2,1)} %all-to-all-done.refs_1_), channel_id=1, source_target_pairs={{0,32},{32,64},{64,96},{96,0},{1,33},{33,65},{65,97},{97,1},{2,34}... | collective-permute-start | bytes 2359304 | tf_op jit(solution)/shard_map/ppermute | solution.py:432
  57.1 28.6 %all-to-all-start.1 = ((bf16[32,20,8,128]{3,2,1,0:T(8,128)(2,1)}), bf16[32,20,8,128]{3,2,1,0:T(8,128)(2,1)}, u32[]{:S(2)}, u32[]{:S(2)}) async-start(bf16[32,20,8,128]{3,2,1,0:T(8,128)(2,1)} %channelize.3), calls=%async_computation.1 | async-start | bytes 2621440 | tf_op jit(solution)/shard_map/all_to_all | solution.py:435
  75.2 12.5 %collective-permute-start.9 = (bf16[16,12,8,128]{3,2,1,0:T(8,128)(2,1)}, bf16[16,12,8,128]{3,2,1,0:T(8,128)(2,1)}, u32[]{:S(2)}, u32[]{:S(2)}) collective-permute-start(bf16[16,12,8,128]{3,2,1,0:T(8,128)(2,1)} %slice.33), channel_id=1, source_target_pairs={{0,96},{32,0},{64,32},{96,64},{1,97},{33,1},{65,33},{97,65},{2,98}... | collective-permute-start | bytes 1179656 | tf_op jit(solution)/shard_map/ppermute | solution.py:432
  79.6 11.5 %collective-permute-start.8 = (bf16[16,12,8,128]{3,2,1,0:T(8,128)(2,1)}, bf16[16,12,8,128]{3,2,1,0:T(8,128)(2,1)}, u32[]{:S(2)}, u32[]{:S(2)}) collective-permute-start(bf16[16,12,8,128]{3,2,1,0:T(8,128)(2,1)} %slice.32), channel_id=1, source_target_pairs={{0,32},{32,64},{64,96},{96,0},{1,33},{33,65},{65,97},{97,1},{2,34}... | collective-permute-start | bytes 1179656 | tf_op jit(solution)/shard_map/ppermute | solution.py:432
  91.1 20.7 %collective-permute-start.13 = (bf16[32,12,8,128]{3,2,1,0:T(8,128)(2,1)}, bf16[32,12,8,128]{3,2,1,0:T(8,128)(2,1)S(1)}, u32[]{:S(2)}, u32[]{:S(2)}) collective-permute-start(bf16[32,12,8,128]{3,2,1,0:T(8,128)(2,1)} %slice.24), channel_id=1, source_target_pairs={{0,96},{32,0},{64,32},{96,64},{1,97},{33,1},{65,33},{97,65},{2,98}... | collective-permute-start | bytes 2359304 | tf_op jit(solution)/shard_map/ppermute | solution.py:432
  91.1 22.0 %collective-permute-start.12 = (bf16[32,12,8,128]{3,2,1,0:T(8,128)(2,1)}, bf16[32,12,8,128]{3,2,1,0:T(8,128)(2,1)}, u32[]{:S(2)}, u32[]{:S(2)}) collective-permute-start(bf16[32,12,8,128]{3,2,1,0:T(8,128)(2,1)} %slice.24), channel_id=1, source_target_pairs={{0,32},{32,64},{64,96},{96,0},{1,33},{33,65},{65,97},{97,1},{2,34}... | collective-permute-start | bytes 2359304 | tf_op jit(solution)/shard_map/ppermute | solution.py:432
  93.1 45.3 %all-to-all-start.2 = ((bf16[32,32,8,128]{3,2,1,0:T(8,128)(2,1)}), bf16[32,32,8,128]{3,2,1,0:T(8,128)(2,1)S(1)}, u32[]{:S(2)}, u32[]{:S(2)}) async-start(bf16[32,32,8,128]{3,2,1,0:T(8,128)(2,1)} %pack.1), calls=%async_computation.2 | async-start | bytes 4194304 | tf_op jit(solution)/shard_map/all_to_all | solution.py:435
  101.0 14.0 %copy-start.1 = (bf16[32,12,8,128]{3,2,1,0:T(8,128)(2,1)S(1)}, bf16[32,12,8,128]{3,2,1,0:T(8,128)(2,1)}, u32[]{:S(2)}) copy-start(bf16[32,12,8,128]{3,2,1,0:T(8,128)(2,1)} %copy-done) | copy-start | bytes 2359300
  101.0 13.9 %copy-start.3 = (bf16[32,12,8,128]{3,2,1,0:T(8,128)(2,1)S(1)}, bf16[32,12,8,128]{3,2,1,0:T(8,128)(2,1)}, u32[]{:S(2)}) copy-start(bf16[32,12,8,128]{3,2,1,0:T(8,128)(2,1)} %copy-done.2) | copy-start | bytes 2359300
  101.1 13.9 %copy-start.8 = (s32[3]{0:T(128)S(1)}, s32[3]{0:T(128)}, u32[]{:S(2)}) copy-start(s32[3]{0:T(128)} %pad_add_fusion.place.refs_0_) | copy-start | bytes 40
  102.3 21.1 %collective-permute-start.11 = (bf16[32,8,8,128]{3,2,1,0:T(8,128)(2,1)S(1)}, bf16[32,8,8,128]{3,2,1,0:T(8,128)(2,1)S(1)}, u32[]{:S(2)}, u32[]{:S(2)}) collective-permute-start(bf16[32,8,8,128]{3,2,1,0:T(8,128)(2,1)S(1)} %slice.27), channel_id=1, source_target_pairs={{0,96},{32,0},{64,32},{96,64},{1,97},{33,1},{65,33},{97,65},{2,98}... | collective-permute-start | bytes 1572872 | tf_op jit(solution)/shard_map/ppermute | solution.py:432
  103.7 20.3 %collective-permute-start.10 = (bf16[32,8,8,128]{3,2,1,0:T(8,128)(2,1)S(1)}, bf16[32,8,8,128]{3,2,1,0:T(8,128)(2,1)S(1)}, u32[]{:S(2)}, u32[]{:S(2)}) collective-permute-start(bf16[32,8,8,128]{3,2,1,0:T(8,128)(2,1)S(1)} %slice.27), channel_id=1, source_target_pairs={{0,32},{32,64},{64,96},{96,0},{1,33},{33,65},{65,97},{97,1},{2,34}... | collective-permute-start | bytes 1572872 | tf_op jit(solution)/shard_map/ppermute | solution.py:432
  111.8 19.4 %collective-permute-start.17 = (bf16[16,12,8,128]{3,2,1,0:T(8,128)(2,1)S(1)}, bf16[16,12,8,128]{3,2,1,0:T(8,128)(2,1)S(1)}, u32[]{:S(2)}, u32[]{:S(2)}) collective-permute-start(bf16[16,12,8,128]{3,2,1,0:T(8,128)(2,1)S(1)} %slice.35), channel_id=1, source_target_pairs={{0,96},{32,0},{64,32},{96,64},{1,97},{33,1},{65,33},{97,65},{2,98}... | collective-permute-start | bytes 1179656 | tf_op jit(solution)/shard_map/ppermute | solution.py:432
  114.1 18.3 %collective-permute-start.16 = (bf16[16,12,8,128]{3,2,1,0:T(8,128)(2,1)S(1)}, bf16[16,12,8,128]{3,2,1,0:T(8,128)(2,1)S(1)}, u32[]{:S(2)}, u32[]{:S(2)}) collective-permute-start(bf16[16,12,8,128]{3,2,1,0:T(8,128)(2,1)S(1)} %slice.34), channel_id=1, source_target_pairs={{0,32},{32,64},{64,96},{96,0},{1,33},{33,65},{65,97},{97,1},{2,34}... | collective-permute-start | bytes 1179656 | tf_op jit(solution)/shard_map/ppermute | solution.py:432
  124.0 13.6 %collective-permute-start.15 = (bf16[16,8,8,128]{3,2,1,0:T(8,128)(2,1)S(1)}, bf16[16,8,8,128]{3,2,1,0:T(8,128)(2,1)S(1)}, u32[]{:S(2)}, u32[]{:S(2)}) collective-permute-start(bf16[16,8,8,128]{3,2,1,0:T(8,128)(2,1)S(1)} %slice.29), channel_id=1, source_target_pairs={{0,96},{32,0},{64,32},{96,64},{1,97},{33,1},{65,33},{97,65},{2,98}... | collective-permute-start | bytes 786440 | tf_op jit(solution)/shard_map/ppermute | solution.py:432
  125.9 11.8 %collective-permute-start.14 = (bf16[16,8,8,128]{3,2,1,0:T(8,128)(2,1)S(1)}, bf16[16,8,8,128]{3,2,1,0:T(8,128)(2,1)S(1)}, u32[]{:S(2)}, u32[]{:S(2)}) collective-permute-start(bf16[16,8,8,128]{3,2,1,0:T(8,128)(2,1)S(1)} %slice.28), channel_id=1, source_target_pairs={{0,32},{32,64},{64,96},{96,0},{1,33},{33,65},{65,97},{97,1},{2,34}... | collective-permute-start | bytes 786440 | tf_op jit(solution)/shard_map/ppermute | solution.py:432
  (10 other events, 59.0 us)
